TPU v7x, 128 devices: a whole 4x4x4 slice. The times are simulated.
128 devices in a mesh: dp: 16 (over x, z), seq: 8 (over y, core).
Axes of the slice: x: 4, y: 4, z: 4, core: 2. Of those that a mesh axis runs over, the one named last changes fastest.
Arguments:
- queries: bfloat16 [16, 8, 256, 1536], P('dp', 'seq'), may hold values from -6 to 6
- keys_proj: bfloat16 [16, 8, 256, 1536], P('dp', 'seq'), may hold values from -6 to 6
- values_proj: bfloat16 [16, 8, 256, 1536], P('dp', 'seq'), may hold values from -6 to 6
- gain_query: float32 [64], replicated, may hold values from 0.5 to 6
- gain_key: float32 [64], replicated, may hold values from 0.5 to 6
- frame_counts: int32 [16], P('dp'), may hold values from 4 to 8, as said below
- heights: int32 [16], P('dp'), may hold values from 8 to 16, as said below
- widths: int32 [16], P('dp'), may hold values from 8 to 16, as said below
- out_weight: bfloat16 [1536, 3072], replicated, may hold values from -0.15625 to 0.15625
- cotangent: bfloat16 [16, 8, 256, 3072], P('dp', 'seq'), may hold values from -6 to 6
Outputs:
- block_out: bfloat16 [16, 8, 256, 3072], P('dp', 'seq')
- grad_queries: bfloat16 [16, 8, 256, 1536], P('dp', 'seq')
- grad_keys: bfloat16 [16, 8, 256, 1536], P('dp', 'seq')
- grad_values: bfloat16 [16, 8, 256, 1536], P('dp', 'seq')
- grad_weight: float32 [1536, 3072], P(('dp', 'seq'))
- grad_gain_query: float32 [64], replicated
- grad_gain_key: float32 [64], replicated
Inputs may be any that keep to these rules, and one draw needn't show every extreme that they name: `frame_counts`: some clip has exactly 8 frames. `heights`: some clip has exactly 16 patch rows. `widths`: some clip has exactly 16 patch columns.
All inputs are finite; a program needn't handle non-finite values.
Results may differ from a plain program's by a relative error of at most 0.015.
The roundings to bfloat16 on the way count: a program that leaves them out, or rounds other values in their place, can miss the bound.
Values may be sent and summed in bfloat16 or wider, within the bound.
No kernel may reach another device: no remote copies, remote signals or barrier semaphores. Data moves between devices by JAX's collectives and lax.ppermute only.
A program may use at most 192 MiB of HBM per device.

v0:
```python
import jax
import jax.numpy as jnp
from jax import lax
from jax.sharding import PartitionSpec as P

HD = 64
PW = 16


def product(form, left, right):
    return jnp.einsum(form, left, right, preferred_element_type=jnp.float32)


def split_heads(tensor):
    return tensor.reshape(tensor.shape[:-1] + (tensor.shape[-1] // HD, HD))


def layer_norm(tensor, gain):
    rows = split_heads(tensor.astype(jnp.float32))
    centre = rows - jnp.mean(rows, -1, keepdims=True)
    inverse = lax.rsqrt(jnp.mean(centre * centre, -1, keepdims=True) + 1e-06)
    normed = centre * inverse
    return ((normed * gain).reshape(tensor.shape).astype(jnp.bfloat16), normed, inverse)


def norm_back(upstream, normed, inverse, gain):
    upstream_heads = upstream.reshape(normed.shape)
    scaled = upstream_heads * gain
    dinput = inverse * (
        scaled
        - jnp.mean(scaled, -1, keepdims=True)
        - normed * jnp.mean(scaled * normed, -1, keepdims=True)
    )
    gain_grad = jnp.sum((upstream_heads * normed).reshape(-1, HD), 0)
    return (dinput.reshape(upstream.shape).astype(jnp.bfloat16), gain_grad)


def probabilities(query, key_rows, key_ok):
    scores = product("bqhd,bkhd->bhqk", split_heads(query), split_heads(key_rows)) * HD ** (-0.5)
    scores = jnp.where(key_ok[:, None, None, :] > 0, scores, -1e30)
    expo = jnp.exp(scores - jnp.max(scores, -1, keepdims=True))
    return expo / jnp.sum(expo, -1, keepdims=True)


def attend(query, key_rows, value_rows, key_ok, query_ok):
    weights = probabilities(query, key_rows, key_ok).astype(jnp.bfloat16)
    result = (
        product("bhqk,bkhd->bqhd", weights, split_heads(value_rows)) * query_ok[:, :, None, None]
    )
    return result.reshape(value_rows.shape).astype(jnp.bfloat16)


def attend_back(query, key_rows, value_rows, key_ok, query_ok, upstream):
    chances = probabilities(query, key_rows, key_ok)
    weights = chances.astype(jnp.bfloat16)
    masked = jnp.where(query_ok[:, :, None, None] > 0, split_heads(upstream), 0)
    dvalues = product("bhqk,bqhd->bkhd", weights, masked)
    dchances = product("bqhd,bkhd->bhqk", masked, split_heads(value_rows))
    dscores = (
        chances * (dchances - jnp.sum(chances * dchances, -1, keepdims=True)) * HD ** (-0.5)
    ).astype(jnp.bfloat16)
    dquery = product("bhqk,bkhd->bqhd", dscores, split_heads(key_rows))
    dkeys = product("bhqk,bqhd->bkhd", dscores, split_heads(query))
    layout = value_rows.shape
    return (dquery.reshape(layout), dkeys.reshape(layout), dvalues.reshape(layout))


def flip_axes(tensor):
    return jnp.swapaxes(tensor, 0, 1)


def local(
    queries,
    keys_proj,
    values_proj,
    gain_query,
    gain_key,
    frame_counts,
    heights,
    widths,
    out_weight,
    cotangent,
):
    group_size = lax.axis_size("seq")
    seq_rank = lax.axis_index("seq")
    frame_here = queries.shape[1]
    cell_count = queries.shape[2]
    all_frames = frame_here * group_size
    cells_here = cell_count // group_size
    frame_total = frame_counts[0]
    height = heights[0]
    width_now = widths[0]
    frame_ids = seq_rank * frame_here + jnp.arange(frame_here)
    cell_ids = jnp.arange(cell_count)
    usable = (
        (frame_ids[:, None] < frame_total)
        & (cell_ids[None, :] // PW < height)
        & (cell_ids[None, :] % PW < width_now)
    ).astype(jnp.float32)
    position_ids = seq_rank * cells_here + jnp.arange(cells_here)
    usable_pos = (
        (jnp.arange(all_frames)[None, :] < frame_total)
        & (position_ids[:, None] // PW < height)
        & (position_ids[:, None] % PW < width_now)
    ).astype(jnp.float32)
    query_norm, query_hat, query_inv = layer_norm(queries[0], gain_query)
    key_norm, key_hat, key_inv = layer_norm(keys_proj[0], gain_key)
    spatial = attend(query_norm, key_norm, values_proj[0], usable, usable)
    query_pos, key_pos, spatial_pos = (
        lax.all_to_all(query_norm, "seq", split_axis=1, concat_axis=0, tiled=True),
        lax.all_to_all(key_norm, "seq", split_axis=1, concat_axis=0, tiled=True),
        lax.all_to_all(spatial, "seq", split_axis=1, concat_axis=0, tiled=True),
    )
    query_cells = flip_axes(query_pos)
    key_cells = flip_axes(key_pos)
    spatial_cells = flip_axes(spatial_pos)
    mixed_pos = flip_axes(attend(query_cells, key_cells, spatial_cells, usable_pos, usable_pos))
    mixed = lax.all_to_all(mixed_pos, "seq", split_axis=0, concat_axis=1, tiled=True)
    mixed_rows = mixed.reshape(-1, mixed.shape[-1])
    grad_rows = cotangent[0].reshape(-1, cotangent.shape[-1])
    block_out = jnp.dot(mixed_rows, out_weight, preferred_element_type=jnp.float32).astype(
        jnp.bfloat16
    )
    grad_mixed = lax.dot_general(
        grad_rows, out_weight, (((1,), (1,)), ((), ())), preferred_element_type=jnp.float32
    ).astype(jnp.bfloat16)
    grad_mixed_pos = lax.all_to_all(
        grad_mixed.reshape(mixed.shape), "seq", split_axis=1, concat_axis=0, tiled=True
    )
    dq_time, dk_time, dspatial = attend_back(
        query_cells, key_cells, spatial_cells, usable_pos, usable_pos, flip_axes(grad_mixed_pos)
    )
    returned = (
        flip_axes(dq_time).astype(jnp.bfloat16),
        flip_axes(dk_time).astype(jnp.bfloat16),
        flip_axes(dspatial).astype(jnp.bfloat16),
    )
    dq_time, dk_time, dspatial = (
        lax.all_to_all(returned[0], "seq", split_axis=0, concat_axis=1, tiled=True),
        lax.all_to_all(returned[1], "seq", split_axis=0, concat_axis=1, tiled=True),
        lax.all_to_all(returned[2], "seq", split_axis=0, concat_axis=1, tiled=True),
    )
    dq_space, dk_space, dvalues = attend_back(
        query_norm, key_norm, values_proj[0], usable, usable, dspatial
    )
    grad_queries, gain_q_part = norm_back(
        dq_space + dq_time.astype(jnp.float32), query_hat, query_inv, gain_query
    )
    grad_keys, gain_k_part = norm_back(
        dk_space + dk_time.astype(jnp.float32), key_hat, key_inv, gain_key
    )
    grad_gain_query, grad_gain_key = lax.psum((gain_q_part, gain_k_part), ("dp", "seq"))
    grad_weight = lax.psum_scatter(
        lax.dot_general(
            mixed_rows, grad_rows, (((0,), (0,)), ((), ())), preferred_element_type=jnp.float32
        ),
        ("dp", "seq"),
        scatter_dimension=0,
        tiled=True,
    )
    return (
        block_out.reshape(cotangent.shape),
        grad_queries[None],
        grad_keys[None],
        dvalues.astype(jnp.bfloat16)[None],
        grad_weight,
        grad_gain_query,
        grad_gain_key,
    )


def solution(mesh):
    return jax.shard_map(
        local,
        mesh=mesh,
        in_specs=(
            P("dp", "seq", None, None),
            P("dp", "seq", None, None),
            P("dp", "seq", None, None),
            P(),
            P(),
            P("dp"),
            P("dp"),
            P("dp"),
            P(),
            P("dp", "seq", None, None),
        ),
        out_specs=(
            P("dp", "seq", None, None),
            P("dp", "seq", None, None),
            P("dp", "seq", None, None),
            P("dp", "seq", None, None),
            P(("dp", "seq"), None),
            P(),
            P(),
        ),
        check_vma=False,
    )
```

profile of v0, /device:TPU:0, one launch (start us, length us, event | category | flops | bytes accessed | tf_op | source)
XLA Modules:
  0.0 999.3 jit_solution(8872963037232669616)
XLA Ops:
  18.0 6.4 fusion.88
  24.4 4.7 fusion.26
  29.2 4.8 copy.156
  34.5 7.2 reduce.16
  45.0 14.4 %all-to-all-start = ((bf16[8,2,24576]{2,1,0:T(2,128)(2,1)}), bf16[8,2,24576]{2,1,0:T(2,128)(2,1)}, u32[]{:S(2)}, u32[]{:S(2)}) async-start(bf16[8,2,24576]{2,1,0:T(2,128)(2,1)} %reshape.959), calls=%async_computation | async-start | bytes 1572864 | tf_op jit(solution)/shard_map/all_to_all | solution.py:112
  61.7 4.8 copy.160
  66.5 7.3 reduce.17
  77.0 4.8 all-to-all-start.2
  84.2 4.8 copy.158
  89.0 7.3 reduce.18
  99.5 5.1 all-to-all-start.1
  104.6 6.3 fusion.24
  113.2 7.3 reduce.19
  123.8 5.3 all-to-all-start.4
  129.1 5.5 reshape.960
  140.1 5.5 reshape.958
  151.1 5.5 reshape.964
  162.1 5.5 reshape.962
  173.5 3.8 fusion.55
  177.3 4.9 fusion.89
  192.0 5.0 all-to-all-start.5
  197.1 4.1 fusion.44
  211.1 8.9 fusion.42
  228.6 8.7 fusion.43
  245.9 5.1 all-to-all-start.3
  259.6 5.2 fusion.94
  264.8 4.8 fusion.51
  269.6 4.8 all-to-all-start.6
  274.4 9.0 fusion.27
  283.4 368.9 %fusion = f32[16,3072]{1,0:T(8,128)S(1)} fusion(f32[1536,3072]{1,0:T(8,128)} %fusion.27), kind=kCustom, calls=%all-reduce-scatter | all-reduce-scatter fusion | flops 6291457 | bytes 19070976
  660.8 7.7 fusion.9
  668.5 4.2 all-to-all-start.7
  679.3 4.4 collective-permute-start.31
  683.7 12.8 %multiply_reduce_fusion.3 = (f32[64]{0:T(128)S(1)}, f32[256,24]{0,1:T(8,128)S(1)}, f32[256,24]{0,1:T(8,128)S(1)}, f32[1,256,24,64]{1,3,2,0:T(8,128)}) fusion(f32[1,256,24,64]{1,3,2,0:T(8,128)} %bitcast.144, f32[256,24]{0,1:T(8,128)S(1)} %add_rsqrt_fusion.1, f32[256,24]{0,1:T(8,128)S(1)} %broadcast_multiply_fusion.5, f32[64]{0:T(128)S(1)} %copy-done.26, ...), kind=kOutput, calls=%fused_computation.48 | convolution fusion | flops 215869632 | bytes 18211328 | tf_op jit(solution)/shard_map/bhqk,bkhd->bqhd/dot_general | solution.py:11
  699.2 3.9 collective-permute-start.24
  703.1 5.8 collective-permute-start.23
  709.0 3.8 collective-permute-start.22
  730.3 5.6 collective-permute-start.19
  738.4 8.0 collective-permute-start.17
  751.2 12.5 %multiply_reduce_fusion.2 = (f32[64]{0:T(128)S(1)}, f32[256,24]{0,1:T(8,128)S(1)}, f32[256,24]{0,1:T(8,128)S(1)}, f32[1,256,24,64]{1,3,2,0:T(8,128)}) fusion(f32[1,256,24,64]{1,3,2,0:T(8,128)S(1)} %bitcast.140, f32[256,24]{0,1:T(8,128)S(1)} %add_rsqrt_fusion, f32[256,24]{0,1:T(8,128)S(1)} %broadcast_multiply_fusion.4, f32[64]{0:T(128)S(1)} %copy-done.27, ...), kind=kOutput, calls=%fused_computation.47 | convolution fusion | flops 215869632 | bytes 18211328 | tf_op jit(solution)/shard_map/bhqk,bqhd->bkhd/dot_general | solution.py:11
  765.9 6.5 collective-permute-start.13
  777.2 8.4 collective-permute-start.10
  787.5 3.8 collective-permute-start.8
  794.4 5.5 collective-permute-start.6
  802.6 17.1 %collective-permute-start.4 = (f32[16,3072]{1,0:T(8,128)S(1)}, f32[16,3072]{1,0:T(8,128)}, u32[]{:S(2)}, u32[]{:S(2)}) collective-permute-start(f32[16,3072]{1,0:T(8,128)S(1)} %fusion), channel_id=1, source_target_pairs={{0,5},{1,6},{2,7},{3,8},{4,9},{5,10},{6,11},{7,12},{8,13},{9,14},{... | collective-permute-start | bytes 589832
  822.2 7.7 collective-permute-start.2
  841.1 70.7 %all-reduce.2 = (f32[64]{0:T(128)}, f32[64]{0:T(128)}) all-reduce(f32[64]{0:T(128)S(1)} %get-tuple-element.44, f32[64]{0:T(128)S(1)} %get-tuple-element.42), channel_id=1, replica_groups=mesh['dp'=16,'seq'=8] {'dp','seq'}, use_global_device_ids=true, to_apply=%region_16.17 | all-reduce | flops 128 | bytes 1024 | tf_op jit(solution)/shard_map/psum | solution.py:152
  911.9 85.4 %concatenate = f32[524,3072]{1,0:T(8,128)} concatenate(f32[12,3072]{1,0:T(8,128)} %collective-permute-done.31, f32[16,3072]{1,0:T(8,128)} %collective-permute-done.30, f32[16,3072]{1,0:T(8,128)} %collective-permute-done.29, f32[16,3072]{1,0:T(8,128)} %collective-permute-done.28, f32[16,3072]{1,0:T(8,128)} %collective-permute-done.27, f32[16,3072]{1,0:T(8,128)S(1)} %copy-done.10, ...), dimensions={0} | concatenate | bytes 12877824
  (192 shorter events, 176.2 us)
Async XLA Ops:
  0.6 103.9 %copy-start = (bf16[1,1,256,3072]{3,2,1,0:T(8,128)(2,1)S(1)}, bf16[1,1,256,3072]{3,2,1,0:T(8,128)(2,1)}, u32[]{:S(2)}) copy-start(bf16[1,1,256,3072]{3,2,1,0:T(8,128)(2,1)} %param.19) | copy-start | bytes 4718596
  45.0 32.1 %all-to-all-start = ((bf16[8,2,24576]{2,1,0:T(2,128)(2,1)}), bf16[8,2,24576]{2,1,0:T(2,128)(2,1)}, u32[]{:S(2)}, u32[]{:S(2)}) async-start(bf16[8,2,24576]{2,1,0:T(2,128)(2,1)} %reshape.959), calls=%async_computation | async-start | bytes 1572864 | tf_op jit(solution)/shard_map/all_to_all | solution.py:112
  77.0 22.4 %all-to-all-start.2 = ((bf16[8,2,24576]{2,1,0:T(2,128)(2,1)}), bf16[8,2,24576]{2,1,0:T(2,128)(2,1)}, u32[]{:S(2)}, u32[]{:S(2)}) async-start(bf16[8,2,24576]{2,1,0:T(2,128)(2,1)} %reshape.957), calls=%async_computation.2 | async-start | bytes 1572864 | tf_op jit(solution)/shard_map/all_to_all | solution.py:111
  99.5 24.3 %all-to-all-start.1 = ((bf16[8,2,24576]{2,1,0:T(2,128)(2,1)}), bf16[8,2,24576]{2,1,0:T(2,128)(2,1)}, u32[]{:S(2)}, u32[]{:S(2)}) async-start(bf16[8,2,24576]{2,1,0:T(2,128)(2,1)} %reshape.963), calls=%async_computation.1 | async-start | bytes 1572864 | tf_op jit(solution)/shard_map/all_to_all | solution.py:110
  123.8 38.3 %all-to-all-start.4 = ((bf16[8,2,24576]{2,1,0:T(2,128)(2,1)}), bf16[8,2,24576]{2,1,0:T(2,128)(2,1)}, u32[]{:S(2)}, u32[]{:S(2)}) async-start(bf16[8,2,24576]{2,1,0:T(2,128)(2,1)} %reshape.961), calls=%async_computation.4 | async-start | bytes 1572864 | tf_op jit(solution)/shard_map/all_to_all | solution.py:127
  192.0 53.9 %all-to-all-start.5 = ((bf16[8,32,1536]{2,1,0:T(8,128)(2,1)}), bf16[8,32,1536]{2,1,0:T(8,128)(2,1)}, u32[]{:S(2)}, u32[]{:S(2)}) async-start(bf16[8,32,1536]{2,1,0:T(8,128)(2,1)} %copy.172), calls=%async_computation.5 | async-start | bytes 1572864 | tf_op jit(solution)/shard_map/all_to_all | solution.py:141
  245.9 23.7 %all-to-all-start.3 = ((bf16[8,32,1536]{2,1,0:T(8,128)(2,1)}), bf16[8,32,1536]{2,1,0:T(8,128)(2,1)}, u32[]{:S(2)}, u32[]{:S(2)}) async-start(bf16[8,32,1536]{2,1,0:T(8,128)(2,1)} %copy.167), calls=%async_computation.3 | async-start | bytes 1572864 | tf_op jit(solution)/shard_map/all_to_all | solution.py:118
  269.6 399.0 %all-to-all-start.6 = ((bf16[8,32,1536]{2,1,0:T(8,128)(2,1)}), bf16[8,32,1536]{2,1,0:T(8,128)(2,1)}, u32[]{:S(2)}, u32[]{:S(2)}) async-start(bf16[8,32,1536]{2,1,0:T(8,128)(2,1)} %copy.180), calls=%async_computation.6 | async-start | bytes 1572864 | tf_op jit(solution)/shard_map/all_to_all | solution.py:139
  653.0 44.9 %collective-permute-start.30 = (f32[16,3072]{1,0:T(8,128)S(1)}, f32[16,3072]{1,0:T(8,128)}, u32[]{:S(2)}, u32[]{:S(2)}) collective-permute-start(f32[16,3072]{1,0:T(8,128)S(1)} %fusion), channel_id=1, source_target_pairs={{0,31},{1,32},{2,33},{3,34},{4,35},{5,36},{6,37},{7,38},{8,39},{9,... | collective-permute-start | bytes 589832
  654.9 44.3 %collective-permute-start.29 = (f32[16,3072]{1,0:T(8,128)S(1)}, f32[16,3072]{1,0:T(8,128)}, u32[]{:S(2)}, u32[]{:S(2)}) collective-permute-start(f32[16,3072]{1,0:T(8,128)S(1)} %fusion), channel_id=1, source_target_pairs={{0,30},{1,31},{2,32},{3,33},{4,34},{5,35},{6,36},{7,37},{8,38},{9,... | collective-permute-start | bytes 589832
  656.9 46.2 %collective-permute-start.28 = (f32[16,3072]{1,0:T(8,128)S(1)}, f32[16,3072]{1,0:T(8,128)}, u32[]{:S(2)}, u32[]{:S(2)}) collective-permute-start(f32[16,3072]{1,0:T(8,128)S(1)} %fusion), channel_id=1, source_target_pairs={{0,29},{1,30},{2,31},{3,32},{4,33},{5,34},{6,35},{7,36},{8,37},{9,... | collective-permute-start | bytes 589832
  658.9 50.1 %collective-permute-start.27 = (f32[16,3072]{1,0:T(8,128)S(1)}, f32[16,3072]{1,0:T(8,128)}, u32[]{:S(2)}, u32[]{:S(2)}) collective-permute-start(f32[16,3072]{1,0:T(8,128)S(1)} %fusion), channel_id=1, source_target_pairs={{0,28},{1,29},{2,30},{3,31},{4,32},{5,33},{6,34},{7,35},{8,36},{9,... | collective-permute-start | bytes 589832
  668.5 55.3 %all-to-all-start.7 = ((bf16[8,32,1536]{2,1,0:T(8,128)(2,1)}), bf16[8,32,1536]{2,1,0:T(8,128)(2,1)}, u32[]{:S(2)}, u32[]{:S(2)}) async-start(bf16[8,32,1536]{2,1,0:T(8,128)(2,1)} %copy.185), calls=%async_computation.7 | async-start | bytes 1572864 | tf_op jit(solution)/shard_map/all_to_all | solution.py:140
  679.3 17.2 %collective-permute-start.31 = (f32[12,3072]{1,0:T(8,128)}, f32[12,3072]{1,0:T(8,128)}, u32[]{:S(2)}, u32[]{:S(2)}) collective-permute-start(f32[12,3072]{1,0:T(8,128)} %slice), channel_id=1, source_target_pairs={{0,32},{1,33},{2,34},{3,35},{4,36},{5,37},{6,38},{7,39},{8,40},{9,... | collective-permute-start | bytes 442376
  696.5 16.2 %collective-permute-start.26 = (f32[16,3072]{1,0:T(8,128)S(1)}, f32[16,3072]{1,0:T(8,128)S(1)}, u32[]{:S(2)}, u32[]{:S(2)}) collective-permute-start(f32[16,3072]{1,0:T(8,128)S(1)} %fusion), channel_id=1, source_target_pairs={{0,27},{1,28},{2,29},{3,30},{4,31},{5,32},{6,33},{7,34},{8,35},{9,... | collective-permute-start | bytes 589832
  697.9 17.4 %collective-permute-start.25 = (f32[16,3072]{1,0:T(8,128)S(1)}, f32[16,3072]{1,0:T(8,128)S(1)}, u32[]{:S(2)}, u32[]{:S(2)}) collective-permute-start(f32[16,3072]{1,0:T(8,128)S(1)} %fusion), channel_id=1, source_target_pairs={{0,26},{1,27},{2,28},{3,29},{4,30},{5,31},{6,32},{7,33},{8,34},{9,... | collective-permute-start | bytes 589832
  699.2 31.1 %collective-permute-start.24 = (f32[16,3072]{1,0:T(8,128)S(1)}, f32[16,3072]{1,0:T(8,128)}, u32[]{:S(2)}, u32[]{:S(2)}) collective-permute-start(f32[16,3072]{1,0:T(8,128)S(1)} %fusion), channel_id=1, source_target_pairs={{0,25},{1,26},{2,27},{3,28},{4,29},{5,30},{6,31},{7,32},{8,33},{9,... | collective-permute-start | bytes 589832
  703.1 32.8 %collective-permute-start.23 = (f32[16,3072]{1,0:T(8,128)S(1)}, f32[16,3072]{1,0:T(8,128)}, u32[]{:S(2)}, u32[]{:S(2)}) collective-permute-start(f32[16,3072]{1,0:T(8,128)S(1)} %fusion), channel_id=1, source_target_pairs={{0,24},{1,25},{2,26},{3,27},{4,28},{5,29},{6,30},{7,31},{8,32},{9,... | collective-permute-start | bytes 589832
  709.0 29.4 %collective-permute-start.22 = (f32[16,3072]{1,0:T(8,128)S(1)}, f32[16,3072]{1,0:T(8,128)}, u32[]{:S(2)}, u32[]{:S(2)}) collective-permute-start(f32[16,3072]{1,0:T(8,128)S(1)} %fusion), channel_id=1, source_target_pairs={{0,23},{1,24},{2,25},{3,26},{4,27},{5,28},{6,29},{7,30},{8,31},{9,... | collective-permute-start | bytes 589832
  712.8 33.6 %collective-permute-start.21 = (f32[16,3072]{1,0:T(8,128)S(1)}, f32[16,3072]{1,0:T(8,128)}, u32[]{:S(2)}, u32[]{:S(2)}) collective-permute-start(f32[16,3072]{1,0:T(8,128)S(1)} %fusion), channel_id=1, source_target_pairs={{0,22},{1,23},{2,24},{3,25},{4,26},{5,27},{6,28},{7,29},{8,30},{9,... | collective-permute-start | bytes 589832
  715.3 33.0 %collective-permute-start.20 = (f32[16,3072]{1,0:T(8,128)S(1)}, f32[16,3072]{1,0:T(8,128)}, u32[]{:S(2)}, u32[]{:S(2)}) collective-permute-start(f32[16,3072]{1,0:T(8,128)S(1)} %fusion), channel_id=1, source_target_pairs={{0,21},{1,22},{2,23},{3,24},{4,25},{5,26},{6,27},{7,28},{8,29},{9,... | collective-permute-start | bytes 589832
  730.3 33.4 %collective-permute-start.19 = (f32[16,3072]{1,0:T(8,128)S(1)}, f32[16,3072]{1,0:T(8,128)}, u32[]{:S(2)}, u32[]{:S(2)}) collective-permute-start(f32[16,3072]{1,0:T(8,128)S(1)} %fusion), channel_id=1, source_target_pairs={{0,20},{1,21},{2,22},{3,23},{4,24},{5,25},{6,26},{7,27},{8,28},{9,... | collective-permute-start | bytes 589832
  735.9 30.0 %collective-permute-start.18 = (f32[16,3072]{1,0:T(8,128)S(1)}, f32[16,3072]{1,0:T(8,128)}, u32[]{:S(2)}, u32[]{:S(2)}) collective-permute-start(f32[16,3072]{1,0:T(8,128)S(1)} %fusion), channel_id=1, source_target_pairs={{0,19},{1,20},{2,21},{3,22},{4,23},{5,24},{6,25},{7,26},{8,27},{9,... | collective-permute-start | bytes 589832
  738.4 34.0 %collective-permute-start.17 = (f32[16,3072]{1,0:T(8,128)S(1)}, f32[16,3072]{1,0:T(8,128)}, u32[]{:S(2)}, u32[]{:S(2)}) collective-permute-start(f32[16,3072]{1,0:T(8,128)S(1)} %fusion), channel_id=1, source_target_pairs={{0,18},{1,19},{2,20},{3,21},{4,22},{5,23},{6,24},{7,25},{8,26},{9,... | collective-permute-start | bytes 589832
  746.4 28.6 %collective-permute-start.16 = (f32[16,3072]{1,0:T(8,128)S(1)}, f32[16,3072]{1,0:T(8,128)}, u32[]{:S(2)}, u32[]{:S(2)}) collective-permute-start(f32[16,3072]{1,0:T(8,128)S(1)} %fusion), channel_id=1, source_target_pairs={{0,17},{1,18},{2,19},{3,20},{4,21},{5,22},{6,23},{7,24},{8,25},{9,... | collective-permute-start | bytes 589832
  748.3 28.8 %collective-permute-start.15 = (f32[16,3072]{1,0:T(8,128)S(1)}, f32[16,3072]{1,0:T(8,128)}, u32[]{:S(2)}, u32[]{:S(2)}) collective-permute-start(f32[16,3072]{1,0:T(8,128)S(1)} %fusion), channel_id=1, source_target_pairs={{0,16},{1,17},{2,18},{3,19},{4,20},{5,21},{6,22},{7,23},{8,24},{9,... | collective-permute-start | bytes 589832
  763.7 21.9 %collective-permute-start.14 = (f32[16,3072]{1,0:T(8,128)S(1)}, f32[16,3072]{1,0:T(8,128)S(1)}, u32[]{:S(2)}, u32[]{:S(2)}) collective-permute-start(f32[16,3072]{1,0:T(8,128)S(1)} %fusion), channel_id=1, source_target_pairs={{0,15},{1,16},{2,17},{3,18},{4,19},{5,20},{6,21},{7,22},{8,23},{9,... | collective-permute-start | bytes 589832
  765.9 21.6 %collective-permute-start.13 = (f32[16,3072]{1,0:T(8,128)S(1)}, f32[16,3072]{1,0:T(8,128)S(1)}, u32[]{:S(2)}, u32[]{:S(2)}) collective-permute-start(f32[16,3072]{1,0:T(8,128)S(1)} %fusion), channel_id=1, source_target_pairs={{0,14},{1,15},{2,16},{3,17},{4,18},{5,19},{6,20},{7,21},{8,22},{9,... | collective-permute-start | bytes 589832
  772.4 18.9 %collective-permute-start.12 = (f32[16,3072]{1,0:T(8,128)S(1)}, f32[16,3072]{1,0:T(8,128)S(1)}, u32[]{:S(2)}, u32[]{:S(2)}) collective-permute-start(f32[16,3072]{1,0:T(8,128)S(1)} %fusion), channel_id=1, source_target_pairs={{0,13},{1,14},{2,15},{3,16},{4,17},{5,18},{6,19},{7,20},{8,21},{9,... | collective-permute-start | bytes 589832
  774.9 19.5 %collective-permute-start.11 = (f32[16,3072]{1,0:T(8,128)S(1)}, f32[16,3072]{1,0:T(8,128)S(1)}, u32[]{:S(2)}, u32[]{:S(2)}) collective-permute-start(f32[16,3072]{1,0:T(8,128)S(1)} %fusion), channel_id=1, source_target_pairs={{0,12},{1,13},{2,14},{3,15},{4,16},{5,17},{6,18},{7,19},{8,20},{9,... | collective-permute-start | bytes 589832
  777.2 22.7 %collective-permute-start.10 = (f32[16,3072]{1,0:T(8,128)S(1)}, f32[16,3072]{1,0:T(8,128)S(1)}, u32[]{:S(2)}, u32[]{:S(2)}) collective-permute-start(f32[16,3072]{1,0:T(8,128)S(1)} %fusion), channel_id=1, source_target_pairs={{0,11},{1,12},{2,13},{3,14},{4,15},{5,16},{6,17},{7,18},{8,19},{9,... | collective-permute-start | bytes 589832
  785.6 46.2 %copy-start.13 = (f32[16,3072]{1,0:T(8,128)}, f32[16,3072]{1,0:T(8,128)S(1)}, u32[]{:S(2)}) copy-start(f32[16,3072]{1,0:T(8,128)S(1)} %collective-permute-done.14) | copy-start | bytes 589828
  785.6 16.9 %collective-permute-start.9 = (f32[16,3072]{1,0:T(8,128)S(1)}, f32[16,3072]{1,0:T(8,128)S(1)}, u32[]{:S(2)}, u32[]{:S(2)}) collective-permute-start(f32[16,3072]{1,0:T(8,128)S(1)} %fusion), channel_id=1, source_target_pairs={{0,10},{1,11},{2,12},{3,13},{4,14},{5,15},{6,16},{7,17},{8,18},{9,... | collective-permute-start | bytes 589832
  787.5 47.0 %copy-start.15 = (f32[16,3072]{1,0:T(8,128)}, f32[16,3072]{1,0:T(8,128)S(1)}, u32[]{:S(2)}) copy-start(f32[16,3072]{1,0:T(8,128)S(1)} %collective-permute-done.13) | copy-start | bytes 589828
  787.5 32.1 %collective-permute-start.8 = (f32[16,3072]{1,0:T(8,128)S(1)}, f32[16,3072]{1,0:T(8,128)S(1)}, u32[]{:S(2)}, u32[]{:S(2)}) collective-permute-start(f32[16,3072]{1,0:T(8,128)S(1)} %fusion), channel_id=1, source_target_pairs={{0,9},{1,10},{2,11},{3,12},{4,13},{5,14},{6,15},{7,16},{8,17},{9,1... | collective-permute-start | bytes 589832
  791.4 30.8 %collective-permute-start.7 = (f32[16,3072]{1,0:T(8,128)S(1)}, f32[16,3072]{1,0:T(8,128)S(1)}, u32[]{:S(2)}, u32[]{:S(2)}) collective-permute-start(f32[16,3072]{1,0:T(8,128)S(1)} %fusion), channel_id=1, source_target_pairs={{0,8},{1,9},{2,10},{3,11},{4,12},{5,13},{6,14},{7,15},{8,16},{9,17... | collective-permute-start | bytes 589832
  794.4 35.5 %collective-permute-start.6 = (f32[16,3072]{1,0:T(8,128)S(1)}, f32[16,3072]{1,0:T(8,128)S(1)}, u32[]{:S(2)}, u32[]{:S(2)}) collective-permute-start(f32[16,3072]{1,0:T(8,128)S(1)} %fusion), channel_id=1, source_target_pairs={{0,7},{1,8},{2,9},{3,10},{4,11},{5,12},{6,13},{7,14},{8,15},{9,16}... | collective-permute-start | bytes 589832
  799.9 31.9 %collective-permute-start.5 = (f32[16,3072]{1,0:T(8,128)S(1)}, f32[16,3072]{1,0:T(8,128)S(1)}, u32[]{:S(2)}, u32[]{:S(2)}) collective-permute-start(f32[16,3072]{1,0:T(8,128)S(1)} %fusion), channel_id=1, source_target_pairs={{0,6},{1,7},{2,8},{3,9},{4,10},{5,11},{6,12},{7,13},{8,14},{9,15},... | collective-permute-start | bytes 589832
  802.6 109.2 %collective-permute-start.4 = (f32[16,3072]{1,0:T(8,128)S(1)}, f32[16,3072]{1,0:T(8,128)}, u32[]{:S(2)}, u32[]{:S(2)}) collective-permute-start(f32[16,3072]{1,0:T(8,128)S(1)} %fusion), channel_id=1, source_target_pairs={{0,5},{1,6},{2,7},{3,8},{4,9},{5,10},{6,11},{7,12},{8,13},{9,14},{... | collective-permute-start | bytes 589832
  819.7 92.1 %collective-permute-start.3 = (f32[16,3072]{1,0:T(8,128)S(1)}, f32[16,3072]{1,0:T(8,128)}, u32[]{:S(2)}, u32[]{:S(2)}) collective-permute-start(f32[16,3072]{1,0:T(8,128)S(1)} %fusion), channel_id=1, source_target_pairs={{0,4},{1,5},{2,6},{3,7},{4,8},{5,9},{6,10},{7,11},{8,12},{9,13},{1... | collective-permute-start | bytes 589832
  822.2 89.6 %collective-permute-start.2 = (f32[16,3072]{1,0:T(8,128)S(1)}, f32[16,3072]{1,0:T(8,128)}, u32[]{:S(2)}, u32[]{:S(2)}) collective-permute-start(f32[16,3072]{1,0:T(8,128)S(1)} %fusion), channel_id=1, source_target_pairs={{0,3},{1,4},{2,5},{3,6},{4,7},{5,8},{6,9},{7,10},{8,11},{9,12},{10... | collective-permute-start | bytes 589832
  829.9 81.9 %collective-permute-start.1 = (f32[16,3072]{1,0:T(8,128)S(1)}, f32[16,3072]{1,0:T(8,128)}, u32[]{:S(2)}, u32[]{:S(2)}) collective-permute-start(f32[16,3072]{1,0:T(8,128)S(1)} %fusion), channel_id=1, source_target_pairs={{0,2},{1,3},{2,4},{3,5},{4,6},{5,7},{6,8},{7,9},{8,10},{9,11},{10,... | collective-permute-start | bytes 589832
  831.9 79.9 %collective-permute-start = (f32[16,3072]{1,0:T(8,128)S(1)}, f32[16,3072]{1,0:T(8,128)}, u32[]{:S(2)}, u32[]{:S(2)}) collective-permute-start(f32[16,3072]{1,0:T(8,128)S(1)} %fusion), channel_id=1, source_target_pairs={{0,1},{1,2},{2,3},{3,4},{4,5},{5,6},{6,7},{7,8},{8,9},{9,10},{10,1... | collective-permute-start | bytes 589832
  837.5 74.3 %copy-start.10 = (f32[16,3072]{1,0:T(8,128)S(1)}, f32[16,3072]{1,0:T(8,128)}, u32[]{:S(2)}) copy-start(f32[16,3072]{1,0:T(8,128)} %copy-done.9) | copy-start | bytes 589828
  837.5 74.3 %copy-start.12 = (f32[16,3072]{1,0:T(8,128)S(1)}, f32[16,3072]{1,0:T(8,128)}, u32[]{:S(2)}) copy-start(f32[16,3072]{1,0:T(8,128)} %copy-done.11) | copy-start | bytes 589828
  837.5 74.4 %copy-start.14 = (f32[16,3072]{1,0:T(8,128)S(1)}, f32[16,3072]{1,0:T(8,128)}, u32[]{:S(2)}) copy-start(f32[16,3072]{1,0:T(8,128)} %copy-done.13) | copy-start | bytes 589828
  837.5 74.4 %copy-start.16 = (f32[16,3072]{1,0:T(8,128)S(1)}, f32[16,3072]{1,0:T(8,128)}, u32[]{:S(2)}) copy-start(f32[16,3072]{1,0:T(8,128)} %copy-done.15) | copy-start | bytes 589828
  837.5 74.4 %copy-start.18 = (f32[16,3072]{1,0:T(8,128)S(1)}, f32[16,3072]{1,0:T(8,128)}, u32[]{:S(2)}) copy-start(f32[16,3072]{1,0:T(8,128)} %copy-done.17) | copy-start | bytes 589828
  (22 other events, 230.0 us)
where the time goes:
time: 1020 us; the launch traced here: 999 us
  blocking collectives  440 us (43%)
  local copies, waits for them, and re-layouts  225 us (22%)
  starting transfers between devices  174 us (17%)
  matrix products  98.7 us (10%)
  other arithmetic  57.7 us (6%)
    unnamed x1, blocking collectives  369 us
    unnamed x82, local copies, waits for them, and re-layouts  145 us
    unnamed x32, starting transfers between devices  125 us
    psum x1, blocking collectives, local(): lax.psum((gain_q_part, gain_k_part), ('dp', 'seq'))  70.7 us
    dot_general x11, matrix products, product(): return jnp.einsum(form, left, right, preferred_element_type=jnp.float32)  69.3 us
    unnamed x4, other arithmetic  29 us
  transfers between devices with their start and end apart: 40, of which 0 were waited for; matrix products, arithmetic and copies ran while one was open for 59% of the time, Pallas kernels for 0%

commit v1 on v0

v1 whole, which is shorter than its diff:
```python
import jax
import jax.numpy as jnp
import numpy as np
from jax import lax
from jax.experimental import pallas as pl
from jax.experimental.pallas import tpu as pltpu
from jax.sharding import Mesh
from jax.sharding import PartitionSpec as P

BF = jnp.bfloat16
F32 = jnp.float32
HD = 64
PW = 16
CELLS = 256
FRAMES = 8
LANES = 128
WIDE = 384
PAIRS = WIDE // LANES
CELLS_HERE = CELLS // FRAMES
BLOCK = 16
NEG = -1e30
SCALE = HD**-0.5
PARAMS = pltpu.CompilerParams(vmem_limit_bytes=56 * 1024 * 1024)


def cost(microseconds):
    return pl.CostEstimate(flops=0, bytes_accessed=int(microseconds * 3.69e6), transcendentals=0)


SMEM = pl.BlockSpec(memory_space=pltpu.SMEM)
VMEM = pl.BlockSpec(memory_space=pltpu.VMEM)


def nn(left, right):
    return jnp.dot(left, right, preferred_element_type=F32)


def nt(left, right):
    return lax.dot_general(left, right, (((1,), (1,)), ((), ())), preferred_element_type=F32)


def tn(left, right):
    return lax.dot_general(left, right, (((0,), (0,)), ((), ())), preferred_element_type=F32)


def low_lanes(shape):
    return lax.broadcasted_iota(jnp.int32, shape, len(shape) - 1) < HD


def stack_heads(pair):
    low = low_lanes((1, LANES)).astype(F32)
    return jnp.concatenate([pair * low.astype(BF), pair * (1.0 - low).astype(BF)], 0)


def pick_heads(stacked):
    half = stacked.shape[0] // 2
    return jnp.where(low_lanes((half, LANES)), stacked[:half], stacked[half:])


def softmax_rows(scores):
    grouped = scores.reshape(2, scores.shape[0] // 2, scores.shape[1])
    expo = jnp.exp(grouped - jnp.max(grouped, 1, keepdims=True))
    return expo * (1.0 / jnp.sum(expo, 1, keepdims=True))


def score_back(chances, dchances):
    grouped = dchances.reshape(chances.shape)
    total = jnp.sum(chances * grouped, 1, keepdims=True)
    return (chances * (grouped - total)).astype(BF).reshape(dchances.shape)


def cell_ok(cells, height, width):
    row = lax.shift_right_logical(cells, 4)
    return (row < height) & ((cells & (PW - 1)) < width)


def head_ones(rows, columns):
    row = lax.broadcasted_iota(jnp.int32, (rows, columns), 0) & (columns - 1)
    column = lax.broadcasted_iota(jnp.int32, (rows, columns), 1)
    same = lax.shift_right_logical(row, 6) == lax.shift_right_logical(column, 6)
    return jnp.where(same, 1.0, 0.0).astype(BF)


def head_mean(tensor, twice):
    high = tensor.astype(BF)
    rest = (tensor - high.astype(F32)).astype(BF)
    return nn(jnp.concatenate([high, rest], 1), twice) * (1.0 / HD)


def hat_of(raw, ones, twice):
    centre = raw.astype(F32) - nn(raw, ones) * (1.0 / HD)
    hats, inverses = [], []
    for left in range(0, raw.shape[1], LANES):
        part = centre[:, left : left + LANES]
        inverse = lax.rsqrt(head_mean(part * part, twice) + 1e-06)
        hats.append(part * inverse)
        inverses.append(inverse)
    return hats, inverses


def pair_slice(number):
    return slice(number * LANES, (number + 1) * LANES)


NORM_WIDE = 512
DUO = 2 * LANES


def both_heads(gain_ref):
    return jnp.concatenate([gain_ref[...], gain_ref[...]], 1)


def norm_kernel(q_ref, k_ref, gain_q_ref, gain_k_ref, out_ref):
    ones, twice = head_ones(DUO, DUO), head_ones(DUO, LANES)
    gains = both_heads(gain_q_ref), both_heads(gain_k_ref)
    for left in range(0, NORM_WIDE, DUO):
        for number, source in enumerate((q_ref, k_ref)):
            hats, _ = hat_of(source[:, left : left + DUO], ones, twice)
            for pair, hat in enumerate(hats):
                normed = (hat * gains[number]).astype(BF)
                if number == 0:
                    normed = normed * jnp.asarray(SCALE, BF)
                at = slice(left + pair * LANES, left + (pair + 1) * LANES)
                out_ref[:, number, :, at] = normed.reshape(FRAMES, CELLS_HERE, LANES)


def norm(queries, keys, gain_query, gain_key):
    inner = queries.shape[1]
    tokens = pl.BlockSpec((CELLS, NORM_WIDE), lambda n: (0, n))
    gain = pl.BlockSpec((1, HD), lambda n: (0, 0))
    return pl.pallas_call(
        norm_kernel,
        grid=(inner // NORM_WIDE,),
        in_specs=[tokens, tokens, gain, gain],
        out_specs=pl.BlockSpec((FRAMES, 2, CELLS_HERE, NORM_WIDE), lambda n: (0, 0, 0, n)),
        out_shape=jax.ShapeDtypeStruct((FRAMES, 2, CELLS_HERE, inner), BF),
        compiler_params=PARAMS,
        cost_estimate=cost(5),
        name="norm",
    )(queries, keys, gain_query, gain_key)


def hats_kernel(q_ref, k_ref, *out_refs):
    ones, twice = head_ones(DUO, DUO), head_ones(DUO, LANES)
    for left in range(0, NORM_WIDE, DUO):
        for number, source in enumerate((q_ref, k_ref)):
            hats, inverses = hat_of(source[:, left : left + DUO], ones, twice)
            at = slice(left, left + DUO)
            out_refs[number][:, at] = jnp.concatenate(hats, 1)
            out_refs[2 + number][:, at] = jnp.concatenate(inverses, 1)


def hats_of(queries, keys):
    inner = queries.shape[1]
    tokens = pl.BlockSpec((CELLS, NORM_WIDE), lambda n: (0, n))
    return pl.pallas_call(
        hats_kernel,
        grid=(inner // NORM_WIDE,),
        in_specs=[tokens, tokens],
        out_specs=[tokens] * 4,
        out_shape=[jax.ShapeDtypeStruct((CELLS, inner), F32)] * 4,
        compiler_params=PARAMS,
        cost_estimate=cost(5.6),
        name="hats",
    )(queries, keys)


def space_kernel(counts_ref, qk_ref, v_ref, gm_ref, out_ref, chances_ref):
    height, width = counts_ref[1], counts_ref[2]
    frame_on = jnp.where(counts_ref[3] < counts_ref[0], 1.0, 0.0)
    key_cell = lax.broadcasted_iota(jnp.int32, (2 * CELLS, CELLS), 0) & (CELLS - 1)
    bias = jnp.where(cell_ok(key_cell, height, width), 0.0, NEG)
    cell = lax.broadcasted_iota(jnp.int32, (CELLS, LANES), 0)
    usable = cell_ok(cell, height, width).astype(F32) * frame_on
    scores = []
    for pair in range(PAIRS):
        query = qk_ref[:, 0, :, pair_slice(pair)].reshape(CELLS, LANES)
        key = qk_ref[:, 1, :, pair_slice(pair)].reshape(CELLS, LANES)
        scores.append(nt(stack_heads(key), query) + bias)
    weights = []
    for pair in range(PAIRS):
        probs = softmax_rows(scores[pair]).reshape(scores[pair].shape)
        chances_ref[pair] = probs
        weights.append(probs.astype(BF))
    for pair in range(PAIRS):
        mixed = tn(weights[pair], stack_heads(v_ref[:, pair_slice(pair)]))
        mixed = (mixed * usable).astype(BF)
        out_ref[:, 0, :, pair_slice(pair)] = mixed.reshape(FRAMES, CELLS_HERE, LANES)
    out_ref[:, 1] = gm_ref[...].reshape(FRAMES, CELLS_HERE, WIDE)


def space_forward(counts, normed, values, grad_mixed):
    inner = values.shape[1]
    tokens = pl.BlockSpec((CELLS, WIDE), lambda n: (0, n))
    return pl.pallas_call(
        space_kernel,
        grid=(inner // WIDE,),
        in_specs=[
            SMEM,
            pl.BlockSpec((FRAMES, 2, CELLS_HERE, WIDE), lambda n: (0, 0, 0, n)),
            tokens,
            tokens,
        ],
        out_specs=[
            pl.BlockSpec((FRAMES, 2, CELLS_HERE, WIDE), lambda n: (0, 0, 0, n)),
            pl.BlockSpec((PAIRS, 2 * CELLS, CELLS), lambda n: (n, 0, 0)),
        ],
        out_shape=[
            jax.ShapeDtypeStruct((FRAMES, 2, CELLS_HERE, inner), BF),
            jax.ShapeDtypeStruct((inner // LANES, 2 * CELLS, CELLS), F32),
        ],
        compiler_params=PARAMS,
        cost_estimate=cost(7),
        name="space_forward",
    )(counts, normed, values, grad_mixed)


def gain_part(grad, normed):
    return jnp.sum(grad * normed.astype(F32), 0, keepdims=True)


def add_gains(sums_ref, of_query, of_key):
    @pl.when(pl.program_id(0) == 0)
    def _():
        sums_ref[...] = jnp.zeros_like(sums_ref)

    sums_ref[0:1] += of_query
    sums_ref[1:2] += of_key


def space_back_kernel(
    hat_q_ref, hat_k_ref, qk_ref, v_ref, up_ref, chances_ref, dq_ref, dk_ref, dv_ref, sums_ref
):
    of_query = jnp.zeros((1, LANES), F32)
    of_key = jnp.zeros((1, LANES), F32)
    slices = [pair_slice(pair) for pair in range(PAIRS)]
    queries = [qk_ref[:, 0, :, at].reshape(CELLS, LANES) for at in slices]
    keys = [stack_heads(qk_ref[:, 1, :, at].reshape(CELLS, LANES)) for at in slices]
    dchances = [nt(stack_heads(v_ref[:, at]), up_ref[:, at]) for at in slices]
    dscores = []
    for pair, at in enumerate(slices):
        probs = chances_ref[pair]
        dv_ref[:, at] = pick_heads(nn(probs.astype(BF), up_ref[:, at])).astype(BF)
        dscores.append(score_back(probs.reshape(2, CELLS, CELLS), dchances[pair]))
    for pair, at in enumerate(slices):
        dk = pick_heads(nn(dscores[pair], queries[pair]))
        dq = tn(dscores[pair], keys[pair]) * SCALE
        dk_ref[:, at] = dk
        dq_ref[:, at] = dq
        of_query += gain_part(dq, hat_q_ref[:, at])
        of_key += gain_part(dk, hat_k_ref[:, at])
    add_gains(sums_ref, of_query, of_key)


def space_back(queries, keys, normed, values, upstream, chances):
    inner = values.shape[1]
    tokens = pl.BlockSpec((CELLS, WIDE), lambda n: (0, n))
    wide = jax.ShapeDtypeStruct((CELLS, inner), F32)
    return pl.pallas_call(
        space_back_kernel,
        grid=(inner // WIDE,),
        in_specs=[
            tokens,
            tokens,
            pl.BlockSpec((FRAMES, 2, CELLS_HERE, WIDE), lambda n: (0, 0, 0, n)),
            tokens,
            tokens,
            pl.BlockSpec((PAIRS, 2 * CELLS, CELLS), lambda n: (n, 0, 0)),
        ],
        out_specs=[tokens, tokens, tokens, pl.BlockSpec((8, LANES), lambda n: (0, 0))],
        out_shape=[
            wide,
            wide,
            jax.ShapeDtypeStruct((CELLS, inner), BF),
            jax.ShapeDtypeStruct((8, LANES), F32),
        ],
        compiler_params=PARAMS,
        cost_estimate=cost(9),
        name="space_back",
    )(queries, keys, normed, values, upstream, chances)


def time_bias(frame_total):
    key = lax.broadcasted_iota(jnp.int32, (2 * LANES, LANES), 0) & (LANES - 1)
    query = lax.broadcasted_iota(jnp.int32, (2 * LANES, LANES), 1)
    same = (key & (BLOCK - 1)) == (query & (BLOCK - 1))
    return jnp.where(same & (lax.shift_right_logical(key, 4) < frame_total), 0.0, NEG)


def time_usable(counts_ref, block):
    row = lax.broadcasted_iota(jnp.int32, (LANES, LANES), 0)
    cell = counts_ref[3] * CELLS_HERE + block * BLOCK + (row & (BLOCK - 1))
    on = cell_ok(cell, counts_ref[1], counts_ref[2])
    return (on & (lax.shift_right_logical(row, 4) < counts_ref[0])).astype(F32)


def time_blocks():
    for block in range(CELLS_HERE // BLOCK):
        for pair in range(PAIRS):
            yield block, slice(block * BLOCK, (block + 1) * BLOCK), pair_slice(pair)


def time_kernel(counts_ref, qk_ref, sg_ref, out_ref):
    bias = time_bias(counts_ref[0])
    usable = [time_usable(counts_ref, block) for block in range(CELLS_HERE // BLOCK)]
    scores = []
    for block, rows, at in time_blocks():
        query = qk_ref[:, 0, rows, at].reshape(LANES, LANES)
        keys = stack_heads(qk_ref[:, 1, rows, at].reshape(LANES, LANES))
        scores.append(nt(keys, query) + bias)
    weights = [softmax_rows(part).astype(BF).reshape(part.shape) for part in scores]
    for number, (block, rows, at) in enumerate(time_blocks()):
        values = stack_heads(sg_ref[:, 0, rows, at].reshape(LANES, LANES))
        mixed = tn(weights[number], values) * usable[block]
        out_ref[:, rows, at] = mixed.astype(BF).reshape(FRAMES, BLOCK, LANES)


def time_back_kernel(counts_ref, qk_ref, sg_ref, dqk_ref, ds_ref, sums_ref):
    bias = time_bias(counts_ref[0])
    of_query = jnp.zeros((1, LANES), F32)
    of_key = jnp.zeros((1, LANES), F32)
    usable = [time_usable(counts_ref, block) for block in range(CELLS_HERE // BLOCK)]
    blocks = list(time_blocks())

    def load(ref, number, rows, at):
        return ref[:, number, rows, at].reshape(LANES, LANES)

    def shaped(tensor):
        return tensor.astype(BF).reshape(FRAMES, BLOCK, LANES)

    queries = [load(qk_ref, 0, rows, at) for _, rows, at in blocks]
    singles = [load(qk_ref, 1, rows, at) for _, rows, at in blocks]
    keys = [stack_heads(key) for key in singles]
    upstreams = [
        (load(sg_ref, 1, rows, at).astype(F32) * usable[block]).astype(BF)
        for block, rows, at in blocks
    ]
    scores = [nt(key, query) + bias for key, query in zip(keys, queries)]
    dchances = [
        nt(stack_heads(load(sg_ref, 0, rows, at)), upstream)
        for (_, rows, at), upstream in zip(blocks, upstreams)
    ]
    chances = [softmax_rows(part) for part in scores]
    dscores = [score_back(probs, part) for probs, part in zip(chances, dchances)]
    for number, (_, rows, at) in enumerate(blocks):
        weights = chances[number].astype(BF).reshape(2 * LANES, LANES)
        ds_ref[:, rows, at] = shaped(pick_heads(nn(weights, upstreams[number])))
        dq = tn(dscores[number], keys[number]) * SCALE
        dk = pick_heads(nn(dscores[number], queries[number]))
        dqk_ref[:, 0, rows, at] = shaped(dq)
        dqk_ref[:, 1, rows, at] = shaped(dk)
        of_query += gain_part(dq, queries[number])
        of_key += gain_part(dk, singles[number])
    add_gains(sums_ref, of_query, of_key)


def time_specs(inner):
    double = pl.BlockSpec((FRAMES, 2, CELLS_HERE, WIDE), lambda n: (0, 0, 0, n))
    single = pl.BlockSpec((FRAMES, CELLS_HERE, WIDE), lambda n: (0, 0, n))
    return (
        double,
        single,
        jax.ShapeDtypeStruct((FRAMES, 2, CELLS_HERE, inner), BF),
        jax.ShapeDtypeStruct((FRAMES, CELLS_HERE, inner), BF),
    )


def time_forward(counts, normed, arrived):
    inner = arrived.shape[3]
    double, single, _, single_shape = time_specs(inner)
    return pl.pallas_call(
        time_kernel,
        grid=(inner // WIDE,),
        in_specs=[SMEM, double, double],
        out_specs=single,
        out_shape=single_shape,
        compiler_params=PARAMS,
        cost_estimate=cost(5),
        name="time_forward",
    )(counts, normed, arrived)


def time_back(counts, normed, arrived):
    inner = arrived.shape[3]
    double, single, double_shape, single_shape = time_specs(inner)
    return pl.pallas_call(
        time_back_kernel,
        grid=(inner // WIDE,),
        in_specs=[SMEM, double, double],
        out_specs=[double, single, pl.BlockSpec((8, LANES), lambda n: (0, 0))],
        out_shape=[double_shape, single_shape, jax.ShapeDtypeStruct((8, LANES), F32)],
        compiler_params=PARAMS,
        cost_estimate=cost(6.5),
        name="time_back",
    )(counts, normed, arrived)


def norm_back_kernel(
    hat_q_ref,
    hat_k_ref,
    inverse_q_ref,
    inverse_k_ref,
    gain_q_ref,
    gain_k_ref,
    dq_ref,
    dk_ref,
    late_ref,
    gq_ref,
    gk_ref,
):
    twice = head_ones(DUO, LANES)
    for left in range(0, NORM_WIDE, LANES):
        at = slice(left, left + LANES)
        for number, (hat_ref, inverse_ref, gain_ref, early, target) in enumerate(
            (
                (hat_q_ref, inverse_q_ref, gain_q_ref, dq_ref, gq_ref),
                (hat_k_ref, inverse_k_ref, gain_k_ref, dk_ref, gk_ref),
            )
        ):
            hat = hat_ref[:, at]
            late = late_ref[:, number, :, at].reshape(CELLS, LANES)
            scaled = (early[:, at] + late.astype(F32)) * both_heads(gain_ref)
            mean = head_mean(scaled, twice)
            dinput = scaled - mean - hat * head_mean(scaled * hat, twice)
            target[:, at] = (inverse_ref[:, at] * dinput).astype(BF)


def norm_back(hats, gain_query, gain_key, dq, dk, late):
    inner = dq.shape[1]
    tokens = pl.BlockSpec((CELLS, NORM_WIDE), lambda n: (0, n))
    gain = pl.BlockSpec((1, HD), lambda n: (0, 0))
    grads = jax.ShapeDtypeStruct((CELLS, inner), BF)
    return pl.pallas_call(
        norm_back_kernel,
        grid=(inner // NORM_WIDE,),
        in_specs=[
            tokens,
            tokens,
            tokens,
            tokens,
            gain,
            gain,
            tokens,
            tokens,
            pl.BlockSpec((FRAMES, 2, CELLS_HERE, NORM_WIDE), lambda n: (0, 0, 0, n)),
        ],
        out_specs=[tokens, tokens],
        out_shape=[grads, grads],
        compiler_params=PARAMS,
        cost_estimate=cost(7),
        name="norm_back",
    )(*hats, gain_query, gain_key, dq, dk, late)


def grad_mixed_kernel(cot_ref, weight_ref, out_ref):
    out_ref[...] = nt(cot_ref[...], weight_ref[...]).astype(BF)


def grad_mixed_of(cotangent, weight):
    inner, width = weight.shape
    return pl.pallas_call(
        grad_mixed_kernel,
        grid=(inner // WIDE,),
        in_specs=[
            pl.BlockSpec((CELLS, width), lambda n: (0, 0)),
            pl.BlockSpec((WIDE, width), lambda n: (n, 0)),
        ],
        out_specs=pl.BlockSpec((CELLS, WIDE), lambda n: (0, n)),
        out_shape=jax.ShapeDtypeStruct((CELLS, inner), BF),
        compiler_params=PARAMS,
        cost_estimate=cost(8.7),
        name="grad_mixed",
    )(cotangent, weight)


def project_kernel(mixed_ref, weight_ref, out_ref):
    out_ref[...] = nn(mixed_ref[...], weight_ref[...]).astype(BF)


def project(mixed, weight):
    inner, width = weight.shape
    block = width // 4
    return pl.pallas_call(
        project_kernel,
        grid=(4,),
        in_specs=[
            pl.BlockSpec((CELLS, inner), lambda n: (0, 0)),
            pl.BlockSpec((inner, block), lambda n: (0, n)),
        ],
        out_specs=pl.BlockSpec((CELLS, block), lambda n: (0, n)),
        out_shape=jax.ShapeDtypeStruct((CELLS, width), BF),
        compiler_params=PARAMS,
        cost_estimate=cost(7),
        name="project",
    )(mixed, weight)


TAIL = 16


def weight_kernel(place_ref, order_ref, mixed_ref, cot_ref, out_ref, turned, product):
    shares, rows, _ = out_ref.shape
    own = (rows - TAIL) // 4

    @pl.when(pl.program_id(0) == 0)
    def _():
        turned[...] = nt(order_ref[0], mixed_ref[...]).astype(BF)

    product[...] = nn(turned[...], cot_ref[...])
    for quarter in range(4):

        @pl.when(pl.program_id(0) == quarter)
        def _():
            for share in range(shares):
                out_ref[share, quarter * own : (quarter + 1) * own] = product[
                    share * own : (share + 1) * own
                ].astype(BF)


def weight_parts(place, order, mixed, cotangents, shares):
    tokens, width = cotangents.shape
    _, features, wide = order.shape
    block = width // 4
    rows = 4 * (features // shares) + TAIL
    return pl.pallas_call(
        weight_kernel,
        grid_spec=pltpu.PrefetchScalarGridSpec(
            num_scalar_prefetch=1,
            grid=(4,),
            in_specs=[
                pl.BlockSpec((1, features, wide), lambda n, place: (place[1], 0, 0)),
                pl.BlockSpec((tokens, wide), lambda n, place: (0, place[0])),
                pl.BlockSpec((tokens, block), lambda n, place: (0, n)),
            ],
            out_specs=pl.BlockSpec((shares, rows, block), lambda n, place: (0, 0, 0)),
            scratch_shapes=[
                pltpu.VMEM((features, tokens), BF),
                pltpu.VMEM((features, block), F32),
            ],
        ),
        out_shape=jax.ShapeDtypeStruct((shares, rows, block), BF),
        compiler_params=PARAMS,
        cost_estimate=cost(9.5),
        name="weight_parts",
    )(place, order, mixed, cotangents)


def tail_kernel(gain_ref, _, out_ref):
    terms = []
    for row in range(2):
        rest = gain_ref[row : row + 1]
        for _ in range(3):
            terms.append(rest.astype(BF).astype(F32))
            rest = rest - terms[-1]
    block = out_ref.shape[2]
    rows = jnp.concatenate(terms + [jnp.zeros((TAIL - 6, LANES), F32)], 0)
    rows = jnp.concatenate([rows, jnp.zeros((TAIL, block - LANES), F32)], 1).astype(BF)
    for share in range(out_ref.shape[0]):
        out_ref[share] = rows


def add_tail(gain_sums, parts):
    shares, rows, block = parts.shape
    return pl.pallas_call(
        tail_kernel,
        grid=(1,),
        in_specs=[
            pl.BlockSpec(gain_sums.shape, lambda n: (0, 0)),
            pl.BlockSpec(memory_space=pl.ANY),
        ],
        out_specs=pl.BlockSpec((shares, TAIL, block), lambda n: (0, rows // TAIL - 1, 0)),
        out_shape=jax.ShapeDtypeStruct(parts.shape, BF),
        input_output_aliases={1: 0},
        compiler_params=PARAMS,
        cost_estimate=cost(1.5),
        name="add_tail",
    )(gain_sums, parts)


def sum_kernel(parts_ref, out_ref, gain_ref):
    shares, rows, block = parts_ref.shape
    own = (rows - TAIL) // 4
    total = parts_ref[0].astype(F32)
    for share in range(1, shares):
        total = total + parts_ref[share].astype(F32)
    for quarter in range(4):
        out_ref[:, quarter * block : (quarter + 1) * block] = total[
            quarter * own : (quarter + 1) * own
        ]
    gain_ref[...] = total[rows - TAIL : rows - TAIL + 8, :LANES]


def sum_parts(parts):
    _, rows, block = parts.shape
    return pl.pallas_call(
        sum_kernel,
        in_specs=[VMEM],
        out_specs=[VMEM, VMEM],
        out_shape=[
            jax.ShapeDtypeStruct(((rows - TAIL) // 4, 4 * block), F32),
            jax.ShapeDtypeStruct((8, LANES), F32),
        ],
        compiler_params=PARAMS,
        cost_estimate=cost(2.2),
        name="sum_parts",
    )(parts)


def feature_order(inner, planes, cores, shares):
    wide = inner // planes
    features = wide // cores
    own = features // shares
    order = np.zeros((cores, features, wide), np.float32)
    for core in range(cores):
        for feature in range(features):
            share, row = divmod(feature, own)
            order[core, feature, own * (cores * share + core) + row] = 1.0
    return jnp.asarray(order, BF)


def local(
    queries,
    keys_proj,
    values_proj,
    gain_query,
    gain_key,
    frame_counts,
    heights,
    widths,
    out_weight,
    cotangent,
):
    seq = ("y", "core")
    group = ("x", "core")
    sums = ("z", "y")
    planes, cores = lax.axis_size("x"), lax.axis_size("core")
    shares = lax.axis_size("z") * lax.axis_size("y")
    inner = out_weight.shape[0]
    rank = lax.axis_index(seq).astype(jnp.int32)
    counts = jnp.stack([frame_counts[0], heights[0], widths[0], rank])
    gains = gain_query.reshape(1, HD), gain_key.reshape(1, HD)
    query_rows, key_rows, value_rows = queries[0, 0], keys_proj[0, 0], values_proj[0, 0]
    cot_rows = cotangent[0, 0]
    by_cells = (FRAMES, CELLS_HERE, inner)

    def exchange(tensor, axes):
        return lax.all_to_all(tensor, axes, split_axis=0, concat_axis=0, tiled=True)

    def after(tensor, earlier):
        return lax.optimization_barrier((tensor, earlier))[0]

    cotangents = lax.all_gather(cot_rows, group, axis=0, tiled=True)
    normed = norm(query_rows, key_rows, *gains)
    normed_cells = exchange(normed, seq)
    grad_mixed = grad_mixed_of(cot_rows, out_weight)
    outgoing, chances = space_forward(counts, normed, value_rows, grad_mixed)
    arrived = exchange(after(outgoing, normed_cells), seq)
    hats = hats_of(*lax.optimization_barrier((query_rows, key_rows, outgoing))[:2])
    arrived, *hats = lax.optimization_barrier((arrived, *hats))
    mixed_cells = time_forward(counts, normed_cells, arrived)
    mixed = exchange(mixed_cells, seq).reshape(CELLS, inner)
    late_cells, dspatial_cells, late_gains = time_back(counts, normed_cells, arrived)
    place = jnp.stack([lax.axis_index("x"), lax.axis_index("core")]).astype(jnp.int32)
    first = (cotangents, dspatial_cells)
    gathered = lax.all_gather(after(mixed, first), group, axis=0, tiled=True)
    dspatial = exchange(after(dspatial_cells, mixed), seq).reshape(CELLS, inner)
    late = exchange(after(late_cells, dspatial), seq)
    block_out = project(mixed, out_weight)
    order = feature_order(inner, planes, cores, shares)
    parts = weight_parts(place, order, gathered, cotangents, shares)
    dq, dk, grad_values, early_gains = space_back(
        hats[0], hats[1], normed, value_rows, dspatial, chances
    )
    late_scale = jnp.stack([gain_query * SCALE, gain_key])
    late_scale = jnp.pad(jnp.tile(late_scale, (1, 2)), ((0, 6), (0, 0)), constant_values=1.0)
    gain_sums = early_gains + late_gains / late_scale
    for axis, extent in (("core", cores), ("x", planes)):
        flip = 1
        while flip < extent:
            pairs = [(i, i ^ flip) for i in range(extent)]
            gain_sums = gain_sums + lax.ppermute(gain_sums, axis, pairs)
            flip *= 2
    grad_queries, grad_keys = norm_back(hats, *gains, dq, dk, late)
    parts = exchange(after(add_tail(gain_sums, parts), late), sums)
    grad_weight, tail = sum_parts(parts)
    gain_sums = jnp.stack([jnp.sum(tail[:3], 0), jnp.sum(tail[3:6], 0)])
    gain_sums = gain_sums[:, :HD] + gain_sums[:, HD:]
    return (
        block_out.reshape(cotangent.shape),
        grad_queries.reshape(queries.shape),
        grad_keys.reshape(queries.shape),
        grad_values.reshape(queries.shape),
        grad_weight,
        gain_sums[0],
        gain_sums[1],
    )


def solution(mesh):
    planes = 4 if mesh.shape["dp"] == 16 else mesh.shape["dp"]
    fine = Mesh(
        mesh.devices.reshape(planes, mesh.shape["dp"] // planes, -1, 2), ("x", "z", "y", "core")
    )
    tokens = P(("x", "z"), ("y", "core"), None, None)
    clips = P(("x", "z"))
    return jax.shard_map(
        local,
        mesh=fine,
        in_specs=(tokens, tokens, tokens, P(), P(), clips, clips, clips, P(), tokens),
        out_specs=(
            tokens,
            tokens,
            tokens,
            tokens,
            P(("x", "z", "y", "core"), None),
            P(),
            P(),
        ),
        check_vma=False,
    )
```

time: 1020 us -> 187 us (0.18); the launches traced: 999 us -> 185 us
  blocking collectives: 440 us -> 17.5 us
  local copies, waits for them, and re-layouts: 225 us -> 6.18 us
  starting transfers between devices: 174 us -> 28.5 us
  matrix products: 98.7 us -> 0 us
  Pallas kernels: 0 us -> 74.4 us
  other arithmetic: 57.7 us -> 3.34 us
  waiting for transfers between devices: 0.11 us -> 39.5 us
  between operations: 3.97 us -> 16.1 us
    unnamed x1 -> x0, blocking collectives: 369 us -> none
    unnamed x82 -> x16, local copies, waits for them, and re-layouts: 145 us -> 5.57 us
    unnamed x32 -> x0, starting transfers between devices: 125 us -> none
    dot_general x14 -> x0, matrix products: 92.3 us -> none  [the longest x11 69.3 us: product(): return jnp.einsum(form, left, right, preferred_element_type=jnp.float32)]
    pallas_call x0 -> x12, Pallas kernels: none -> 74.4 us  [the longest x1 9.71 us: weight_parts(): pl.pallas_call(weight_kernel, grid_spec=pltpu.PrefetchScalarGridSpec(num_...]
    psum x1 -> x0, blocking collectives: 70.7 us -> none  [local(): lax.psum((gain_q_part, gain_k_part), ('dp', 'seq'))]
    convert_element_type x18 -> x0, local copies, waits for them, and re-layouts: 56.5 us -> none  [the longest x3 9.62 us: attend(): return result.reshape(value_rows.shape).astype(jnp.bfloat16)]
    all_to_all x8 -> x5, waiting for transfers between devices: 0.02 us -> 34.2 us  [exchange(): return lax.all_to_all(tensor, axes, split_axis=0, concat_axis=0, tiled=True)]
  transfers between devices with their start and end apart: 40 -> 10, of which waited for: 0 -> 7; matrix products, arithmetic and copies ran while one was open for 59% -> 1% of each run, Pallas kernels for 0% -> 39%
where the time goes in v1:
time: 187 us; the launch traced here: 185 us
  Pallas kernels  74.4 us (40%)
  waiting for transfers between devices  39.5 us (21%)
  starting transfers between devices  28.5 us (15%)
  blocking collectives  17.5 us (9%)
  between operations  16.1 us (9%)
  local copies, waits for them, and re-layouts  6.18 us (3%)
  other arithmetic  3.34 us (2%)
    all_to_all x5, waiting for transfers between devices, exchange(): return lax.all_to_all(tensor, axes, split_axis=0, concat_axis=0, tiled=True)  34.2 us
    all_to_all x5, starting transfers between devices, exchange(): return lax.all_to_all(tensor, axes, split_axis=0, concat_axis=0, tiled=True)  23.6 us
    all_to_all x1, blocking collectives, exchange(): return lax.all_to_all(tensor, axes, split_axis=0, concat_axis=0, tiled=True)  17.5 us
    pallas_call x1, Pallas kernels, weight_parts(): pl.pallas_call(weight_kernel, grid_spec=pltpu.PrefetchScalarGridSpec(num_...  9.71 us
    pallas_call x1, Pallas kernels, space_back(): pl.pallas_call(space_back_kernel, grid=(inner // WIDE,), in_specs=[tokens...  9.18 us
    pallas_call x1, Pallas kernels, grad_mixed_of(): pl.pallas_call(grad_mixed_kernel, grid=(inner // WIDE,), in_specs=[pl.Blo...  8.65 us
    pallas_call x1, Pallas kernels, space_forward(): pl.pallas_call(space_kernel, grid=(inner // WIDE,), in_specs=[SMEM, pl.Bl...  7.05 us
    pallas_call x1, Pallas kernels, project(): pl.pallas_call(project_kernel, grid=(4,), in_specs=[pl.BlockSpec((CELLS,...  6.98 us
  transfers between devices with their start and end apart: 10, of which 7 were waited for; matrix products, arithmetic and copies ran while one was open for 1% of the time, Pallas kernels for 39%

profile of v1, /device:TPU:0, one launch (start us, length us, event | category | flops | bytes accessed | tf_op | source)
XLA Modules:
  0.0 185.4 jit_solution(4264416224884504805)
XLA Ops:
  7.2 0.0 all-gather.6.cloned.1.call-start
  7.2 0.7 all-gather.6.cloned.1.call-update
  7.9 5.0 %norm.1.qk_ref = bf16[8,2,32,1536]{3,2,1,0:T(8,128)(2,1)} custom-call(bf16[256,1536]{1,0:T(8,128)(2,1)} %bitcast.29, bf16[256,1536]{1,0:T(8,128)(2,1)} %bitcast.31, f32[1,64]{1,0:T(1,128)} %bitcast.39, f32[1,64]{1,0:T(1,128)} %bitcast.36), custom_call_target="tpu_custom_call" | custom-call | bytes 18450000 | tf_op jit(solution)/shard_map/norm/pallas_call | solution.py:131
  12.9 4.6 %all-to-all-start = ((bf16[8,2,32,1536]{3,2,1,0:T(8,128)(2,1)}), bf16[8,2,32,1536]{3,2,1,0:T(8,128)(2,1)S(1)}, u32[]{:S(2)}, u32[]{:S(2)}) async-start(bf16[8,2,32,1536]{3,2,1,0:T(8,128)(2,1)} %norm.1.qk_ref), calls=%async_computation | async-start | bytes 3145728 | tf_op jit(solution)/shard_map/all_to_all | solution.py:647
  19.4 8.6 %grad_mixed.1.gm_ref = bf16[256,1536]{1,0:T(8,128)(2,1)} custom-call(bf16[256,3072]{1,0:T(8,128)(2,1)} %bitcast.27, bf16[1536,3072]{1,0:T(8,128)(2,1)} %weight_ref.3), custom_call_target="tpu_custom_call" | custom-call | bytes 32103000 | tf_op jit(solution)/shard_map/grad_mixed/pallas_call | solution.py:461
  28.0 0.6 pad_add_fusion.counts_ref
  28.6 7.0 %space_forward.1 = (bf16[8,2,32,1536]{3,2,1,0:T(8,128)(2,1)}, f32[12,512,256]{2,1,0:T(8,128)}) custom-call(s32[4]{0:T(128)} %pad_add_fusion.counts_ref, bf16[8,2,32,1536]{3,2,1,0:T(8,128)(2,1)} %norm.1.qk_ref, bf16[256,1536]{1,0:T(8,128)(2,1)} %bitcast.33, bf16[256,1536]{1,0:T(8,128)(2,1)} %grad_mixed.1.gm_ref), custom_call_target="tpu_custom_call" | custom-call | bytes 25830000 | tf_op jit(solution)/shard_map/space_forward/pallas_call | solution.py:195
  35.7 3.4 %all-to-all-done.qk_ref = bf16[8,2,32,1536]{3,2,1,0:T(8,128)(2,1)S(1)} async-done(((bf16[8,2,32,1536]{3,2,1,0:T(8,128)(2,1)}), bf16[8,2,32,1536]{3,2,1,0:T(8,128)(2,1)S(1)}, u32[]{:S(2)}, u32[]{:S(2)}) %all-to-all-start) | async-done | bytes 1572896 | tf_op jit(solution)/shard_map/all_to_all | solution.py:647
  39.0 1.2 copy-done
  40.2 3.6 %all-to-all-start.1 = ((bf16[8,2,32,1536]{3,2,1,0:T(8,128)(2,1)}), bf16[8,2,32,1536]{3,2,1,0:T(8,128)(2,1)S(1)}, u32[]{:S(2)}, u32[]{:S(2)}) async-start(bf16[8,2,32,1536]{3,2,1,0:T(8,128)(2,1)} %get-tuple-element.37), calls=%async_computation.1 | async-start | bytes 3145728 | tf_op jit(solution)/shard_map/all_to_all | solution.py:647
  43.8 5.7 %hats.1 = (f32[256,1536]{1,0:T(8,128)}, f32[256,1536]{1,0:T(8,128)}, f32[256,1536]{1,0:T(8,128)}, f32[256,1536]{1,0:T(8,128)}) custom-call(bf16[256,1536]{1,0:T(8,128)(2,1)} %bitcast.30, bf16[256,1536]{1,0:T(8,128)(2,1)} %bitcast.32), custom_call_target="tpu_custom_call" | custom-call | bytes 20664000 | tf_op jit(solution)/shard_map/hats/pallas_call | solution.py:156
  49.4 15.8 %all-to-all-done.1.sg_ref = bf16[8,2,32,1536]{3,2,1,0:T(8,128)(2,1)S(1)} async-done(((bf16[8,2,32,1536]{3,2,1,0:T(8,128)(2,1)}), bf16[8,2,32,1536]{3,2,1,0:T(8,128)(2,1)S(1)}, u32[]{:S(2)}, u32[]{:S(2)}) %all-to-all-start.1) | async-done | bytes 1572896 | tf_op jit(solution)/shard_map/all_to_all | solution.py:647
  65.3 1.1 copy-done.1
  66.4 5.0 %time_forward.1 = bf16[8,32,1536]{2,1,0:T(8,128)(2,1)} custom-call(s32[4]{0:T(128)} %pad_add_fusion.counts_ref, bf16[8,2,32,1536]{3,2,1,0:T(8,128)(2,1)} %copy-done, bf16[8,2,32,1536]{3,2,1,0:T(8,128)(2,1)} %copy-done.1), custom_call_target="tpu_custom_call" | custom-call | bytes 18450000 | tf_op jit(solution)/shard_map/time_forward/pallas_call | solution.py:371
  71.5 3.5 %all-to-all-start.2 = ((bf16[8,32,1536]{2,1,0:T(8,128)(2,1)}), bf16[8,32,1536]{2,1,0:T(8,128)(2,1)S(1)}, u32[]{:S(2)}, u32[]{:S(2)}) async-start(bf16[8,32,1536]{2,1,0:T(8,128)(2,1)} %time_forward.1), calls=%async_computation.2 | async-start | bytes 1572864 | tf_op jit(solution)/shard_map/all_to_all | solution.py:647
  75.0 0.0 all-gather.4.cloned.1.call-start
  75.1 6.5 %time_back.1 = (bf16[8,2,32,1536]{3,2,1,0:T(8,128)(2,1)}, bf16[8,32,1536]{2,1,0:T(8,128)(2,1)}, f32[8,128]{1,0:T(8,128)}) custom-call(s32[4]{0:T(128)} %pad_add_fusion.counts_ref, bf16[8,2,32,1536]{3,2,1,0:T(8,128)(2,1)} %copy-done, bf16[8,2,32,1536]{3,2,1,0:T(8,128)(2,1)} %copy-done.1), custom_call_target="tpu_custom_call" | custom-call | bytes 23985000 | tf_op jit(solution)/shard_map/time_back/pallas_call | solution.py:386
  81.6 6.5 %all-to-all-done.2 = bf16[8,32,1536]{2,1,0:T(8,128)(2,1)S(1)} async-done(((bf16[8,32,1536]{2,1,0:T(8,128)(2,1)}), bf16[8,32,1536]{2,1,0:T(8,128)(2,1)S(1)}, u32[]{:S(2)}, u32[]{:S(2)}) %all-to-all-start.2) | async-done | bytes 786464 | tf_op jit(solution)/shard_map/all_to_all | solution.py:647
  88.1 0.9 copy-done.2
  89.0 0.0 all-gather.4.cloned.1.call-update
  89.0 17.5 %all_to_all.30 = bf16[8,32,1536]{2,1,0:T(8,128)(2,1)} all-to-all(bf16[8,32,1536]{2,1,0:T(8,128)(2,1)} %get-tuple-element.50), channel_id=1, replica_groups=mesh['x'=4,'z'=4,'y'=4,'core'=2] {'y','core'}, dimensions={0} | all-to-all | bytes 1572864 | tf_op jit(solution)/shard_map/all_to_all | solution.py:647
  106.5 3.7 %all-to-all-start.4 = ((bf16[8,2,32,1536]{3,2,1,0:T(8,128)(2,1)}), bf16[8,2,32,1536]{3,2,1,0:T(8,128)(2,1)S(1)}, u32[]{:S(2)}, u32[]{:S(2)}) async-start(bf16[8,2,32,1536]{3,2,1,0:T(8,128)(2,1)} %get-tuple-element.55), calls=%async_computation.4 | async-start | bytes 3145728 | tf_op jit(solution)/shard_map/all_to_all | solution.py:647
  110.2 0.0 copy-done.7
  110.2 0.0 copy-done.5
  110.3 0.1 tile.10
  110.3 9.2 %space_back.1 = (f32[256,1536]{1,0:T(8,128)}, f32[256,1536]{1,0:T(8,128)}, bf16[256,1536]{1,0:T(8,128)(2,1)}, f32[8,128]{1,0:T(8,128)}) custom-call(f32[256,1536]{1,0:T(8,128)} %get-tuple-element.45.hat_q_ref, f32[256,1536]{1,0:T(8,128)} %get-tuple-element.46.hat_k_ref, bf16[8,2,32,1536]{3,2,1,0:T(8,128)(2,1)} %norm.1.qk_ref, bf16[256,1536]{1,0:T(8,128)(2,1)} %bitcast.34, ...), custom_call_target="tpu_custom_call" | custom-call | bytes 33210000 | tf_op jit(solution)/shard_map/space_back/pallas_call | solution.py:259
  119.5 0.7 divide_add_fusion
  120.2 0.3 collective-permute-start
  120.5 0.9 collective-permute-done
  121.4 1.5 collective-permute-start.1
  122.9 2.2 %collective-permute-done.1 = f32[8,128]{1,0:T(8,128)S(1)} collective-permute-done((f32[8,128]{1,0:T(8,128)S(1)}, f32[8,128]{1,0:T(8,128)S(1)}, u32[]{:S(2)}, u32[]{:S(2)}) %collective-permute-start.1) | collective-permute-done | bytes 4128 | tf_op jit(solution)/shard_map/ppermute | solution.py:681
  125.1 3.0 %collective-permute-start.2 = (f32[8,128]{1,0:T(8,128)S(1)}, f32[8,128]{1,0:T(8,128)S(1)}, u32[]{:S(2)}, u32[]{:S(2)}) collective-permute-start(f32[8,128]{1,0:T(8,128)S(1)} %add.23), channel_id=1, source_target_pairs={{0,64},{32,96},{64,0},{96,32},{1,65},{33,97},{65,1},{97,33},{2,66}... | collective-permute-start | bytes 12296 | tf_op jit(solution)/shard_map/ppermute | solution.py:681
  128.1 0.6 pad_add_fusion.1.place_ref
  128.7 1.5 collective-permute-done.2
  130.2 0.6 add.24.gain_ref
  130.8 9.7 %weight_parts.1._ = bf16[16,64,768]{2,1,0:T(8,128)(2,1)} custom-call(s32[2]{0:T(128)} %pad_add_fusion.1.place_ref, bf16[2,192,384]{2,1,0:T(8,128)(2,1)} %constant.22.clone.order_ref, bf16[2048,1536]{1,0:T(8,128)(2,1)} %all-gather.4.cloned.1.call-done.mixed_ref, bf16[2048,3072]{1,0:T(8,128)(2,1)} %bitcast.24), custom_call_target="tpu_custom_call" | custom-call | bytes 35055000 | tf_op jit(solution)/shard_map/weight_parts/pallas_call | solution.py:525
  140.5 1.5 add_tail.1
  142.0 0.0 all-to-all-done.4.late_ref
  142.0 1.2 copy-done.4
  143.2 8.2 %all-to-all-start.5 = ((bf16[16,64,768]{2,1,0:T(8,128)(2,1)}), bf16[16,64,768]{2,1,0:T(8,128)(2,1)S(1)}, u32[]{:S(2)}, u32[]{:S(2)}) async-start(bf16[16,64,768]{2,1,0:T(8,128)(2,1)} %add_tail.1), calls=%async_computation.5 | async-start | bytes 3145728 | tf_op jit(solution)/shard_map/all_to_all | solution.py:647
  151.4 7.0 %project.1 = bf16[256,3072]{1,0:T(8,128)(2,1)} custom-call(bf16[256,1536]{1,0:T(8,128)(2,1)} %bitcast.26, bf16[1536,3072]{1,0:T(8,128)(2,1)} %weight_ref.3), custom_call_target="tpu_custom_call" | custom-call | bytes 25830000 | tf_op jit(solution)/shard_map/project/pallas_call | solution.py:483
  158.4 6.9 %norm_back.1 = (bf16[256,1536]{1,0:T(8,128)(2,1)}, bf16[256,1536]{1,0:T(8,128)(2,1)}) custom-call(f32[256,1536]{1,0:T(8,128)} %get-tuple-element.45.hat_q_ref, f32[256,1536]{1,0:T(8,128)} %get-tuple-element.46.hat_k_ref, f32[256,1536]{1,0:T(8,128)} %get-tuple-element.47.inverse_q_ref, f32[256,1536]{1,0:T(8,128)} %get-tuple-element.48.inverse_k_ref, ...), custom_call_target="tpu_custom_call" | custom-call | bytes 25830000 | tf_op jit(solution)/shard_map/norm_back/pallas_call | solution.py:433
  165.3 8.4 %all-to-all-done.5.parts_ref = bf16[16,64,768]{2,1,0:T(8,128)(2,1)S(1)} async-done(((bf16[16,64,768]{2,1,0:T(8,128)(2,1)}), bf16[16,64,768]{2,1,0:T(8,128)(2,1)S(1)}, u32[]{:S(2)}, u32[]{:S(2)}) %all-to-all-start.5) | async-done | bytes 1572896 | tf_op jit(solution)/shard_map/all_to_all | solution.py:647
  173.8 1.2 copy-done.3
  174.9 2.2 %sum_parts.1 = (f32[12,3072]{1,0:T(8,128)}, f32[8,128]{1,0:T(8,128)}) custom-call(bf16[16,64,768]{2,1,0:T(8,128)(2,1)} %copy-done.3), custom_call_target="tpu_custom_call" | custom-call | bytes 8118000 | tf_op jit(solution)/shard_map/sum_parts/pallas_call | solution.py:595
  177.2 0.8 slice_reduce_fusion.1
  178.0 0.1 slice_add_fusion
  178.0 0.5 slice_bitcast_fusion
  (17 shorter events, 0.1 us)
Async XLA Ops:
  7.2 80.9 %all-gather.6.cloned.1.call-start = ((), (), s32[]{:S(2)}) async-start(), calls=%async_computation.7 | async-start | bytes 14155776 | tf_op jit(solution)/shard_map/all_gather | solution.py:652
  12.9 26.1 %all-to-all-start = ((bf16[8,2,32,1536]{3,2,1,0:T(8,128)(2,1)}), bf16[8,2,32,1536]{3,2,1,0:T(8,128)(2,1)S(1)}, u32[]{:S(2)}, u32[]{:S(2)}) async-start(bf16[8,2,32,1536]{3,2,1,0:T(8,128)(2,1)} %norm.1.qk_ref), calls=%async_computation | async-start | bytes 3145728 | tf_op jit(solution)/shard_map/all_to_all | solution.py:647
  39.0 1.2 copy-start
  40.2 25.1 %all-to-all-start.1 = ((bf16[8,2,32,1536]{3,2,1,0:T(8,128)(2,1)}), bf16[8,2,32,1536]{3,2,1,0:T(8,128)(2,1)S(1)}, u32[]{:S(2)}, u32[]{:S(2)}) async-start(bf16[8,2,32,1536]{3,2,1,0:T(8,128)(2,1)} %get-tuple-element.37), calls=%async_computation.1 | async-start | bytes 3145728 | tf_op jit(solution)/shard_map/all_to_all | solution.py:647
  65.3 1.1 copy-start.1
  71.5 16.6 %all-to-all-start.2 = ((bf16[8,32,1536]{2,1,0:T(8,128)(2,1)}), bf16[8,32,1536]{2,1,0:T(8,128)(2,1)S(1)}, u32[]{:S(2)}, u32[]{:S(2)}) async-start(bf16[8,32,1536]{2,1,0:T(8,128)(2,1)} %time_forward.1), calls=%async_computation.2 | async-start | bytes 1572864 | tf_op jit(solution)/shard_map/all_to_all | solution.py:647
  75.0 55.7 %all-gather.4.cloned.1.call-start = ((), (), s32[]{:S(2)}) async-start(), calls=%async_computation.6 | async-start | bytes 7077888 | tf_op jit(solution)/shard_map/all_gather | solution.py:665
  88.1 0.9 copy-start.2
  106.5 3.7 %copy-start.7 = (f32[64]{0:T(128)S(1)}, f32[64]{0:T(128)}, u32[]{:S(2)}) copy-start(f32[64]{0:T(128)} %param.14) | copy-start | bytes 772
  106.5 3.8 %copy-start.5 = (f32[64]{0:T(128)S(1)}, f32[64]{0:T(128)}, u32[]{:S(2)}) copy-start(f32[64]{0:T(128)} %param.15) | copy-start | bytes 772
  106.5 35.5 %all-to-all-start.4 = ((bf16[8,2,32,1536]{3,2,1,0:T(8,128)(2,1)}), bf16[8,2,32,1536]{3,2,1,0:T(8,128)(2,1)S(1)}, u32[]{:S(2)}, u32[]{:S(2)}) async-start(bf16[8,2,32,1536]{3,2,1,0:T(8,128)(2,1)} %get-tuple-element.55), calls=%async_computation.4 | async-start | bytes 3145728 | tf_op jit(solution)/shard_map/all_to_all | solution.py:647
  110.3 9.2 %copy-start.6 = (f32[8,128]{1,0:T(8,128)S(1)}, f32[8,128]{1,0:T(8,128)}, u32[]{:S(2)}) copy-start(f32[8,128]{1,0:T(8,128)} %get-tuple-element.60) | copy-start | bytes 12292
  120.2 1.2 collective-permute-start
  121.4 3.7 %collective-permute-start.1 = (f32[8,128]{1,0:T(8,128)S(1)}, f32[8,128]{1,0:T(8,128)S(1)}, u32[]{:S(2)}, u32[]{:S(2)}) collective-permute-start(f32[8,128]{1,0:T(8,128)S(1)} %add.22), channel_id=1, source_target_pairs={{0,32},{32,0},{64,96},{96,64},{1,33},{33,1},{65,97},{97,65},{2,34}... | collective-permute-start | bytes 12296 | tf_op jit(solution)/shard_map/ppermute | solution.py:681
  125.1 5.1 %collective-permute-start.2 = (f32[8,128]{1,0:T(8,128)S(1)}, f32[8,128]{1,0:T(8,128)S(1)}, u32[]{:S(2)}, u32[]{:S(2)}) collective-permute-start(f32[8,128]{1,0:T(8,128)S(1)} %add.23), channel_id=1, source_target_pairs={{0,64},{32,96},{64,0},{96,32},{1,65},{33,97},{65,1},{97,33},{2,66}... | collective-permute-start | bytes 12296 | tf_op jit(solution)/shard_map/ppermute | solution.py:681
  142.0 1.2 copy-start.4
  143.2 30.6 %all-to-all-start.5 = ((bf16[16,64,768]{2,1,0:T(8,128)(2,1)}), bf16[16,64,768]{2,1,0:T(8,128)(2,1)S(1)}, u32[]{:S(2)}, u32[]{:S(2)}) async-start(bf16[16,64,768]{2,1,0:T(8,128)(2,1)} %add_tail.1), calls=%async_computation.5 | async-start | bytes 3145728 | tf_op jit(solution)/shard_map/all_to_all | solution.py:647
  173.8 1.2 copy-start.3
Sparse Core Ops, SparseCore 0:
  9.7 69.7 all-gather.5
  89.1 41.2 all-gather.3

commit v2 on v1

--- a/solution.py
+++ b/solution.py
@@ -20,7 +20,7 @@
 BLOCK = 16
 NEG = -1e30
 SCALE = HD**-0.5
-PARAMS = pltpu.CompilerParams(vmem_limit_bytes=56 * 1024 * 1024)
+PARAMS = pltpu.CompilerParams(vmem_limit_bytes=60 * 1024 * 1024)
 
 
 def cost(microseconds):
@@ -98,16 +98,16 @@
     return hats, inverses
 
 
+def both_heads(gain_ref):
+    return jnp.concatenate([gain_ref[...], gain_ref[...]], 1)
+
+
 def pair_slice(number):
     return slice(number * LANES, (number + 1) * LANES)
 
 
 NORM_WIDE = 512
 DUO = 2 * LANES
-
-
-def both_heads(gain_ref):
-    return jnp.concatenate([gain_ref[...], gain_ref[...]], 1)
 
 
 def norm_kernel(q_ref, k_ref, gain_q_ref, gain_k_ref, out_ref):
@@ -219,18 +219,34 @@
     return jnp.sum(grad * normed.astype(F32), 0, keepdims=True)
 
 
-def add_gains(sums_ref, of_query, of_key):
+def add_gains(sums_ref, of_query, of_key, begin=None):
     @pl.when(pl.program_id(0) == 0)
     def _():
-        sums_ref[...] = jnp.zeros_like(sums_ref)
+        sums_ref[...] = jnp.zeros_like(sums_ref) if begin is None else begin()
 
     sums_ref[0:1] += of_query
     sums_ref[1:2] += of_key
 
 
 def space_back_kernel(
-    hat_q_ref, hat_k_ref, qk_ref, v_ref, up_ref, chances_ref, dq_ref, dk_ref, dv_ref, sums_ref
+    late_ref,
+    gain_q_ref,
+    gain_k_ref,
+    hat_q_ref,
+    hat_k_ref,
+    qk_ref,
+    v_ref,
+    up_ref,
+    chances_ref,
+    dq_ref,
+    dk_ref,
+    dv_ref,
+    sums_ref,
 ):
+    def late_gains():
+        scale = [both_heads(gain_q_ref) * SCALE, both_heads(gain_k_ref)]
+        return late_ref[...] / jnp.concatenate(scale + [jnp.ones((6, LANES), F32)], 0)
+
     of_query = jnp.zeros((1, LANES), F32)
     of_key = jnp.zeros((1, LANES), F32)
     slices = [pair_slice(pair) for pair in range(PAIRS)]
@@ -249,10 +265,10 @@
         dq_ref[:, at] = dq
         of_query += gain_part(dq, hat_q_ref[:, at])
         of_key += gain_part(dk, hat_k_ref[:, at])
-    add_gains(sums_ref, of_query, of_key)
-
-
-def space_back(queries, keys, normed, values, upstream, chances):
+    add_gains(sums_ref, of_query, of_key, late_gains)
+
+
+def space_back(late_sums, gain_query, gain_key, hats, normed, values, upstream, chances):
     inner = values.shape[1]
     tokens = pl.BlockSpec((CELLS, WIDE), lambda n: (0, n))
     wide = jax.ShapeDtypeStruct((CELLS, inner), F32)
@@ -260,6 +276,9 @@
         space_back_kernel,
         grid=(inner // WIDE,),
         in_specs=[
+            pl.BlockSpec((8, LANES), lambda n: (0, 0)),
+            pl.BlockSpec((1, HD), lambda n: (0, 0)),
+            pl.BlockSpec((1, HD), lambda n: (0, 0)),
             tokens,
             tokens,
             pl.BlockSpec((FRAMES, 2, CELLS_HERE, WIDE), lambda n: (0, 0, 0, n)),
@@ -277,7 +296,7 @@
         compiler_params=PARAMS,
         cost_estimate=cost(9),
         name="space_back",
-    )(queries, keys, normed, values, upstream, chances)
+    )(late_sums, gain_query, gain_key, *hats, normed, values, upstream, chances)
 
 
 def time_bias(frame_total):
@@ -495,24 +514,25 @@
     )(mixed, weight)
 
 
-TAIL = 16
+PIECES = 6
+TAIL = 8
 
 
 def weight_kernel(place_ref, order_ref, mixed_ref, cot_ref, out_ref, turned, product):
-    shares, rows, _ = out_ref.shape
-    own = (rows - TAIL) // 4
+    shares = out_ref.shape[0]
+    own = product.shape[0] // shares
 
     @pl.when(pl.program_id(0) == 0)
     def _():
         turned[...] = nt(order_ref[0], mixed_ref[...]).astype(BF)
 
     product[...] = nn(turned[...], cot_ref[...])
-    for quarter in range(4):
-
-        @pl.when(pl.program_id(0) == quarter)
+    for piece in range(PIECES):
+
+        @pl.when(pl.program_id(0) == piece)
         def _():
             for share in range(shares):
-                out_ref[share, quarter * own : (quarter + 1) * own] = product[
+                out_ref[share, piece * own : (piece + 1) * own] = product[
                     share * own : (share + 1) * own
                 ].astype(BF)
 
@@ -520,13 +540,13 @@
 def weight_parts(place, order, mixed, cotangents, shares):
     tokens, width = cotangents.shape
     _, features, wide = order.shape
-    block = width // 4
-    rows = 4 * (features // shares) + TAIL
+    block = width // PIECES
+    rows = -(-(PIECES * (features // shares) + TAIL) // 16) * 16
     return pl.pallas_call(
         weight_kernel,
         grid_spec=pltpu.PrefetchScalarGridSpec(
             num_scalar_prefetch=1,
-            grid=(4,),
+            grid=(PIECES,),
             in_specs=[
                 pl.BlockSpec((1, features, wide), lambda n, place: (place[1], 0, 0)),
                 pl.BlockSpec((tokens, wide), lambda n, place: (0, place[0])),
@@ -545,61 +565,64 @@
     )(place, order, mixed, cotangents)
 
 
-def tail_kernel(gain_ref, _, out_ref):
+def tail_kernel(*refs):
+    *gain_refs, parts_ref, out_ref = refs
+    total = gain_refs[0][...]
+    for gain_ref in gain_refs[1:]:
+        total = total + gain_ref[...]
     terms = []
     for row in range(2):
-        rest = gain_ref[row : row + 1]
+        rest = total[row : row + 1]
         for _ in range(3):
             terms.append(rest.astype(BF).astype(F32))
             rest = rest - terms[-1]
     block = out_ref.shape[2]
     rows = jnp.concatenate(terms + [jnp.zeros((TAIL - 6, LANES), F32)], 0)
-    rows = jnp.concatenate([rows, jnp.zeros((TAIL, block - LANES), F32)], 1).astype(BF)
+    rows = jnp.concatenate([rows, jnp.zeros((TAIL, block - LANES), F32)], 1)
     for share in range(out_ref.shape[0]):
-        out_ref[share] = rows
+        kept = parts_ref[share].astype(F32)[:TAIL]
+        out_ref[share] = jnp.concatenate([kept, rows], 0).astype(BF)
 
 
 def add_tail(gain_sums, parts):
     shares, rows, block = parts.shape
+    last = pl.BlockSpec((shares, 2 * TAIL, block), lambda n: (0, rows // (2 * TAIL) - 1, 0))
+    gain = pl.BlockSpec((8, LANES), lambda n: (0, 0))
     return pl.pallas_call(
         tail_kernel,
         grid=(1,),
-        in_specs=[
-            pl.BlockSpec(gain_sums.shape, lambda n: (0, 0)),
-            pl.BlockSpec(memory_space=pl.ANY),
-        ],
-        out_specs=pl.BlockSpec((shares, TAIL, block), lambda n: (0, rows // TAIL - 1, 0)),
+        in_specs=[gain] * len(gain_sums) + [last],
+        out_specs=last,
         out_shape=jax.ShapeDtypeStruct(parts.shape, BF),
-        input_output_aliases={1: 0},
+        input_output_aliases={len(gain_sums): 0},
         compiler_params=PARAMS,
         cost_estimate=cost(1.5),
         name="add_tail",
-    )(gain_sums, parts)
-
-
-def sum_kernel(parts_ref, out_ref, gain_ref):
+    )(*gain_sums, parts)
+
+
+def sum_kernel(parts_ref, out_ref, gain_q_ref, gain_k_ref):
     shares, rows, block = parts_ref.shape
-    own = (rows - TAIL) // 4
+    own = out_ref.shape[0]
     total = parts_ref[0].astype(F32)
     for share in range(1, shares):
         total = total + parts_ref[share].astype(F32)
-    for quarter in range(4):
-        out_ref[:, quarter * block : (quarter + 1) * block] = total[
-            quarter * own : (quarter + 1) * own
-        ]
-    gain_ref[...] = total[rows - TAIL : rows - TAIL + 8, :LANES]
-
-
-def sum_parts(parts):
-    _, rows, block = parts.shape
+    for piece in range(PIECES):
+        out_ref[:, piece * block : (piece + 1) * block] = total[piece * own : (piece + 1) * own]
+    tail = total[rows - TAIL :, :LANES]
+    for number, gain_ref in enumerate((gain_q_ref, gain_k_ref)):
+        gain = jnp.sum(tail[3 * number : 3 * number + 3], 0, keepdims=True)
+        gain_ref[...] = gain[:, :HD] + gain[:, HD:]
+
+
+def sum_parts(parts, own):
+    block = parts.shape[2]
+    gain = jax.ShapeDtypeStruct((1, HD), F32)
     return pl.pallas_call(
         sum_kernel,
         in_specs=[VMEM],
-        out_specs=[VMEM, VMEM],
-        out_shape=[
-            jax.ShapeDtypeStruct(((rows - TAIL) // 4, 4 * block), F32),
-            jax.ShapeDtypeStruct((8, LANES), F32),
-        ],
+        out_specs=[VMEM] * 3,
+        out_shape=[jax.ShapeDtypeStruct((own, PIECES * block), F32), gain, gain],
         compiler_params=PARAMS,
         cost_estimate=cost(2.2),
         name="sum_parts",
@@ -668,31 +691,28 @@
     block_out = project(mixed, out_weight)
     order = feature_order(inner, planes, cores, shares)
     parts = weight_parts(place, order, gathered, cotangents, shares)
-    dq, dk, grad_values, early_gains = space_back(
-        hats[0], hats[1], normed, value_rows, dspatial, chances
+    dq, dk, grad_values, gain_sums = space_back(
+        late_gains, *gains, hats[:2], normed, value_rows, dspatial, chances
     )
-    late_scale = jnp.stack([gain_query * SCALE, gain_key])
-    late_scale = jnp.pad(jnp.tile(late_scale, (1, 2)), ((0, 6), (0, 0)), constant_values=1.0)
-    gain_sums = early_gains + late_gains / late_scale
-    for axis, extent in (("core", cores), ("x", planes)):
-        flip = 1
-        while flip < extent:
-            pairs = [(i, i ^ flip) for i in range(extent)]
-            gain_sums = gain_sums + lax.ppermute(gain_sums, axis, pairs)
-            flip *= 2
+    for flip in range(1, cores):
+        pairs = [(i, (i + flip) % cores) for i in range(cores)]
+        gain_sums = gain_sums + lax.ppermute(gain_sums, "core", pairs)
+    gain_sums = [gain_sums] + [
+        lax.ppermute(gain_sums, "x", [(i, (i + step) % planes) for i in range(planes)])
+        for step in range(1, planes)
+    ]
     grad_queries, grad_keys = norm_back(hats, *gains, dq, dk, late)
     parts = exchange(after(add_tail(gain_sums, parts), late), sums)
-    grad_weight, tail = sum_parts(parts)
-    gain_sums = jnp.stack([jnp.sum(tail[:3], 0), jnp.sum(tail[3:6], 0)])
-    gain_sums = gain_sums[:, :HD] + gain_sums[:, HD:]
+    own = order.shape[1] // shares
+    grad_weight, grad_gain_query, grad_gain_key = sum_parts(parts, own)
     return (
         block_out.reshape(cotangent.shape),
         grad_queries.reshape(queries.shape),
         grad_keys.reshape(queries.shape),
         grad_values.reshape(queries.shape),
         grad_weight,
-        gain_sums[0],
-        gain_sums[1],
+        grad_gain_query.reshape(HD),
+        grad_gain_key.reshape(HD),
     )
 
 

time: 187 us -> 184 us (0.984)
    ppermute x3 -> x4, waiting for transfers between devices: 4.58 us -> 1.04 us  [the longest x1 1.03 us: local(): gain_sums = gain_sums + lax.ppermute(gain_sums, 'core', pairs)]
    all_gather x1, waiting for transfers between devices: 0.01 us -> 2.91 us  [local(): gathered = lax.all_gather(after(mixed, first), group, axis=0, tiled=True)]
    ppermute x3 -> x4, starting transfers between devices: 4.78 us -> 6.11 us  [the longest x3 5.64 us: local(): lax.ppermute(gain_sums, 'x', [(i, (i + step) % planes) for i in range(pla...]
    unnamed x16 -> x18, local copies, waits for them, and re-layouts: 5.57 us -> 5.45 us
  transfers between devices with their start and end apart: 10 -> 11, of which waited for: 7 -> 6; matrix products, arithmetic and copies ran while one was open for 1% -> 1% of each run, Pallas kernels for 39% -> 40%
where the time goes in v2:
time: 184 us; the launch traced here: 183 us
  Pallas kernels  75.5 us (41%)
  waiting for transfers between devices  38.3 us (21%)
  starting transfers between devices  28.4 us (15%)
  blocking collectives  17.4 us (9%)
  between operations  16.1 us (9%)
  local copies, waits for them, and re-layouts  5.45 us (3%)
  other arithmetic  1.86 us (1%)
    all_to_all x5, waiting for transfers between devices, exchange(): return lax.all_to_all(tensor, axes, split_axis=0, concat_axis=0, tiled=True)  33.7 us
    all_to_all x5, starting transfers between devices, exchange(): return lax.all_to_all(tensor, axes, split_axis=0, concat_axis=0, tiled=True)  22.3 us
    all_to_all x1, blocking collectives, exchange(): return lax.all_to_all(tensor, axes, split_axis=0, concat_axis=0, tiled=True)  17.4 us
    pallas_call x1, Pallas kernels, weight_parts(): pl.pallas_call(weight_kernel, grid_spec=pltpu.PrefetchScalarGridSpec(num_...  10.6 us
    pallas_call x1, Pallas kernels, space_back(): pl.pallas_call(space_back_kernel, grid=(inner // WIDE,), in_specs=[pl.Blo...  9.2 us
    pallas_call x1, Pallas kernels, grad_mixed_of(): pl.pallas_call(grad_mixed_kernel, grid=(inner // WIDE,), in_specs=[pl.Blo...  8.65 us
    pallas_call x1, Pallas kernels, space_forward(): pl.pallas_call(space_kernel, grid=(inner // WIDE,), in_specs=[SMEM, pl.Bl...  7.02 us
    pallas_call x1, Pallas kernels, project(): pl.pallas_call(project_kernel, grid=(4,), in_specs=[pl.BlockSpec((CELLS,...  6.98 us
  transfers between devices with their start and end apart: 11, of which 6 were waited for; matrix products, arithmetic and copies ran while one was open for 1% of the time, Pallas kernels for 40%

profile of v2, /device:TPU:0, one launch (start us, length us, event | category | flops | bytes accessed | tf_op | source)
XLA Modules:
  0.0 183.1 jit_solution(16812142954167295541)
XLA Ops:
  7.2 0.0 all-gather.6.cloned.1.call-start
  7.2 0.7 all-gather.6.cloned.1.call-update
  7.9 5.0 %norm.1.qk_ref = bf16[8,2,32,1536]{3,2,1,0:T(8,128)(2,1)} custom-call(bf16[256,1536]{1,0:T(8,128)(2,1)} %bitcast.23, bf16[256,1536]{1,0:T(8,128)(2,1)} %bitcast.25, f32[1,64]{1,0:T(1,128)} %bitcast.30, f32[1,64]{1,0:T(1,128)} %bitcast.33), custom_call_target="tpu_custom_call" | custom-call | bytes 18450000 | tf_op jit(solution)/shard_map/norm/pallas_call | solution.py:131
  12.9 4.6 %all-to-all-start = ((bf16[8,2,32,1536]{3,2,1,0:T(8,128)(2,1)}), bf16[8,2,32,1536]{3,2,1,0:T(8,128)(2,1)S(1)}, u32[]{:S(2)}, u32[]{:S(2)}) async-start(bf16[8,2,32,1536]{3,2,1,0:T(8,128)(2,1)} %norm.1.qk_ref), calls=%async_computation | async-start | bytes 3145728 | tf_op jit(solution)/shard_map/all_to_all | solution.py:670
  19.4 8.6 %grad_mixed.1.gm_ref = bf16[256,1536]{1,0:T(8,128)(2,1)} custom-call(bf16[256,3072]{1,0:T(8,128)(2,1)} %bitcast.21, bf16[1536,3072]{1,0:T(8,128)(2,1)} %weight_ref.3), custom_call_target="tpu_custom_call" | custom-call | bytes 32103000 | tf_op jit(solution)/shard_map/grad_mixed/pallas_call | solution.py:480
  28.0 0.6 pad_add_fusion.counts_ref
  28.6 7.0 %space_forward.1 = (bf16[8,2,32,1536]{3,2,1,0:T(8,128)(2,1)}, f32[12,512,256]{2,1,0:T(8,128)}) custom-call(s32[4]{0:T(128)} %pad_add_fusion.counts_ref, bf16[8,2,32,1536]{3,2,1,0:T(8,128)(2,1)} %norm.1.qk_ref, bf16[256,1536]{1,0:T(8,128)(2,1)} %bitcast.27, bf16[256,1536]{1,0:T(8,128)(2,1)} %grad_mixed.1.gm_ref), custom_call_target="tpu_custom_call" | custom-call | bytes 25830000 | tf_op jit(solution)/shard_map/space_forward/pallas_call | solution.py:195
  35.6 3.4 %all-to-all-done.qk_ref = bf16[8,2,32,1536]{3,2,1,0:T(8,128)(2,1)S(1)} async-done(((bf16[8,2,32,1536]{3,2,1,0:T(8,128)(2,1)}), bf16[8,2,32,1536]{3,2,1,0:T(8,128)(2,1)S(1)}, u32[]{:S(2)}, u32[]{:S(2)}) %all-to-all-start) | async-done | bytes 1572896 | tf_op jit(solution)/shard_map/all_to_all | solution.py:670
  39.0 1.2 copy-done
  40.2 3.6 %all-to-all-start.1 = ((bf16[8,2,32,1536]{3,2,1,0:T(8,128)(2,1)}), bf16[8,2,32,1536]{3,2,1,0:T(8,128)(2,1)S(1)}, u32[]{:S(2)}, u32[]{:S(2)}) async-start(bf16[8,2,32,1536]{3,2,1,0:T(8,128)(2,1)} %get-tuple-element.38), calls=%async_computation.1 | async-start | bytes 3145728 | tf_op jit(solution)/shard_map/all_to_all | solution.py:670
  43.8 5.7 %hats.1 = (f32[256,1536]{1,0:T(8,128)}, f32[256,1536]{1,0:T(8,128)}, f32[256,1536]{1,0:T(8,128)}, f32[256,1536]{1,0:T(8,128)}) custom-call(bf16[256,1536]{1,0:T(8,128)(2,1)} %bitcast.24, bf16[256,1536]{1,0:T(8,128)(2,1)} %bitcast.26), custom_call_target="tpu_custom_call" | custom-call | bytes 20664000 | tf_op jit(solution)/shard_map/hats/pallas_call | solution.py:156
  49.4 15.8 %all-to-all-done.1.sg_ref = bf16[8,2,32,1536]{3,2,1,0:T(8,128)(2,1)S(1)} async-done(((bf16[8,2,32,1536]{3,2,1,0:T(8,128)(2,1)}), bf16[8,2,32,1536]{3,2,1,0:T(8,128)(2,1)S(1)}, u32[]{:S(2)}, u32[]{:S(2)}) %all-to-all-start.1) | async-done | bytes 1572896 | tf_op jit(solution)/shard_map/all_to_all | solution.py:670
  65.3 1.1 copy-done.1
  66.4 5.1 %time_forward.1 = bf16[8,32,1536]{2,1,0:T(8,128)(2,1)} custom-call(s32[4]{0:T(128)} %pad_add_fusion.counts_ref, bf16[8,2,32,1536]{3,2,1,0:T(8,128)(2,1)} %copy-done, bf16[8,2,32,1536]{3,2,1,0:T(8,128)(2,1)} %copy-done.1), custom_call_target="tpu_custom_call" | custom-call | bytes 18450000 | tf_op jit(solution)/shard_map/time_forward/pallas_call | solution.py:390
  71.5 3.5 %all-to-all-start.2 = ((bf16[8,32,1536]{2,1,0:T(8,128)(2,1)}), bf16[8,32,1536]{2,1,0:T(8,128)(2,1)S(1)}, u32[]{:S(2)}, u32[]{:S(2)}) async-start(bf16[8,32,1536]{2,1,0:T(8,128)(2,1)} %time_forward.1), calls=%async_computation.2 | async-start | bytes 1572864 | tf_op jit(solution)/shard_map/all_to_all | solution.py:670
  75.0 0.0 all-gather.4.cloned.1.call-start
  75.1 6.5 %time_back.1 = (bf16[8,2,32,1536]{3,2,1,0:T(8,128)(2,1)}, bf16[8,32,1536]{2,1,0:T(8,128)(2,1)}, f32[8,128]{1,0:T(8,128)}) custom-call(s32[4]{0:T(128)} %pad_add_fusion.counts_ref, bf16[8,2,32,1536]{3,2,1,0:T(8,128)(2,1)} %copy-done, bf16[8,2,32,1536]{3,2,1,0:T(8,128)(2,1)} %copy-done.1), custom_call_target="tpu_custom_call" | custom-call | bytes 23985000 | tf_op jit(solution)/shard_map/time_back/pallas_call | solution.py:405
  81.6 6.5 %all-to-all-done.2 = bf16[8,32,1536]{2,1,0:T(8,128)(2,1)S(1)} async-done(((bf16[8,32,1536]{2,1,0:T(8,128)(2,1)}), bf16[8,32,1536]{2,1,0:T(8,128)(2,1)S(1)}, u32[]{:S(2)}, u32[]{:S(2)}) %all-to-all-start.2) | async-done | bytes 786464 | tf_op jit(solution)/shard_map/all_to_all | solution.py:670
  88.1 0.9 copy-done.2
  89.0 0.0 all-gather.4.cloned.1.call-update
  89.0 17.4 %all_to_all.30 = bf16[8,32,1536]{2,1,0:T(8,128)(2,1)} all-to-all(bf16[8,32,1536]{2,1,0:T(8,128)(2,1)} %get-tuple-element.52), channel_id=1, replica_groups=mesh['x'=4,'z'=4,'y'=4,'core'=2] {'y','core'}, dimensions={0} | all-to-all | bytes 1572864 | tf_op jit(solution)/shard_map/all_to_all | solution.py:670
  106.5 3.6 %all-to-all-start.4 = ((bf16[8,2,32,1536]{3,2,1,0:T(8,128)(2,1)}), bf16[8,2,32,1536]{3,2,1,0:T(8,128)(2,1)S(1)}, u32[]{:S(2)}, u32[]{:S(2)}) async-start(bf16[8,2,32,1536]{3,2,1,0:T(8,128)(2,1)} %get-tuple-element.57), calls=%async_computation.4 | async-start | bytes 3145728 | tf_op jit(solution)/shard_map/all_to_all | solution.py:670
  110.1 9.2 %space_back.1 = (f32[256,1536]{1,0:T(8,128)}, f32[256,1536]{1,0:T(8,128)}, bf16[256,1536]{1,0:T(8,128)(2,1)}, f32[8,128]{1,0:T(8,128)}) custom-call(f32[8,128]{1,0:T(8,128)} %get-tuple-element.50.late_ref, f32[1,64]{1,0:T(1,128)} %bitcast.31, f32[1,64]{1,0:T(1,128)} %bitcast.34, f32[256,1536]{1,0:T(8,128)} %get-tuple-element.46.hat_q_ref, ...), custom_call_target="tpu_custom_call" | custom-call | bytes 33210000 | tf_op jit(solution)/shard_map/space_back/pallas_call | solution.py:275
  119.3 0.5 collective-permute-start
  119.8 1.0 collective-permute-done
  120.8 0.7 add.7.refs_0_
  121.5 1.4 collective-permute-start.1
  122.9 2.8 %collective-permute-start.2 = (f32[8,128]{1,0:T(8,128)S(1)}, f32[8,128]{1,0:T(8,128)S(1)}, u32[]{:S(2)}, u32[]{:S(2)}) collective-permute-start(f32[8,128]{1,0:T(8,128)S(1)} %add.7.refs_0_), channel_id=1, source_target_pairs={{0,64},{32,96},{64,0},{96,32},{1,65},{33,97},{65,1},{97,33},{2,66}... | collective-permute-start | bytes 12296 | tf_op jit(solution)/shard_map/ppermute | solution.py:701
  125.7 1.4 collective-permute-start.3
  127.1 0.6 pad_add_fusion.1.place_ref
  127.7 2.9 %all-gather.4.cloned.1.call-done.mixed_ref = bf16[2048,1536]{1,0:T(8,128)(2,1)} async-done(((bf16[256,1536]{1,0:T(8,128)(2,1)}), bf16[2048,1536]{1,0:T(8,128)(2,1)}) %all-gather.4.cloned.1.call-update) | async-done | bytes 6291472 | tf_op jit(solution)/shard_map/all_gather | solution.py:688
  130.6 10.6 %weight_parts.1.refs_4_ = bf16[16,80,512]{2,1,0:T(8,128)(2,1)} custom-call(s32[2]{0:T(128)} %pad_add_fusion.1.place_ref, bf16[2,192,384]{2,1,0:T(8,128)(2,1)} %constant.16.clone.order_ref, bf16[2048,1536]{1,0:T(8,128)(2,1)} %all-gather.4.cloned.1.call-done.mixed_ref, bf16[2048,3072]{1,0:T(8,128)(2,1)} %bitcast.18), custom_call_target="tpu_custom_call" | custom-call | bytes 35055000 | tf_op jit(solution)/shard_map/weight_parts/pallas_call | solution.py:545
  141.3 0.0 copy-done.5
  141.3 0.0 collective-permute-done.1.refs_1_
  141.3 0.0 collective-permute-done.2.refs_2_
  141.3 0.0 copy-start.7
  141.3 0.0 collective-permute-done.3.refs_3_
  141.3 0.6 copy-done.6
  141.9 0.0 copy-done.7
  141.9 0.6 copy-done.8
  142.5 1.8 add_tail.1
  144.2 0.0 all-to-all-done.4.late_ref
  144.2 6.9 %all-to-all-start.5 = ((bf16[16,80,512]{2,1,0:T(8,128)(2,1)}), bf16[16,80,512]{2,1,0:T(8,128)(2,1)S(1)}, u32[]{:S(2)}, u32[]{:S(2)}) async-start(bf16[16,80,512]{2,1,0:T(8,128)(2,1)} %add_tail.1), calls=%async_computation.5 | async-start | bytes 2621440 | tf_op jit(solution)/shard_map/all_to_all | solution.py:670
  151.2 7.0 %project.1 = bf16[256,3072]{1,0:T(8,128)(2,1)} custom-call(bf16[256,1536]{1,0:T(8,128)(2,1)} %bitcast.20, bf16[1536,3072]{1,0:T(8,128)(2,1)} %weight_ref.3), custom_call_target="tpu_custom_call" | custom-call | bytes 25830000 | tf_op jit(solution)/shard_map/project/pallas_call | solution.py:502
  158.2 6.9 %norm_back.1 = (bf16[256,1536]{1,0:T(8,128)(2,1)}, bf16[256,1536]{1,0:T(8,128)(2,1)}) custom-call(f32[256,1536]{1,0:T(8,128)} %get-tuple-element.46.hat_q_ref, f32[256,1536]{1,0:T(8,128)} %get-tuple-element.47.hat_k_ref, f32[256,1536]{1,0:T(8,128)} %get-tuple-element.48.inverse_q_ref, f32[256,1536]{1,0:T(8,128)} %get-tuple-element.49.inverse_k_ref, ...), custom_call_target="tpu_custom_call" | custom-call | bytes 25830000 | tf_op jit(solution)/shard_map/norm_back/pallas_call | solution.py:452
  165.1 7.9 %all-to-all-done.5.parts_ref = bf16[16,80,512]{2,1,0:T(8,128)(2,1)S(1)} async-done(((bf16[16,80,512]{2,1,0:T(8,128)(2,1)}), bf16[16,80,512]{2,1,0:T(8,128)(2,1)S(1)}, u32[]{:S(2)}, u32[]{:S(2)}) %all-to-all-start.5) | async-done | bytes 1310752 | tf_op jit(solution)/shard_map/all_to_all | solution.py:670
  173.0 1.1 copy-done.4
  174.1 2.2 %sum_parts.1 = (f32[12,3072]{1,0:T(8,128)}, f32[1,64]{1,0:T(1,128)}, f32[1,64]{1,0:T(1,128)}) custom-call(bf16[16,80,512]{2,1,0:T(8,128)(2,1)} %copy-done.4), custom_call_target="tpu_custom_call" | custom-call | bytes 8118000 | tf_op jit(solution)/shard_map/sum_parts/pallas_call | solution.py:621
  (10 shorter events, 0.0 us)
Async XLA Ops:
  7.2 81.0 %all-gather.6.cloned.1.call-start = ((), (), s32[]{:S(2)}) async-start(), calls=%async_computation.7 | async-start | bytes 14155776 | tf_op jit(solution)/shard_map/all_gather | solution.py:675
  12.9 26.1 %all-to-all-start = ((bf16[8,2,32,1536]{3,2,1,0:T(8,128)(2,1)}), bf16[8,2,32,1536]{3,2,1,0:T(8,128)(2,1)S(1)}, u32[]{:S(2)}, u32[]{:S(2)}) async-start(bf16[8,2,32,1536]{3,2,1,0:T(8,128)(2,1)} %norm.1.qk_ref), calls=%async_computation | async-start | bytes 3145728 | tf_op jit(solution)/shard_map/all_to_all | solution.py:670
  39.0 1.2 copy-start
  40.2 25.1 %all-to-all-start.1 = ((bf16[8,2,32,1536]{3,2,1,0:T(8,128)(2,1)}), bf16[8,2,32,1536]{3,2,1,0:T(8,128)(2,1)S(1)}, u32[]{:S(2)}, u32[]{:S(2)}) async-start(bf16[8,2,32,1536]{3,2,1,0:T(8,128)(2,1)} %get-tuple-element.38), calls=%async_computation.1 | async-start | bytes 3145728 | tf_op jit(solution)/shard_map/all_to_all | solution.py:670
  65.3 1.1 copy-start.1
  71.5 16.6 %all-to-all-start.2 = ((bf16[8,32,1536]{2,1,0:T(8,128)(2,1)}), bf16[8,32,1536]{2,1,0:T(8,128)(2,1)S(1)}, u32[]{:S(2)}, u32[]{:S(2)}) async-start(bf16[8,32,1536]{2,1,0:T(8,128)(2,1)} %time_forward.1), calls=%async_computation.2 | async-start | bytes 1572864 | tf_op jit(solution)/shard_map/all_to_all | solution.py:670
  75.0 55.6 %all-gather.4.cloned.1.call-start = ((), (), s32[]{:S(2)}) async-start(), calls=%async_computation.6 | async-start | bytes 7077888 | tf_op jit(solution)/shard_map/all_gather | solution.py:688
  88.1 0.9 copy-start.2
  106.5 37.8 %all-to-all-start.4 = ((bf16[8,2,32,1536]{3,2,1,0:T(8,128)(2,1)}), bf16[8,2,32,1536]{3,2,1,0:T(8,128)(2,1)S(1)}, u32[]{:S(2)}, u32[]{:S(2)}) async-start(bf16[8,2,32,1536]{3,2,1,0:T(8,128)(2,1)} %get-tuple-element.57), calls=%async_computation.4 | async-start | bytes 3145728 | tf_op jit(solution)/shard_map/all_to_all | solution.py:670
  119.3 1.5 collective-permute-start
  121.5 19.8 %copy-start.5 = (f32[8,128]{1,0:T(8,128)}, f32[8,128]{1,0:T(8,128)S(1)}, u32[]{:S(2)}) copy-start(f32[8,128]{1,0:T(8,128)S(1)} %add.7.refs_0_) | copy-start | bytes 12292
  121.5 19.8 %collective-permute-start.1 = (f32[8,128]{1,0:T(8,128)S(1)}, f32[8,128]{1,0:T(8,128)S(1)}, u32[]{:S(2)}, u32[]{:S(2)}) collective-permute-start(f32[8,128]{1,0:T(8,128)S(1)} %add.7.refs_0_), channel_id=1, source_target_pairs={{0,32},{32,64},{64,96},{96,0},{1,33},{33,65},{65,97},{97,1},{2,34}... | collective-permute-start | bytes 12296 | tf_op jit(solution)/shard_map/ppermute | solution.py:701
  122.9 18.3 %collective-permute-start.2 = (f32[8,128]{1,0:T(8,128)S(1)}, f32[8,128]{1,0:T(8,128)S(1)}, u32[]{:S(2)}, u32[]{:S(2)}) collective-permute-start(f32[8,128]{1,0:T(8,128)S(1)} %add.7.refs_0_), channel_id=1, source_target_pairs={{0,64},{32,96},{64,0},{96,32},{1,65},{33,97},{65,1},{97,33},{2,66}... | collective-permute-start | bytes 12296 | tf_op jit(solution)/shard_map/ppermute | solution.py:701
  125.7 15.6 %collective-permute-start.3 = (f32[8,128]{1,0:T(8,128)S(1)}, f32[8,128]{1,0:T(8,128)S(1)}, u32[]{:S(2)}, u32[]{:S(2)}) collective-permute-start(f32[8,128]{1,0:T(8,128)S(1)} %add.7.refs_0_), channel_id=1, source_target_pairs={{0,96},{32,0},{64,32},{96,64},{1,97},{33,1},{65,33},{97,65},{2,98}... | collective-permute-start | bytes 12296 | tf_op jit(solution)/shard_map/ppermute | solution.py:701
  141.3 0.6 copy-start.6
  141.3 0.6 copy-start.7
  141.9 0.6 copy-start.8
  144.2 13.9 %copy-start.3 = (bf16[8,2,32,1536]{3,2,1,0:T(8,128)(2,1)}, bf16[8,2,32,1536]{3,2,1,0:T(8,128)(2,1)S(1)}, u32[]{:S(2)}) copy-start(bf16[8,2,32,1536]{3,2,1,0:T(8,128)(2,1)S(1)} %all-to-all-done.4.late_ref) | copy-start | bytes 4718596
  144.2 28.8 %all-to-all-start.5 = ((bf16[16,80,512]{2,1,0:T(8,128)(2,1)}), bf16[16,80,512]{2,1,0:T(8,128)(2,1)S(1)}, u32[]{:S(2)}, u32[]{:S(2)}) async-start(bf16[16,80,512]{2,1,0:T(8,128)(2,1)} %add_tail.1), calls=%async_computation.5 | async-start | bytes 2621440 | tf_op jit(solution)/shard_map/all_to_all | solution.py:670
  173.0 1.1 copy-start.4
Sparse Core Ops, SparseCore 0:
  9.7 69.7 all-gather.5
  89.1 41.4 all-gather.3

commit v3 on v2

--- a/solution.py
+++ b/solution.py
@@ -20,7 +20,7 @@
 BLOCK = 16
 NEG = -1e30
 SCALE = HD**-0.5
-PARAMS = pltpu.CompilerParams(vmem_limit_bytes=60 * 1024 * 1024)
+PARAMS = pltpu.CompilerParams(vmem_limit_bytes=24 * 1024 * 1024)
 
 
 def cost(microseconds):
@@ -515,58 +515,11 @@
 
 
 PIECES = 6
+STEPS = 3
 TAIL = 8
 
 
-def weight_kernel(place_ref, order_ref, mixed_ref, cot_ref, out_ref, turned, product):
-    shares = out_ref.shape[0]
-    own = product.shape[0] // shares
-
-    @pl.when(pl.program_id(0) == 0)
-    def _():
-        turned[...] = nt(order_ref[0], mixed_ref[...]).astype(BF)
-
-    product[...] = nn(turned[...], cot_ref[...])
-    for piece in range(PIECES):
-
-        @pl.when(pl.program_id(0) == piece)
-        def _():
-            for share in range(shares):
-                out_ref[share, piece * own : (piece + 1) * own] = product[
-                    share * own : (share + 1) * own
-                ].astype(BF)
-
-
-def weight_parts(place, order, mixed, cotangents, shares):
-    tokens, width = cotangents.shape
-    _, features, wide = order.shape
-    block = width // PIECES
-    rows = -(-(PIECES * (features // shares) + TAIL) // 16) * 16
-    return pl.pallas_call(
-        weight_kernel,
-        grid_spec=pltpu.PrefetchScalarGridSpec(
-            num_scalar_prefetch=1,
-            grid=(PIECES,),
-            in_specs=[
-                pl.BlockSpec((1, features, wide), lambda n, place: (place[1], 0, 0)),
-                pl.BlockSpec((tokens, wide), lambda n, place: (0, place[0])),
-                pl.BlockSpec((tokens, block), lambda n, place: (0, n)),
-            ],
-            out_specs=pl.BlockSpec((shares, rows, block), lambda n, place: (0, 0, 0)),
-            scratch_shapes=[
-                pltpu.VMEM((features, tokens), BF),
-                pltpu.VMEM((features, block), F32),
-            ],
-        ),
-        out_shape=jax.ShapeDtypeStruct((shares, rows, block), BF),
-        compiler_params=PARAMS,
-        cost_estimate=cost(9.5),
-        name="weight_parts",
-    )(place, order, mixed, cotangents)
-
-
-def tail_kernel(*refs):
-    *gain_refs, parts_ref, out_ref = refs
+def gain_rows(gain_refs, block):
     total = gain_refs[0][...]
     for gain_ref in gain_refs[1:]:
         total = total + gain_ref[...]
@@ -576,29 +529,64 @@
         for _ in range(3):
             terms.append(rest.astype(BF).astype(F32))
             rest = rest - terms[-1]
-    block = out_ref.shape[2]
     rows = jnp.concatenate(terms + [jnp.zeros((TAIL - 6, LANES), F32)], 0)
-    rows = jnp.concatenate([rows, jnp.zeros((TAIL, block - LANES), F32)], 1)
-    for share in range(out_ref.shape[0]):
-        kept = parts_ref[share].astype(F32)[:TAIL]
-        out_ref[share] = jnp.concatenate([kept, rows], 0).astype(BF)
-
-
-def add_tail(gain_sums, parts):
-    shares, rows, block = parts.shape
-    last = pl.BlockSpec((shares, 2 * TAIL, block), lambda n: (0, rows // (2 * TAIL) - 1, 0))
-    gain = pl.BlockSpec((8, LANES), lambda n: (0, 0))
-    return pl.pallas_call(
-        tail_kernel,
-        grid=(1,),
-        in_specs=[gain] * len(gain_sums) + [last],
-        out_specs=last,
-        out_shape=jax.ShapeDtypeStruct(parts.shape, BF),
-        input_output_aliases={len(gain_sums): 0},
-        compiler_params=PARAMS,
-        cost_estimate=cost(1.5),
-        name="add_tail",
-    )(*gain_sums, parts)
+    return jnp.concatenate([rows, jnp.zeros((TAIL, block - LANES), F32)], 1).astype(BF)
+
+
+def weight_kernel(place_ref, order_ref, mixed_ref, cot_ref, *refs):
+    *gain_refs, out_ref, turned, product = refs
+    shares, rows, block = out_ref.shape
+    own = product.shape[0] // shares
+
+    @pl.when(pl.program_id(0) == 0)
+    def _():
+        turned[...] = nt(order_ref[0], mixed_ref[...]).astype(BF)
+        tail = gain_rows(gain_refs, block)
+        for share in range(shares):
+            out_ref[share, rows - TAIL :] = tail
+
+    product[...] = nn(turned[...], cot_ref[...])
+    for step in range(STEPS):
+
+        @pl.when(pl.program_id(0) == step)
+        def _():
+            for share in range(shares):
+                for half in range(PIECES // STEPS):
+                    top = (step * (PIECES // STEPS) + half) * own
+                    out_ref[share, top : top + own] = product[
+                        share * own : (share + 1) * own, half * block : (half + 1) * block
+                    ].astype(BF)
+
+
+def weight_parts(place, order, mixed, cotangents, gain_sums, shares):
+    tokens, width = cotangents.shape
+    _, features, wide = order.shape
+    block = width // PIECES
+    columns = width // STEPS
+    rows = -(-(PIECES * (features // shares) + TAIL) // 16) * 16
+    gain = pl.BlockSpec((8, LANES), lambda n, place: (0, 0))
+    return pl.pallas_call(
+        weight_kernel,
+        grid_spec=pltpu.PrefetchScalarGridSpec(
+            num_scalar_prefetch=1,
+            grid=(STEPS,),
+            in_specs=[
+                pl.BlockSpec((1, features, wide), lambda n, place: (place[1], 0, 0)),
+                pl.BlockSpec((tokens, wide), lambda n, place: (0, place[0])),
+                pl.BlockSpec((tokens, columns), lambda n, place: (0, n)),
+            ]
+            + [gain] * len(gain_sums),
+            out_specs=pl.BlockSpec((shares, rows, block), lambda n, place: (0, 0, 0)),
+            scratch_shapes=[
+                pltpu.VMEM((features, tokens), BF),
+                pltpu.VMEM((features, columns), F32),
+            ],
+        ),
+        out_shape=jax.ShapeDtypeStruct((shares, rows, block), BF),
+        compiler_params=PARAMS,
+        cost_estimate=cost(9.5),
+        name="weight_parts",
+    )(place, order, mixed, cotangents, *gain_sums)
 
 
 def sum_kernel(parts_ref, out_ref, gain_q_ref, gain_k_ref):
@@ -689,8 +677,6 @@
     dspatial = exchange(after(dspatial_cells, mixed), seq).reshape(CELLS, inner)
     late = exchange(after(late_cells, dspatial), seq)
     block_out = project(mixed, out_weight)
-    order = feature_order(inner, planes, cores, shares)
-    parts = weight_parts(place, order, gathered, cotangents, shares)
     dq, dk, grad_values, gain_sums = space_back(
         late_gains, *gains, hats[:2], normed, value_rows, dspatial, chances
     )
@@ -702,7 +688,9 @@
         for step in range(1, planes)
     ]
     grad_queries, grad_keys = norm_back(hats, *gains, dq, dk, late)
-    parts = exchange(after(add_tail(gain_sums, parts), late), sums)
+    order = feature_order(inner, planes, cores, shares)
+    parts = weight_parts(place, order, gathered, cotangents, gain_sums, shares)
+    parts = exchange(after(parts, late), sums)
     own = order.shape[1] // shares
     grad_weight, grad_gain_query, grad_gain_key = sum_parts(parts, own)
     return (

time: 184 us -> 183 us (level)
  local copies, waits for them, and re-layouts: 5.45 us -> 38.2 us
  Pallas kernels: 75.5 us -> 50.4 us
  waiting for transfers between devices: 38.3 us -> 27.9 us
  starting transfers between devices: 28.4 us -> 31.3 us
    unnamed x18 -> x68, local copies, waits for them, and re-layouts: 5.45 us -> 38.2 us
    all_to_all x5, waiting for transfers between devices: 33.7 us -> 24.2 us  [exchange(): return lax.all_to_all(tensor, axes, split_axis=0, concat_axis=0, tiled=True)]
    pallas_call x1, Pallas kernels: 10.6 us -> 5.49 us  [weight_parts(): pl.pallas_call(weight_kernel, grid_spec=pltpu.PrefetchScalarGridSpec(num_...]
    pallas_call x1, Pallas kernels: 8.65 us -> 4.1 us  [grad_mixed_of(): pl.pallas_call(grad_mixed_kernel, grid=(inner // WIDE,), in_specs=[pl.Blo...]
    all_to_all x5, starting transfers between devices: 22.3 us -> 25.2 us  [exchange(): return lax.all_to_all(tensor, axes, split_axis=0, concat_axis=0, tiled=True)]
    all_gather x1, waiting for transfers between devices: 2.91 us -> 0.01 us  [local(): gathered = lax.all_gather(after(mixed, first), group, axis=0, tiled=True)]
    pallas_call x1, Pallas kernels: 9.2 us -> 6.86 us  [space_back(): pl.pallas_call(space_back_kernel, grid=(inner // WIDE,), in_specs=[pl.Blo...]
    pallas_call x1, Pallas kernels: 5.67 us -> 3.38 us  [hats_of(): pl.pallas_call(hats_kernel, grid=(inner // NORM_WIDE,), in_specs=[tokens,...]
  transfers between devices with their start and end apart: 11 -> 11, of which waited for: 6 -> 7; matrix products, arithmetic and copies ran while one was open for 1% -> 0% of each run, Pallas kernels for 40% -> 27%
where the time goes in v3:
time: 183 us; the launch traced here: 182 us
  Pallas kernels  50.4 us (28%)
  local copies, waits for them, and re-layouts  38.2 us (21%)
  starting transfers between devices  31.3 us (17%)
  waiting for transfers between devices  27.9 us (15%)
  blocking collectives  17.4 us (10%)
  between operations  16.2 us (9%)
    unnamed x68, local copies, waits for them, and re-layouts  38.2 us
    all_to_all x5, starting transfers between devices, exchange(): return lax.all_to_all(tensor, axes, split_axis=0, concat_axis=0, tiled=True)  25.2 us
    all_to_all x5, waiting for transfers between devices, exchange(): return lax.all_to_all(tensor, axes, split_axis=0, concat_axis=0, tiled=True)  24.2 us
    all_to_all x1, blocking collectives, exchange(): return lax.all_to_all(tensor, axes, split_axis=0, concat_axis=0, tiled=True)  17.4 us
    pallas_call x1, Pallas kernels, space_back(): pl.pallas_call(space_back_kernel, grid=(inner // WIDE,), in_specs=[pl.Blo...  6.86 us
    pallas_call x1, Pallas kernels, project(): pl.pallas_call(project_kernel, grid=(4,), in_specs=[pl.BlockSpec((CELLS,...  5.68 us
    ppermute x3, starting transfers between devices, local(): lax.ppermute(gain_sums, 'x', [(i, (i + step) % planes) for i in range(pla...  5.62 us
    pallas_call x1, Pallas kernels, weight_parts(): pl.pallas_call(weight_kernel, grid_spec=pltpu.PrefetchScalarGridSpec(num_...  5.49 us
  transfers between devices with their start and end apart: 11, of which 7 were waited for; matrix products, arithmetic and copies ran while one was open for 0% of the time, Pallas kernels for 27%

profile of v3, /device:TPU:0, one launch (start us, length us, event | category | flops | bytes accessed | tf_op | source)
XLA Modules:
  0.0 181.7 jit_solution(11552377662849800060)
XLA Ops:
  8.5 3.8 %norm.1.qk_ref = bf16[8,2,32,1536]{3,2,1,0:T(8,128)(2,1)} custom-call(bf16[256,1536]{1,0:T(8,128)(2,1)S(1)} %bitcast.21, bf16[256,1536]{1,0:T(8,128)(2,1)S(1)} %bitcast.23, f32[1,64]{1,0:T(1,128)S(1)} %bitcast.27, f32[1,64]{1,0:T(1,128)S(1)} %bitcast.30), custom_call_target="tpu_custom_call" | custom-call | bytes 18450000 | tf_op jit(solution)/shard_map/norm/pallas_call | solution.py:131
  12.3 4.7 %all-to-all-start = ((bf16[8,2,32,1536]{3,2,1,0:T(8,128)(2,1)}), bf16[8,2,32,1536]{3,2,1,0:T(8,128)(2,1)S(1)}, u32[]{:S(2)}, u32[]{:S(2)}) async-start(bf16[8,2,32,1536]{3,2,1,0:T(8,128)(2,1)} %norm.1.qk_ref), calls=%async_computation | async-start | bytes 3145728 | tf_op jit(solution)/shard_map/all_to_all | solution.py:658
  19.0 4.4 %copy-done = bf16[1536,3072]{1,0:T(8,128)(2,1)S(1)} copy-done((bf16[1536,3072]{1,0:T(8,128)(2,1)S(1)}, bf16[1536,3072]{1,0:T(8,128)(2,1)}, u32[]{:S(2)}) %copy-start) | copy-done | bytes 9437208
  23.4 4.1 %grad_mixed.1.gm_ref = bf16[256,1536]{1,0:T(8,128)(2,1)S(1)} custom-call(bf16[256,3072]{1,0:T(8,128)(2,1)S(1)} %bitcast.19, bf16[1536,3072]{1,0:T(8,128)(2,1)S(1)} %copy-done), custom_call_target="tpu_custom_call" | custom-call | bytes 32103000 | tf_op jit(solution)/shard_map/grad_mixed/pallas_call | solution.py:480
  27.6 5.2 %space_forward.1 = (bf16[8,2,32,1536]{3,2,1,0:T(8,128)(2,1)S(1)}, f32[12,512,256]{2,1,0:T(8,128)S(1)}) custom-call(s32[4]{0:T(128)S(1)} %pad_add_fusion.counts_ref, bf16[8,2,32,1536]{3,2,1,0:T(8,128)(2,1)} %norm.1.qk_ref, bf16[256,1536]{1,0:T(8,128)(2,1)S(1)} %bitcast.25, bf16[256,1536]{1,0:T(8,128)(2,1)S(1)} %grad_mixed.1.gm_ref), custom_call_target="tpu_custom_call" | custom-call | bytes 25830000 | tf_op jit(solution)/shard_map/space_forward/pallas_call | solution.py:195
  32.8 2.6 %copy-done.3 = f32[12,512,256]{2,1,0:T(8,128)} copy-done((f32[12,512,256]{2,1,0:T(8,128)}, f32[12,512,256]{2,1,0:T(8,128)S(1)}, u32[]{:S(2)}) %copy-start.3) | copy-done | bytes 6291480
  35.4 1.2 copy-done.21
  36.6 2.0 %all-to-all-done.qk_ref = bf16[8,2,32,1536]{3,2,1,0:T(8,128)(2,1)S(1)} async-done(((bf16[8,2,32,1536]{3,2,1,0:T(8,128)(2,1)}), bf16[8,2,32,1536]{3,2,1,0:T(8,128)(2,1)S(1)}, u32[]{:S(2)}, u32[]{:S(2)}) %all-to-all-start) | async-done | bytes 1572896 | tf_op jit(solution)/shard_map/all_to_all | solution.py:658
  38.6 3.6 %all-to-all-start.1 = ((bf16[8,2,32,1536]{3,2,1,0:T(8,128)(2,1)}), bf16[8,2,32,1536]{3,2,1,0:T(8,128)(2,1)S(1)}, u32[]{:S(2)}, u32[]{:S(2)}) async-start(bf16[8,2,32,1536]{3,2,1,0:T(8,128)(2,1)} %copy-done.21), calls=%async_computation.1 | async-start | bytes 3145728 | tf_op jit(solution)/shard_map/all_to_all | solution.py:658
  42.2 1.1 copy-done.14
  43.4 1.1 copy-done.16
  44.5 3.4 %hats.1 = (f32[256,1536]{1,0:T(8,128)S(1)}, f32[256,1536]{1,0:T(8,128)S(1)}, f32[256,1536]{1,0:T(8,128)S(1)}, f32[256,1536]{1,0:T(8,128)S(1)}) custom-call(bf16[256,1536]{1,0:T(8,128)(2,1)S(1)} %bitcast.22, bf16[256,1536]{1,0:T(8,128)(2,1)S(1)} %bitcast.24), custom_call_target="tpu_custom_call" | custom-call | bytes 20664000 | tf_op jit(solution)/shard_map/hats/pallas_call | solution.py:156
  47.9 1.2 copy-done.6
  49.1 1.2 copy-done.8
  50.2 1.1 copy-done.22
  51.4 1.1 copy-done.24
  52.5 11.2 %all-to-all-done.1.sg_ref = bf16[8,2,32,1536]{3,2,1,0:T(8,128)(2,1)S(1)} async-done(((bf16[8,2,32,1536]{3,2,1,0:T(8,128)(2,1)}), bf16[8,2,32,1536]{3,2,1,0:T(8,128)(2,1)S(1)}, u32[]{:S(2)}, u32[]{:S(2)}) %all-to-all-start.1) | async-done | bytes 1572896 | tf_op jit(solution)/shard_map/all_to_all | solution.py:658
  63.7 3.6 %time_forward.1 = bf16[8,32,1536]{2,1,0:T(8,128)(2,1)S(1)} custom-call(s32[4]{0:T(128)S(1)} %pad_add_fusion.counts_ref, bf16[8,2,32,1536]{3,2,1,0:T(8,128)(2,1)S(1)} %all-to-all-done.qk_ref, bf16[8,2,32,1536]{3,2,1,0:T(8,128)(2,1)S(1)} %all-to-all-done.1.sg_ref), custom_call_target="tpu_custom_call" | custom-call | bytes 18450000 | tf_op jit(solution)/shard_map/time_forward/pallas_call | solution.py:390
  67.3 0.9 copy-done.17
  68.2 4.2 %all-to-all-start.2 = ((bf16[8,32,1536]{2,1,0:T(8,128)(2,1)}), bf16[8,32,1536]{2,1,0:T(8,128)(2,1)}, u32[]{:S(2)}, u32[]{:S(2)}) async-start(bf16[8,32,1536]{2,1,0:T(8,128)(2,1)} %copy-done.17), calls=%async_computation.2 | async-start | bytes 1572864 | tf_op jit(solution)/shard_map/all_to_all | solution.py:658
  72.4 5.2 %time_back.1 = (bf16[8,2,32,1536]{3,2,1,0:T(8,128)(2,1)S(1)}, bf16[8,32,1536]{2,1,0:T(8,128)(2,1)S(1)}, f32[8,128]{1,0:T(8,128)S(1)}) custom-call(s32[4]{0:T(128)S(1)} %pad_add_fusion.counts_ref, bf16[8,2,32,1536]{3,2,1,0:T(8,128)(2,1)S(1)} %all-to-all-done.qk_ref, bf16[8,2,32,1536]{3,2,1,0:T(8,128)(2,1)S(1)} %all-to-all-done.1.sg_ref), custom_call_target="tpu_custom_call" | custom-call | bytes 23985000 | tf_op jit(solution)/shard_map/time_back/pallas_call | solution.py:405
  77.7 1.1 copy-done.20
  78.8 0.9 copy-done.30
  79.7 5.8 %all-to-all-done.2 = bf16[8,32,1536]{2,1,0:T(8,128)(2,1)} async-done(((bf16[8,32,1536]{2,1,0:T(8,128)(2,1)}), bf16[8,32,1536]{2,1,0:T(8,128)(2,1)}, u32[]{:S(2)}, u32[]{:S(2)}) %all-to-all-start.2) | async-done | bytes 786464 | tf_op jit(solution)/shard_map/all_to_all | solution.py:658
  85.6 17.4 %all_to_all.30 = bf16[8,32,1536]{2,1,0:T(8,128)(2,1)} all-to-all(bf16[8,32,1536]{2,1,0:T(8,128)(2,1)} %copy-done.30), channel_id=1, replica_groups=mesh['x'=4,'z'=4,'y'=4,'core'=2] {'y','core'}, dimensions={0} | all-to-all | bytes 1572864 | tf_op jit(solution)/shard_map/all_to_all | solution.py:658
  103.0 4.6 %all-to-all-start.4 = ((bf16[8,2,32,1536]{3,2,1,0:T(8,128)(2,1)}), bf16[8,2,32,1536]{3,2,1,0:T(8,128)(2,1)}, u32[]{:S(2)}, u32[]{:S(2)}) async-start(bf16[8,2,32,1536]{3,2,1,0:T(8,128)(2,1)} %copy-done.20), calls=%async_computation.4 | async-start | bytes 3145728 | tf_op jit(solution)/shard_map/all_to_all | solution.py:658
  107.6 2.9 %copy-done.4 = f32[12,512,256]{2,1,0:T(8,128)S(1)} copy-done((f32[12,512,256]{2,1,0:T(8,128)S(1)}, f32[12,512,256]{2,1,0:T(8,128)}, u32[]{:S(2)}) %copy-start.4) | copy-done | bytes 6291480
  110.5 1.1 copy-done.12
  111.7 1.1 copy-done.19
  112.8 6.9 %space_back.1 = (f32[256,1536]{1,0:T(8,128)S(1)}, f32[256,1536]{1,0:T(8,128)S(1)}, bf16[256,1536]{1,0:T(8,128)(2,1)}, f32[8,128]{1,0:T(8,128)S(1)}) custom-call(f32[8,128]{1,0:T(8,128)S(1)} %get-tuple-element.50.late_ref, f32[1,64]{1,0:T(1,128)S(1)} %bitcast.28, f32[1,64]{1,0:T(1,128)S(1)} %bitcast.31, f32[256,1536]{1,0:T(8,128)S(1)} %copy-done.7, ...), custom_call_target="tpu_custom_call" | custom-call | bytes 33210000 | tf_op jit(solution)/shard_map/space_back/pallas_call | solution.py:275
  119.7 1.1 copy-done.26
  120.8 1.2 copy-done.28
  122.4 0.8 collective-permute-done
  123.2 1.5 collective-permute-start.1
  124.7 2.8 %collective-permute-start.2 = (f32[8,128]{1,0:T(8,128)S(1)}, f32[8,128]{1,0:T(8,128)S(1)}, u32[]{:S(2)}, u32[]{:S(2)}) collective-permute-start(f32[8,128]{1,0:T(8,128)S(1)} %add.7.refs_0_), channel_id=1, source_target_pairs={{0,64},{32,96},{64,0},{96,32},{1,65},{33,97},{65,1},{97,33},{2,66}... | collective-permute-start | bytes 12296 | tf_op jit(solution)/shard_map/ppermute | solution.py:687
  127.5 1.3 collective-permute-start.3
  128.9 0.9 collective-permute-done.2.refs_2_
  129.8 1.3 collective-permute-done.3.refs_3_
  131.1 4.6 %copy-done.2 = bf16[1,1,2048,3072]{3,2,1,0:T(8,128)(2,1)S(1)} copy-done((bf16[1,1,2048,3072]{3,2,1,0:T(8,128)(2,1)S(1)}, bf16[1,1,2048,3072]{3,2,1,0:T(8,128)(2,1)}, u32[]{:S(2)}) %copy-start.2) | copy-done | bytes 12582936
  135.7 2.8 %copy-done.5 = bf16[2048,1536]{1,0:T(8,128)(2,1)S(1)} copy-done((bf16[2048,1536]{1,0:T(8,128)(2,1)S(1)}, bf16[2048,1536]{1,0:T(8,128)(2,1)}, u32[]{:S(2)}) %copy-start.5) | copy-done | bytes 6291480
  138.5 5.5 %weight_parts.1 = bf16[16,80,512]{2,1,0:T(8,128)(2,1)S(1)} custom-call(s32[2]{0:T(128)S(1)} %pad_add_fusion.1.place_ref, bf16[2,192,384]{2,1,0:T(8,128)(2,1)S(1)} %copy-done.31, bf16[2048,1536]{1,0:T(8,128)(2,1)S(1)} %copy-done.5, bf16[2048,3072]{1,0:T(8,128)(2,1)S(1)} %bitcast.18, f32[8,128]{1,0:T(8,128)S(1)} %add.7.refs_0_, ...), custom_call_target="tpu_custom_call" | custom-call | bytes 35055000 | tf_op jit(solution)/shard_map/weight_parts/pallas_call | solution.py:568
  144.0 1.1 copy-done.11
  145.0 8.2 %all-to-all-start.5 = ((bf16[16,80,512]{2,1,0:T(8,128)(2,1)}), bf16[16,80,512]{2,1,0:T(8,128)(2,1)}, u32[]{:S(2)}, u32[]{:S(2)}) async-start(bf16[16,80,512]{2,1,0:T(8,128)(2,1)} %copy-done.11), calls=%async_computation.5 | async-start | bytes 2621440 | tf_op jit(solution)/shard_map/all_to_all | solution.py:658
  153.2 3.7 %copy-done.1 = bf16[1536,3072]{1,0:T(8,128)(2,1)S(1)} copy-done((bf16[1536,3072]{1,0:T(8,128)(2,1)S(1)}, bf16[1536,3072]{1,0:T(8,128)(2,1)}, u32[]{:S(2)}) %copy-start.1) | copy-done | bytes 9437208
  156.9 5.7 %project.1 = bf16[256,3072]{1,0:T(8,128)(2,1)} custom-call(bf16[256,1536]{1,0:T(8,128)(2,1)} %bitcast.7.mixed_ref, bf16[1536,3072]{1,0:T(8,128)(2,1)S(1)} %copy-done.1), custom_call_target="tpu_custom_call" | custom-call | bytes 25830000 | tf_op jit(solution)/shard_map/project/pallas_call | solution.py:502
  162.6 4.9 %norm_back.1 = (bf16[256,1536]{1,0:T(8,128)(2,1)}, bf16[256,1536]{1,0:T(8,128)(2,1)}) custom-call(f32[256,1536]{1,0:T(8,128)S(1)} %copy-done.7, f32[256,1536]{1,0:T(8,128)S(1)} %copy-done.9, f32[256,1536]{1,0:T(8,128)S(1)} %copy-done.23, f32[256,1536]{1,0:T(8,128)S(1)} %copy-done.25, f32[1,64]{1,0:T(1,128)S(1)} %bitcast.29, f32[1,64]{1,0:T(1,128)S(1)} %bitcast.32, ...), custom_call_target="tpu_custom_call" | custom-call | bytes 25830000 | tf_op jit(solution)/shard_map/norm_back/pallas_call | solution.py:452
  167.5 5.1 %all-to-all-done.5.parts_ref = bf16[16,80,512]{2,1,0:T(8,128)(2,1)} async-done(((bf16[16,80,512]{2,1,0:T(8,128)(2,1)}), bf16[16,80,512]{2,1,0:T(8,128)(2,1)}, u32[]{:S(2)}, u32[]{:S(2)}) %all-to-all-start.5) | async-done | bytes 1310752 | tf_op jit(solution)/shard_map/all_to_all | solution.py:658
  172.6 2.2 %sum_parts.1 = (f32[12,3072]{1,0:T(8,128)}, f32[1,64]{1,0:T(1,128)}, f32[1,64]{1,0:T(1,128)}) custom-call(bf16[16,80,512]{2,1,0:T(8,128)(2,1)} %all-to-all-done.5.parts_ref), custom_call_target="tpu_custom_call" | custom-call | bytes 8118000 | tf_op jit(solution)/shard_map/sum_parts/pallas_call | solution.py:609
  (59 shorter events, 2.0 us)
Async XLA Ops:
  7.2 1.1 copy-start.13
  7.2 1.4 copy-start.15
  7.2 1.4 copy-start.32
  7.2 1.3 copy-start.33
  7.2 78.3 %all-gather.6.cloned.1.call-start = ((), (), s32[]{:S(2)}) async-start(), calls=%async_computation.7 | async-start | bytes 14155776 | tf_op jit(solution)/shard_map/all_gather | solution.py:663
  12.3 6.6 %copy-start.10 = (bf16[1,1,256,3072]{3,2,1,0:T(8,128)(2,1)S(1)}, bf16[1,1,256,3072]{3,2,1,0:T(8,128)(2,1)}, u32[]{:S(2)}) copy-start(bf16[1,1,256,3072]{3,2,1,0:T(8,128)(2,1)} %param.20) | copy-start | bytes 4718596
  12.3 26.3 %all-to-all-start = ((bf16[8,2,32,1536]{3,2,1,0:T(8,128)(2,1)}), bf16[8,2,32,1536]{3,2,1,0:T(8,128)(2,1)S(1)}, u32[]{:S(2)}, u32[]{:S(2)}) async-start(bf16[8,2,32,1536]{3,2,1,0:T(8,128)(2,1)} %norm.1.qk_ref), calls=%async_computation | async-start | bytes 3145728 | tf_op jit(solution)/shard_map/all_to_all | solution.py:658
  19.0 4.4 %copy-start = (bf16[1536,3072]{1,0:T(8,128)(2,1)S(1)}, bf16[1536,3072]{1,0:T(8,128)(2,1)}, u32[]{:S(2)}) copy-start(bf16[1536,3072]{1,0:T(8,128)(2,1)} %weight_ref.3) | copy-start | bytes 28311556
  23.4 4.2 %copy-start.18 = (bf16[1,1,256,1536]{3,2,1,0:T(8,128)(2,1)S(1)}, bf16[1,1,256,1536]{3,2,1,0:T(8,128)(2,1)}, u32[]{:S(2)}) copy-start(bf16[1,1,256,1536]{3,2,1,0:T(8,128)(2,1)} %param.13) | copy-start | bytes 2359300
  32.8 2.6 %copy-start.3 = (f32[12,512,256]{2,1,0:T(8,128)}, f32[12,512,256]{2,1,0:T(8,128)S(1)}, u32[]{:S(2)}) copy-start(f32[12,512,256]{2,1,0:T(8,128)S(1)} %get-tuple-element.53.chances_ref) | copy-start | bytes 18874372
  35.4 1.2 copy-start.21
  38.6 25.1 %all-to-all-start.1 = ((bf16[8,2,32,1536]{3,2,1,0:T(8,128)(2,1)}), bf16[8,2,32,1536]{3,2,1,0:T(8,128)(2,1)S(1)}, u32[]{:S(2)}, u32[]{:S(2)}) async-start(bf16[8,2,32,1536]{3,2,1,0:T(8,128)(2,1)} %copy-done.21), calls=%async_computation.1 | async-start | bytes 3145728 | tf_op jit(solution)/shard_map/all_to_all | solution.py:658
  42.2 1.1 copy-start.14
  43.4 1.1 copy-start.16
  47.9 1.2 copy-start.6
  49.1 1.2 copy-start.8
  50.2 1.2 copy-start.22
  51.4 1.1 copy-start.24
  67.3 0.9 copy-start.17
  68.2 17.4 %all-to-all-start.2 = ((bf16[8,32,1536]{2,1,0:T(8,128)(2,1)}), bf16[8,32,1536]{2,1,0:T(8,128)(2,1)}, u32[]{:S(2)}, u32[]{:S(2)}) async-start(bf16[8,32,1536]{2,1,0:T(8,128)(2,1)} %copy-done.17), calls=%async_computation.2 | async-start | bytes 1572864 | tf_op jit(solution)/shard_map/all_to_all | solution.py:658
  72.4 58.7 %all-gather.4.cloned.1.call-start = ((), (), s32[]{:S(2)}) async-start(), calls=%async_computation.6 | async-start | bytes 7077888 | tf_op jit(solution)/shard_map/all_gather | solution.py:676
  77.7 1.1 copy-start.20
  78.8 0.9 copy-start.30
  103.0 4.6 %copy-start.7 = (f32[256,1536]{1,0:T(8,128)S(1)}, f32[256,1536]{1,0:T(8,128)}, u32[]{:S(2)}) copy-start(f32[256,1536]{1,0:T(8,128)} %copy-done.6) | copy-start | bytes 4718596
  103.0 4.6 %copy-start.9 = (f32[256,1536]{1,0:T(8,128)S(1)}, f32[256,1536]{1,0:T(8,128)}, u32[]{:S(2)}) copy-start(f32[256,1536]{1,0:T(8,128)} %copy-done.8) | copy-start | bytes 4718596
  103.0 42.0 %all-to-all-start.4 = ((bf16[8,2,32,1536]{3,2,1,0:T(8,128)(2,1)}), bf16[8,2,32,1536]{3,2,1,0:T(8,128)(2,1)}, u32[]{:S(2)}, u32[]{:S(2)}) async-start(bf16[8,2,32,1536]{3,2,1,0:T(8,128)(2,1)} %copy-done.20), calls=%async_computation.4 | async-start | bytes 3145728 | tf_op jit(solution)/shard_map/all_to_all | solution.py:658
  107.6 2.9 %copy-start.4 = (f32[12,512,256]{2,1,0:T(8,128)S(1)}, f32[12,512,256]{2,1,0:T(8,128)}, u32[]{:S(2)}) copy-start(f32[12,512,256]{2,1,0:T(8,128)} %copy-done.3) | copy-start | bytes 18874372
  110.5 1.1 copy-start.12
  111.7 1.1 copy-start.19
  112.8 18.3 %copy-start.31 = (bf16[2,192,384]{2,1,0:T(8,128)(2,1)S(1)}, bf16[2,192,384]{2,1,0:T(8,128)(2,1)}, u32[]{:S(2)}) copy-start(bf16[2,192,384]{2,1,0:T(8,128)(2,1)} %constant.16.clone.order_ref) | copy-start | bytes 884740
  119.7 1.1 copy-start.26
  120.8 1.2 copy-start.28
  122.0 1.2 collective-permute-start
  123.2 5.7 %collective-permute-start.1 = (f32[8,128]{1,0:T(8,128)S(1)}, f32[8,128]{1,0:T(8,128)S(1)}, u32[]{:S(2)}, u32[]{:S(2)}) collective-permute-start(f32[8,128]{1,0:T(8,128)S(1)} %add.7.refs_0_), channel_id=1, source_target_pairs={{0,32},{32,64},{64,96},{96,0},{1,33},{33,65},{65,97},{97,1},{2,34}... | collective-permute-start | bytes 12296 | tf_op jit(solution)/shard_map/ppermute | solution.py:687
  124.7 5.1 %collective-permute-start.2 = (f32[8,128]{1,0:T(8,128)S(1)}, f32[8,128]{1,0:T(8,128)S(1)}, u32[]{:S(2)}, u32[]{:S(2)}) collective-permute-start(f32[8,128]{1,0:T(8,128)S(1)} %add.7.refs_0_), channel_id=1, source_target_pairs={{0,64},{32,96},{64,0},{96,32},{1,65},{33,97},{65,1},{97,33},{2,66}... | collective-permute-start | bytes 12296 | tf_op jit(solution)/shard_map/ppermute | solution.py:687
  127.5 3.6 %collective-permute-start.3 = (f32[8,128]{1,0:T(8,128)S(1)}, f32[8,128]{1,0:T(8,128)S(1)}, u32[]{:S(2)}, u32[]{:S(2)}) collective-permute-start(f32[8,128]{1,0:T(8,128)S(1)} %add.7.refs_0_), channel_id=1, source_target_pairs={{0,96},{32,0},{64,32},{96,64},{1,97},{33,1},{65,33},{97,65},{2,98}... | collective-permute-start | bytes 12296 | tf_op jit(solution)/shard_map/ppermute | solution.py:687
  131.1 4.6 %copy-start.2 = (bf16[1,1,2048,3072]{3,2,1,0:T(8,128)(2,1)S(1)}, bf16[1,1,2048,3072]{3,2,1,0:T(8,128)(2,1)}, u32[]{:S(2)}) copy-start(bf16[1,1,2048,3072]{3,2,1,0:T(8,128)(2,1)} %all-gather.6.cloned.1.call-done) | copy-start | bytes 37748740
  135.7 2.8 %copy-start.5 = (bf16[2048,1536]{1,0:T(8,128)(2,1)S(1)}, bf16[2048,1536]{1,0:T(8,128)(2,1)}, u32[]{:S(2)}) copy-start(bf16[2048,1536]{1,0:T(8,128)(2,1)} %all-gather.4.cloned.1.call-done.mixed_ref) | copy-start | bytes 18874372
  144.0 1.1 copy-start.11
  145.0 27.6 %all-to-all-start.5 = ((bf16[16,80,512]{2,1,0:T(8,128)(2,1)}), bf16[16,80,512]{2,1,0:T(8,128)(2,1)}, u32[]{:S(2)}, u32[]{:S(2)}) async-start(bf16[16,80,512]{2,1,0:T(8,128)(2,1)} %copy-done.11), calls=%async_computation.5 | async-start | bytes 2621440 | tf_op jit(solution)/shard_map/all_to_all | solution.py:658
  153.2 3.7 %copy-start.1 = (bf16[1536,3072]{1,0:T(8,128)(2,1)S(1)}, bf16[1536,3072]{1,0:T(8,128)(2,1)}, u32[]{:S(2)}) copy-start(bf16[1536,3072]{1,0:T(8,128)(2,1)} %weight_ref.3) | copy-start | bytes 28311556
  156.9 5.7 %copy-start.23 = (f32[256,1536]{1,0:T(8,128)S(1)}, f32[256,1536]{1,0:T(8,128)}, u32[]{:S(2)}) copy-start(f32[256,1536]{1,0:T(8,128)} %copy-done.22) | copy-start | bytes 4718596
  156.9 5.7 %copy-start.25 = (f32[256,1536]{1,0:T(8,128)S(1)}, f32[256,1536]{1,0:T(8,128)}, u32[]{:S(2)}) copy-start(f32[256,1536]{1,0:T(8,128)} %copy-done.24) | copy-start | bytes 4718596
  156.9 5.7 %copy-start.27 = (f32[256,1536]{1,0:T(8,128)S(1)}, f32[256,1536]{1,0:T(8,128)}, u32[]{:S(2)}) copy-start(f32[256,1536]{1,0:T(8,128)} %copy-done.26) | copy-start | bytes 4718596
  156.9 5.7 %copy-start.29 = (f32[256,1536]{1,0:T(8,128)S(1)}, f32[256,1536]{1,0:T(8,128)}, u32[]{:S(2)}) copy-start(f32[256,1536]{1,0:T(8,128)} %copy-done.28) | copy-start | bytes 4718596
Sparse Core Ops, SparseCore 0:
  9.7 69.7 all-gather.5
  85.7 41.1 all-gather.3

commit v4 on v3

--- a/solution.py
+++ b/solution.py
@@ -20,7 +20,8 @@
 BLOCK = 16
 NEG = -1e30
 SCALE = HD**-0.5
-PARAMS = pltpu.CompilerParams(vmem_limit_bytes=24 * 1024 * 1024)
+PARAMS = pltpu.CompilerParams(vmem_limit_bytes=56 * 1024 * 1024)
+SMALL = pltpu.CompilerParams(vmem_limit_bytes=16 * 1024 * 1024)
 
 
 def cost(microseconds):
@@ -393,7 +394,7 @@
         in_specs=[SMEM, double, double],
         out_specs=single,
         out_shape=single_shape,
-        compiler_params=PARAMS,
+        compiler_params=SMALL,
         cost_estimate=cost(5),
         name="time_forward",
     )(counts, normed, arrived)
@@ -408,7 +409,7 @@
         in_specs=[SMEM, double, double],
         out_specs=[double, single, pl.BlockSpec((8, LANES), lambda n: (0, 0))],
         out_shape=[double_shape, single_shape, jax.ShapeDtypeStruct((8, LANES), F32)],
-        compiler_params=PARAMS,
+        compiler_params=SMALL,
         cost_estimate=cost(6.5),
         name="time_back",
     )(counts, normed, arrived)
@@ -611,7 +612,7 @@
         in_specs=[VMEM],
         out_specs=[VMEM] * 3,
         out_shape=[jax.ShapeDtypeStruct((own, PIECES * block), F32), gain, gain],
-        compiler_params=PARAMS,
+        compiler_params=SMALL,
         cost_estimate=cost(2.2),
         name="sum_parts",
     )(parts)

time: 183 us -> 174 us (0.951)
  local copies, waits for them, and re-layouts: 38.2 us -> 2.37 us
  Pallas kernels: 50.4 us -> 69.2 us
  waiting for transfers between devices: 27.9 us -> 36.3 us
    unnamed x68 -> x18, local copies, waits for them, and re-layouts: 38.2 us -> 2.37 us
    all_to_all x5, waiting for transfers between devices: 24.2 us -> 31.7 us  [exchange(): return lax.all_to_all(tensor, axes, split_axis=0, concat_axis=0, tiled=True)]
    pallas_call x1, Pallas kernels: 4.1 us -> 8.65 us  [grad_mixed_of(): pl.pallas_call(grad_mixed_kernel, grid=(inner // WIDE,), in_specs=[pl.Blo...]
    pallas_call x1, Pallas kernels: 5.49 us -> 9.58 us  [weight_parts(): pl.pallas_call(weight_kernel, grid_spec=pltpu.PrefetchScalarGridSpec(num_...]
    pallas_call x1, Pallas kernels: 6.86 us -> 9.21 us  [space_back(): pl.pallas_call(space_back_kernel, grid=(inner // WIDE,), in_specs=[pl.Blo...]
    pallas_call x1, Pallas kernels: 3.38 us -> 5.69 us  [hats_of(): pl.pallas_call(hats_kernel, grid=(inner // NORM_WIDE,), in_specs=[tokens,...]
    pallas_call x1, Pallas kernels: 4.91 us -> 6.92 us  [norm_back(): pl.pallas_call(norm_back_kernel, grid=(inner // NORM_WIDE,), in_specs=[to...]
  transfers between devices with their start and end apart: 11 -> 11, of which waited for: 7 -> 8; matrix products, arithmetic and copies ran while one was open for 0% -> 1% of each run, Pallas kernels for 27% -> 40%
where the time goes in v4:
time: 174 us; the launch traced here: 173 us
  Pallas kernels  69.2 us (40%)
  waiting for transfers between devices  36.3 us (21%)
  starting transfers between devices  29.6 us (17%)
  blocking collectives  17.5 us (10%)
  between operations  16.1 us (9%)
  local copies, waits for them, and re-layouts  2.37 us (1%)
  other arithmetic  1.93 us (1%)
    all_to_all x5, waiting for transfers between devices, exchange(): return lax.all_to_all(tensor, axes, split_axis=0, concat_axis=0, tiled=True)  31.7 us
    all_to_all x5, starting transfers between devices, exchange(): return lax.all_to_all(tensor, axes, split_axis=0, concat_axis=0, tiled=True)  23.4 us
    all_to_all x1, blocking collectives, exchange(): return lax.all_to_all(tensor, axes, split_axis=0, concat_axis=0, tiled=True)  17.5 us
    pallas_call x1, Pallas kernels, weight_parts(): pl.pallas_call(weight_kernel, grid_spec=pltpu.PrefetchScalarGridSpec(num_...  9.58 us
    pallas_call x1, Pallas kernels, space_back(): pl.pallas_call(space_back_kernel, grid=(inner // WIDE,), in_specs=[pl.Blo...  9.21 us
    pallas_call x1, Pallas kernels, grad_mixed_of(): pl.pallas_call(grad_mixed_kernel, grid=(inner // WIDE,), in_specs=[pl.Blo...  8.65 us
    pallas_call x1, Pallas kernels, space_forward(): pl.pallas_call(space_kernel, grid=(inner // WIDE,), in_specs=[SMEM, pl.Bl...  7.02 us
    pallas_call x1, Pallas kernels, project(): pl.pallas_call(project_kernel, grid=(4,), in_specs=[pl.BlockSpec((CELLS,...  6.98 us
  transfers between devices with their start and end apart: 11, of which 8 were waited for; matrix products, arithmetic and copies ran while one was open for 1% of the time, Pallas kernels for 40%

profile of v4, /device:TPU:0, one launch (start us, length us, event | category | flops | bytes accessed | tf_op | source)
XLA Modules:
  0.0 172.9 jit_solution(8049674913514456657)
XLA Ops:
  7.2 0.0 all-gather.6.cloned.1.call-start
  7.2 0.7 all-gather.6.cloned.1.call-update
  7.9 5.0 %norm.1.qk_ref = bf16[8,2,32,1536]{3,2,1,0:T(8,128)(2,1)} custom-call(bf16[256,1536]{1,0:T(8,128)(2,1)} %bitcast.21, bf16[256,1536]{1,0:T(8,128)(2,1)} %bitcast.23, f32[1,64]{1,0:T(1,128)} %bitcast.28, f32[1,64]{1,0:T(1,128)} %bitcast.31), custom_call_target="tpu_custom_call" | custom-call | bytes 18450000 | tf_op jit(solution)/shard_map/norm/pallas_call | solution.py:132
  12.9 4.6 %all-to-all-start = ((bf16[8,2,32,1536]{3,2,1,0:T(8,128)(2,1)}), bf16[8,2,32,1536]{3,2,1,0:T(8,128)(2,1)S(1)}, u32[]{:S(2)}, u32[]{:S(2)}) async-start(bf16[8,2,32,1536]{3,2,1,0:T(8,128)(2,1)} %norm.1.qk_ref), calls=%async_computation | async-start | bytes 3145728 | tf_op jit(solution)/shard_map/all_to_all | solution.py:659
  19.4 8.6 %grad_mixed.1.gm_ref = bf16[256,1536]{1,0:T(8,128)(2,1)} custom-call(bf16[256,3072]{1,0:T(8,128)(2,1)} %bitcast.19, bf16[1536,3072]{1,0:T(8,128)(2,1)} %weight_ref.3), custom_call_target="tpu_custom_call" | custom-call | bytes 32103000 | tf_op jit(solution)/shard_map/grad_mixed/pallas_call | solution.py:481
  28.0 0.6 pad_add_fusion.counts_ref
  28.6 7.0 %space_forward.1 = (bf16[8,2,32,1536]{3,2,1,0:T(8,128)(2,1)}, f32[12,512,256]{2,1,0:T(8,128)}) custom-call(s32[4]{0:T(128)} %pad_add_fusion.counts_ref, bf16[8,2,32,1536]{3,2,1,0:T(8,128)(2,1)} %norm.1.qk_ref, bf16[256,1536]{1,0:T(8,128)(2,1)} %bitcast.25, bf16[256,1536]{1,0:T(8,128)(2,1)} %grad_mixed.1.gm_ref), custom_call_target="tpu_custom_call" | custom-call | bytes 25830000 | tf_op jit(solution)/shard_map/space_forward/pallas_call | solution.py:196
  35.6 3.4 %all-to-all-done.qk_ref = bf16[8,2,32,1536]{3,2,1,0:T(8,128)(2,1)S(1)} async-done(((bf16[8,2,32,1536]{3,2,1,0:T(8,128)(2,1)}), bf16[8,2,32,1536]{3,2,1,0:T(8,128)(2,1)S(1)}, u32[]{:S(2)}, u32[]{:S(2)}) %all-to-all-start) | async-done | bytes 1572896 | tf_op jit(solution)/shard_map/all_to_all | solution.py:659
  39.0 3.6 %all-to-all-start.1 = ((bf16[8,2,32,1536]{3,2,1,0:T(8,128)(2,1)}), bf16[8,2,32,1536]{3,2,1,0:T(8,128)(2,1)S(1)}, u32[]{:S(2)}, u32[]{:S(2)}) async-start(bf16[8,2,32,1536]{3,2,1,0:T(8,128)(2,1)} %get-tuple-element.38), calls=%async_computation.1 | async-start | bytes 3145728 | tf_op jit(solution)/shard_map/all_to_all | solution.py:659
  42.6 0.0 copy-start.2
  42.6 5.7 %hats.1 = (f32[256,1536]{1,0:T(8,128)}, f32[256,1536]{1,0:T(8,128)}, f32[256,1536]{1,0:T(8,128)}, f32[256,1536]{1,0:T(8,128)}) custom-call(bf16[256,1536]{1,0:T(8,128)(2,1)} %bitcast.22, bf16[256,1536]{1,0:T(8,128)(2,1)} %bitcast.24), custom_call_target="tpu_custom_call" | custom-call | bytes 20664000 | tf_op jit(solution)/shard_map/hats/pallas_call | solution.py:157
  48.3 15.8 %all-to-all-done.1.sg_ref = bf16[8,2,32,1536]{3,2,1,0:T(8,128)(2,1)S(1)} async-done(((bf16[8,2,32,1536]{3,2,1,0:T(8,128)(2,1)}), bf16[8,2,32,1536]{3,2,1,0:T(8,128)(2,1)S(1)}, u32[]{:S(2)}, u32[]{:S(2)}) %all-to-all-start.1) | async-done | bytes 1572896 | tf_op jit(solution)/shard_map/all_to_all | solution.py:659
  64.1 0.0 copy-done.2
  64.1 3.5 %time_forward.1 = bf16[8,32,1536]{2,1,0:T(8,128)(2,1)S(1)} custom-call(s32[4]{0:T(128)S(1)} %copy-done.2, bf16[8,2,32,1536]{3,2,1,0:T(8,128)(2,1)S(1)} %all-to-all-done.qk_ref, bf16[8,2,32,1536]{3,2,1,0:T(8,128)(2,1)S(1)} %all-to-all-done.1.sg_ref), custom_call_target="tpu_custom_call" | custom-call | bytes 18450000 | tf_op jit(solution)/shard_map/time_forward/pallas_call | solution.py:391
  67.7 0.0 copy-start
  67.7 0.9 copy-done
  68.5 4.2 %all-to-all-start.2 = ((bf16[8,32,1536]{2,1,0:T(8,128)(2,1)}), bf16[8,32,1536]{2,1,0:T(8,128)(2,1)}, u32[]{:S(2)}, u32[]{:S(2)}) async-start(bf16[8,32,1536]{2,1,0:T(8,128)(2,1)} %copy-done), calls=%async_computation.2 | async-start | bytes 1572864 | tf_op jit(solution)/shard_map/all_to_all | solution.py:659
  72.8 0.0 all-gather.4.cloned.1.call-start
  72.8 5.8 %time_back.1 = (bf16[8,2,32,1536]{3,2,1,0:T(8,128)(2,1)}, bf16[8,32,1536]{2,1,0:T(8,128)(2,1)S(1)}, f32[8,128]{1,0:T(8,128)S(1)}) custom-call(s32[4]{0:T(128)S(1)} %copy-done.2, bf16[8,2,32,1536]{3,2,1,0:T(8,128)(2,1)S(1)} %all-to-all-done.qk_ref, bf16[8,2,32,1536]{3,2,1,0:T(8,128)(2,1)S(1)} %all-to-all-done.1.sg_ref), custom_call_target="tpu_custom_call" | custom-call | bytes 23985000 | tf_op jit(solution)/shard_map/time_back/pallas_call | solution.py:406
  78.6 0.9 copy-done.1
  79.5 0.6 copy-done.3
  80.1 5.8 %all-to-all-done.2 = bf16[8,32,1536]{2,1,0:T(8,128)(2,1)} async-done(((bf16[8,32,1536]{2,1,0:T(8,128)(2,1)}), bf16[8,32,1536]{2,1,0:T(8,128)(2,1)}, u32[]{:S(2)}, u32[]{:S(2)}) %all-to-all-start.2) | async-done | bytes 786464 | tf_op jit(solution)/shard_map/all_to_all | solution.py:659
  85.9 0.0 all-gather.4.cloned.1.call-update
  85.9 17.5 %all_to_all.30 = bf16[8,32,1536]{2,1,0:T(8,128)(2,1)} all-to-all(bf16[8,32,1536]{2,1,0:T(8,128)(2,1)} %copy-done.1), channel_id=1, replica_groups=mesh['x'=4,'z'=4,'y'=4,'core'=2] {'y','core'}, dimensions={0} | all-to-all | bytes 1572864 | tf_op jit(solution)/shard_map/all_to_all | solution.py:659
  103.4 3.6 %all-to-all-start.4 = ((bf16[8,2,32,1536]{3,2,1,0:T(8,128)(2,1)}), bf16[8,2,32,1536]{3,2,1,0:T(8,128)(2,1)S(1)}, u32[]{:S(2)}, u32[]{:S(2)}) async-start(bf16[8,2,32,1536]{3,2,1,0:T(8,128)(2,1)} %get-tuple-element.57), calls=%async_computation.4 | async-start | bytes 3145728 | tf_op jit(solution)/shard_map/all_to_all | solution.py:659
  107.0 9.2 %space_back.1 = (f32[256,1536]{1,0:T(8,128)}, f32[256,1536]{1,0:T(8,128)}, bf16[256,1536]{1,0:T(8,128)(2,1)}, f32[8,128]{1,0:T(8,128)}) custom-call(f32[8,128]{1,0:T(8,128)} %copy-done.3, f32[1,64]{1,0:T(1,128)} %bitcast.29, f32[1,64]{1,0:T(1,128)} %bitcast.32, f32[256,1536]{1,0:T(8,128)} %get-tuple-element.46.hat_q_ref, ...), custom_call_target="tpu_custom_call" | custom-call | bytes 33210000 | tf_op jit(solution)/shard_map/space_back/pallas_call | solution.py:276
  116.2 0.4 collective-permute-start
  116.6 1.0 collective-permute-done
  117.7 0.7 add.7.refs_0_
  118.4 1.5 collective-permute-start.1
  119.8 2.8 %collective-permute-start.2 = (f32[8,128]{1,0:T(8,128)S(1)}, f32[8,128]{1,0:T(8,128)S(1)}, u32[]{:S(2)}, u32[]{:S(2)}) collective-permute-start(f32[8,128]{1,0:T(8,128)S(1)} %add.7.refs_0_), channel_id=1, source_target_pairs={{0,64},{32,96},{64,0},{96,32},{1,65},{33,97},{65,1},{97,33},{2,66}... | collective-permute-start | bytes 12296 | tf_op jit(solution)/shard_map/ppermute | solution.py:688
  122.6 1.4 collective-permute-start.3
  124.0 0.7 pad_add_fusion.1.place_ref
  124.6 0.0 collective-permute-done.1.refs_1_
  124.7 0.4 collective-permute-done.2.refs_2_
  125.0 1.2 collective-permute-done.3.refs_3_
  126.2 1.2 all-gather.4.cloned.1.call-done.mixed_ref
  127.5 0.0 copy-done.5
  127.5 0.0 copy-done.6
  127.5 0.0 copy-done.7
  127.5 9.6 %weight_parts.1 = bf16[16,80,512]{2,1,0:T(8,128)(2,1)} custom-call(s32[2]{0:T(128)} %pad_add_fusion.1.place_ref, bf16[2,192,384]{2,1,0:T(8,128)(2,1)} %constant.16.clone.order_ref, bf16[2048,1536]{1,0:T(8,128)(2,1)} %all-gather.4.cloned.1.call-done.mixed_ref, bf16[2048,3072]{1,0:T(8,128)(2,1)} %bitcast.18, f32[8,128]{1,0:T(8,128)} %copy-done.5, ...), custom_call_target="tpu_custom_call" | custom-call | bytes 35055000 | tf_op jit(solution)/shard_map/weight_parts/pallas_call | solution.py:569
  137.1 0.0 all-to-all-done.4.late_ref
  137.1 7.5 %all-to-all-start.5 = ((bf16[16,80,512]{2,1,0:T(8,128)(2,1)}), bf16[16,80,512]{2,1,0:T(8,128)(2,1)S(1)}, u32[]{:S(2)}, u32[]{:S(2)}) async-start(bf16[16,80,512]{2,1,0:T(8,128)(2,1)} %weight_parts.1), calls=%async_computation.5 | async-start | bytes 2621440 | tf_op jit(solution)/shard_map/all_to_all | solution.py:659
  144.6 7.0 %project.1 = bf16[256,3072]{1,0:T(8,128)(2,1)} custom-call(bf16[256,1536]{1,0:T(8,128)(2,1)} %bitcast.7.mixed_ref, bf16[1536,3072]{1,0:T(8,128)(2,1)} %weight_ref.3), custom_call_target="tpu_custom_call" | custom-call | bytes 25830000 | tf_op jit(solution)/shard_map/project/pallas_call | solution.py:503
  151.6 0.0 copy-done.4
  151.6 6.9 %norm_back.1 = (bf16[256,1536]{1,0:T(8,128)(2,1)}, bf16[256,1536]{1,0:T(8,128)(2,1)}) custom-call(f32[256,1536]{1,0:T(8,128)} %get-tuple-element.46.hat_q_ref, f32[256,1536]{1,0:T(8,128)} %get-tuple-element.47.hat_k_ref, f32[256,1536]{1,0:T(8,128)} %get-tuple-element.48.inverse_q_ref, f32[256,1536]{1,0:T(8,128)} %get-tuple-element.49.inverse_k_ref, ...), custom_call_target="tpu_custom_call" | custom-call | bytes 25830000 | tf_op jit(solution)/shard_map/norm_back/pallas_call | solution.py:453
  158.5 6.7 %all-to-all-done.5.parts_ref = bf16[16,80,512]{2,1,0:T(8,128)(2,1)S(1)} async-done(((bf16[16,80,512]{2,1,0:T(8,128)(2,1)}), bf16[16,80,512]{2,1,0:T(8,128)(2,1)S(1)}, u32[]{:S(2)}, u32[]{:S(2)}) %all-to-all-start.5) | async-done | bytes 1310752 | tf_op jit(solution)/shard_map/all_to_all | solution.py:659
  165.2 0.9 sum_parts.1
  (9 shorter events, 0.0 us)
Async XLA Ops:
  7.2 78.8 %all-gather.6.cloned.1.call-start = ((), (), s32[]{:S(2)}) async-start(), calls=%async_computation.7 | async-start | bytes 14155776 | tf_op jit(solution)/shard_map/all_gather | solution.py:664
  12.9 26.1 %all-to-all-start = ((bf16[8,2,32,1536]{3,2,1,0:T(8,128)(2,1)}), bf16[8,2,32,1536]{3,2,1,0:T(8,128)(2,1)S(1)}, u32[]{:S(2)}, u32[]{:S(2)}) async-start(bf16[8,2,32,1536]{3,2,1,0:T(8,128)(2,1)} %norm.1.qk_ref), calls=%async_computation | async-start | bytes 3145728 | tf_op jit(solution)/shard_map/all_to_all | solution.py:659
  39.0 25.1 %all-to-all-start.1 = ((bf16[8,2,32,1536]{3,2,1,0:T(8,128)(2,1)}), bf16[8,2,32,1536]{3,2,1,0:T(8,128)(2,1)S(1)}, u32[]{:S(2)}, u32[]{:S(2)}) async-start(bf16[8,2,32,1536]{3,2,1,0:T(8,128)(2,1)} %get-tuple-element.38), calls=%async_computation.1 | async-start | bytes 3145728 | tf_op jit(solution)/shard_map/all_to_all | solution.py:659
  42.6 21.5 %copy-start.2 = (s32[4]{0:T(128)S(1)}, s32[4]{0:T(128)}, u32[]{:S(2)}) copy-start(s32[4]{0:T(128)} %pad_add_fusion.counts_ref) | copy-start | bytes 52
  67.7 0.9 copy-start
  68.5 17.4 %all-to-all-start.2 = ((bf16[8,32,1536]{2,1,0:T(8,128)(2,1)}), bf16[8,32,1536]{2,1,0:T(8,128)(2,1)}, u32[]{:S(2)}, u32[]{:S(2)}) async-start(bf16[8,32,1536]{2,1,0:T(8,128)(2,1)} %copy-done), calls=%async_computation.2 | async-start | bytes 1572864 | tf_op jit(solution)/shard_map/all_to_all | solution.py:659
  72.8 54.7 %all-gather.4.cloned.1.call-start = ((), (), s32[]{:S(2)}) async-start(), calls=%async_computation.6 | async-start | bytes 7077888 | tf_op jit(solution)/shard_map/all_gather | solution.py:677
  78.6 0.9 copy-start.1
  79.5 0.6 copy-start.3
  103.4 33.7 %all-to-all-start.4 = ((bf16[8,2,32,1536]{3,2,1,0:T(8,128)(2,1)}), bf16[8,2,32,1536]{3,2,1,0:T(8,128)(2,1)S(1)}, u32[]{:S(2)}, u32[]{:S(2)}) async-start(bf16[8,2,32,1536]{3,2,1,0:T(8,128)(2,1)} %get-tuple-element.57), calls=%async_computation.4 | async-start | bytes 3145728 | tf_op jit(solution)/shard_map/all_to_all | solution.py:659
  116.2 1.5 collective-permute-start
  118.4 9.1 %copy-start.5 = (f32[8,128]{1,0:T(8,128)}, f32[8,128]{1,0:T(8,128)S(1)}, u32[]{:S(2)}) copy-start(f32[8,128]{1,0:T(8,128)S(1)} %add.7.refs_0_) | copy-start | bytes 12292
  118.4 6.3 %collective-permute-start.1 = (f32[8,128]{1,0:T(8,128)S(1)}, f32[8,128]{1,0:T(8,128)S(1)}, u32[]{:S(2)}, u32[]{:S(2)}) collective-permute-start(f32[8,128]{1,0:T(8,128)S(1)} %add.7.refs_0_), channel_id=1, source_target_pairs={{0,32},{32,64},{64,96},{96,0},{1,33},{33,65},{65,97},{97,1},{2,34}... | collective-permute-start | bytes 12296 | tf_op jit(solution)/shard_map/ppermute | solution.py:688
  119.8 5.2 %collective-permute-start.2 = (f32[8,128]{1,0:T(8,128)S(1)}, f32[8,128]{1,0:T(8,128)S(1)}, u32[]{:S(2)}, u32[]{:S(2)}) collective-permute-start(f32[8,128]{1,0:T(8,128)S(1)} %add.7.refs_0_), channel_id=1, source_target_pairs={{0,64},{32,96},{64,0},{96,32},{1,65},{33,97},{65,1},{97,33},{2,66}... | collective-permute-start | bytes 12296 | tf_op jit(solution)/shard_map/ppermute | solution.py:688
  122.6 3.6 %collective-permute-start.3 = (f32[8,128]{1,0:T(8,128)S(1)}, f32[8,128]{1,0:T(8,128)S(1)}, u32[]{:S(2)}, u32[]{:S(2)}) collective-permute-start(f32[8,128]{1,0:T(8,128)S(1)} %add.7.refs_0_), channel_id=1, source_target_pairs={{0,96},{32,0},{64,32},{96,64},{1,97},{33,1},{65,33},{97,65},{2,98}... | collective-permute-start | bytes 12296 | tf_op jit(solution)/shard_map/ppermute | solution.py:688
  124.7 2.8 %copy-start.6 = (f32[8,128]{1,0:T(8,128)}, f32[8,128]{1,0:T(8,128)S(1)}, u32[]{:S(2)}) copy-start(f32[8,128]{1,0:T(8,128)S(1)} %collective-permute-done.1.refs_1_) | copy-start | bytes 12292
  125.0 2.5 %copy-start.7 = (f32[8,128]{1,0:T(8,128)}, f32[8,128]{1,0:T(8,128)S(1)}, u32[]{:S(2)}) copy-start(f32[8,128]{1,0:T(8,128)S(1)} %collective-permute-done.2.refs_2_) | copy-start | bytes 12292
  126.2 1.3 copy-start.8
  137.1 14.5 %copy-start.4 = (bf16[8,2,32,1536]{3,2,1,0:T(8,128)(2,1)}, bf16[8,2,32,1536]{3,2,1,0:T(8,128)(2,1)S(1)}, u32[]{:S(2)}) copy-start(bf16[8,2,32,1536]{3,2,1,0:T(8,128)(2,1)S(1)} %all-to-all-done.4.late_ref) | copy-start | bytes 4718596
  137.1 28.1 %all-to-all-start.5 = ((bf16[16,80,512]{2,1,0:T(8,128)(2,1)}), bf16[16,80,512]{2,1,0:T(8,128)(2,1)S(1)}, u32[]{:S(2)}, u32[]{:S(2)}) async-start(bf16[16,80,512]{2,1,0:T(8,128)(2,1)} %weight_parts.1), calls=%async_computation.5 | async-start | bytes 2621440 | tf_op jit(solution)/shard_map/all_to_all | solution.py:659
Sparse Core Ops, SparseCore 0:
  9.7 69.7 all-gather.5
  86.1 41.3 all-gather.3

commit v5 on v4

--- a/solution.py
+++ b/solution.py
@@ -516,7 +516,6 @@
 
 
 PIECES = 6
-STEPS = 3
 TAIL = 8
 
 
@@ -534,60 +533,62 @@
     return jnp.concatenate([rows, jnp.zeros((TAIL, block - LANES), F32)], 1).astype(BF)
 
 
-def weight_kernel(place_ref, order_ref, mixed_ref, cot_ref, *refs):
-    *gain_refs, out_ref, turned, product = refs
+def weight_kernel(counts_ref, order_ref, mixed_hbm, cot_hbm, *refs):
+    *gain_refs, out_ref, mixed_ref, cot_ref, turned, product, mixed_sem, cot_sems = refs
     shares, rows, block = out_ref.shape
-    own = product.shape[0] // shares
-
-    @pl.when(pl.program_id(0) == 0)
-    def _():
-        turned[...] = nt(order_ref[0], mixed_ref[...]).astype(BF)
-        tail = gain_rows(gain_refs, block)
+    wide = mixed_ref.shape[1]
+    own = turned.shape[0] // shares
+    left = pl.multiple_of(counts_ref[4] * wide, LANES)
+    mixed_copy = pltpu.make_async_copy(mixed_hbm.at[:, pl.ds(left, wide)], mixed_ref, mixed_sem)
+    mixed_copy.start()
+    copies = [
+        pltpu.make_async_copy(
+            cot_hbm.at[:, piece * block : (piece + 1) * block],
+            cot_ref.at[piece],
+            cot_sems.at[piece],
+        )
+        for piece in range(PIECES)
+    ]
+    for copy in copies:
+        copy.start()
+    tail = gain_rows(gain_refs, block)
+    for share in range(shares):
+        out_ref[share, rows - TAIL :] = tail
+    mixed_copy.wait()
+    turned[...] = nt(order_ref[counts_ref[5]], mixed_ref[...]).astype(BF)
+    for piece, copy in enumerate(copies):
+        copy.wait()
+        slot = piece % 2
+        product[slot] = nn(turned[...], cot_ref[piece])
         for share in range(shares):
-            out_ref[share, rows - TAIL :] = tail
-
-    product[...] = nn(turned[...], cot_ref[...])
-    for step in range(STEPS):
-
-        @pl.when(pl.program_id(0) == step)
-        def _():
-            for share in range(shares):
-                for half in range(PIECES // STEPS):
-                    top = (step * (PIECES // STEPS) + half) * own
-                    out_ref[share, top : top + own] = product[
-                        share * own : (share + 1) * own, half * block : (half + 1) * block
-                    ].astype(BF)
-
-
-def weight_parts(place, order, mixed, cotangents, gain_sums, shares):
+            out_ref[share, piece * own : (piece + 1) * own] = product[
+                slot, share * own : (share + 1) * own
+            ].astype(BF)
+
+
+def weight_parts(counts, order, mixed, cotangents, gain_sums, shares):
     tokens, width = cotangents.shape
     _, features, wide = order.shape
     block = width // PIECES
-    columns = width // STEPS
     rows = -(-(PIECES * (features // shares) + TAIL) // 16) * 16
-    gain = pl.BlockSpec((8, LANES), lambda n, place: (0, 0))
+    anywhere = pl.BlockSpec(memory_space=pl.ANY)
     return pl.pallas_call(
         weight_kernel,
-        grid_spec=pltpu.PrefetchScalarGridSpec(
-            num_scalar_prefetch=1,
-            grid=(STEPS,),
-            in_specs=[
-                pl.BlockSpec((1, features, wide), lambda n, place: (place[1], 0, 0)),
-                pl.BlockSpec((tokens, wide), lambda n, place: (0, place[0])),
-                pl.BlockSpec((tokens, columns), lambda n, place: (0, n)),
-            ]
-            + [gain] * len(gain_sums),
-            out_specs=pl.BlockSpec((shares, rows, block), lambda n, place: (0, 0, 0)),
-            scratch_shapes=[
-                pltpu.VMEM((features, tokens), BF),
-                pltpu.VMEM((features, columns), F32),
-            ],
-        ),
+        in_specs=[SMEM, VMEM, anywhere, anywhere] + [VMEM] * len(gain_sums),
+        out_specs=VMEM,
         out_shape=jax.ShapeDtypeStruct((shares, rows, block), BF),
+        scratch_shapes=[
+            pltpu.VMEM((tokens, wide), BF),
+            pltpu.VMEM((PIECES, tokens, block), BF),
+            pltpu.VMEM((features, tokens), BF),
+            pltpu.VMEM((2, features, block), F32),
+            pltpu.SemaphoreType.DMA,
+            pltpu.SemaphoreType.DMA((PIECES,)),
+        ],
         compiler_params=PARAMS,
-        cost_estimate=cost(9.5),
+        cost_estimate=cost(7.5),
         name="weight_parts",
-    )(place, order, mixed, cotangents, *gain_sums)
+    )(counts, order, mixed, cotangents, *gain_sums)
 
 
 def sum_kernel(parts_ref, out_ref, gain_q_ref, gain_k_ref):
@@ -649,7 +650,9 @@
     shares = lax.axis_size("z") * lax.axis_size("y")
     inner = out_weight.shape[0]
     rank = lax.axis_index(seq).astype(jnp.int32)
-    counts = jnp.stack([frame_counts[0], heights[0], widths[0], rank])
+    counts = [frame_counts[0], heights[0], widths[0], rank]
+    counts += [lax.axis_index("x").astype(jnp.int32), lax.axis_index("core").astype(jnp.int32)]
+    counts = jnp.stack(counts)
     gains = gain_query.reshape(1, HD), gain_key.reshape(1, HD)
     query_rows, key_rows, value_rows = queries[0, 0], keys_proj[0, 0], values_proj[0, 0]
     cot_rows = cotangent[0, 0]
@@ -672,7 +675,6 @@
     mixed_cells = time_forward(counts, normed_cells, arrived)
     mixed = exchange(mixed_cells, seq).reshape(CELLS, inner)
     late_cells, dspatial_cells, late_gains = time_back(counts, normed_cells, arrived)
-    place = jnp.stack([lax.axis_index("x"), lax.axis_index("core")]).astype(jnp.int32)
     first = (cotangents, dspatial_cells)
     gathered = lax.all_gather(after(mixed, first), group, axis=0, tiled=True)
     dspatial = exchange(after(dspatial_cells, mixed), seq).reshape(CELLS, inner)
@@ -690,7 +692,7 @@
     ]
     grad_queries, grad_keys = norm_back(hats, *gains, dq, dk, late)
     order = feature_order(inner, planes, cores, shares)
-    parts = weight_parts(place, order, gathered, cotangents, gain_sums, shares)
+    parts = weight_parts(counts, order, gathered, cotangents, gain_sums, shares)
     parts = exchange(after(parts, late), sums)
     own = order.shape[1] // shares
     grad_weight, grad_gain_query, grad_gain_key = sum_parts(parts, own)

time: 174 us -> 176 us (1.011)
  Pallas kernels: 69.2 us -> 71.3 us
    pallas_call x1, Pallas kernels: 9.58 us -> 11.6 us  [weight_parts(): pl.pallas_call(weight_kernel, in_specs=[SMEM, VMEM, anywhere, anywhere] +...]
where the time goes in v5:
time: 176 us; the launch traced here: 175 us
  Pallas kernels  71.3 us (41%)
  waiting for transfers between devices  36.8 us (21%)
  starting transfers between devices  29.6 us (17%)
  blocking collectives  17.5 us (10%)
  between operations  16.1 us (9%)
  local copies, waits for them, and re-layouts  3.03 us (2%)
    all_to_all x5, waiting for transfers between devices, exchange(): return lax.all_to_all(tensor, axes, split_axis=0, concat_axis=0, tiled=True)  31.6 us
    all_to_all x5, starting transfers between devices, exchange(): return lax.all_to_all(tensor, axes, split_axis=0, concat_axis=0, tiled=True)  23.4 us
    all_to_all x1, blocking collectives, exchange(): return lax.all_to_all(tensor, axes, split_axis=0, concat_axis=0, tiled=True)  17.5 us
    pallas_call x1, Pallas kernels, weight_parts(): pl.pallas_call(weight_kernel, in_specs=[SMEM, VMEM, anywhere, anywhere] +...  11.6 us
    pallas_call x1, Pallas kernels, space_back(): pl.pallas_call(space_back_kernel, grid=(inner // WIDE,), in_specs=[pl.Blo...  9.21 us
    pallas_call x1, Pallas kernels, grad_mixed_of(): pl.pallas_call(grad_mixed_kernel, grid=(inner // WIDE,), in_specs=[pl.Blo...  8.65 us
    pallas_call x1, Pallas kernels, space_forward(): pl.pallas_call(space_kernel, grid=(inner // WIDE,), in_specs=[SMEM, pl.Bl...  7.06 us
    pallas_call x1, Pallas kernels, project(): pl.pallas_call(project_kernel, grid=(4,), in_specs=[pl.BlockSpec((CELLS,...  6.98 us
  transfers between devices with their start and end apart: 11, of which 8 were waited for; matrix products, arithmetic and copies ran while one was open for 1% of the time, Pallas kernels for 40%

profile of v5, /device:TPU:0, one launch (start us, length us, event | category | flops | bytes accessed | tf_op | source)
XLA Modules:
  0.0 175.0 jit_solution(1189255785611842206)
XLA Ops:
  7.2 0.0 all-gather.6.cloned.1.call-start
  7.2 0.7 all-gather.6.cloned.1.call-update
  7.9 5.0 %norm.1.qk_ref = bf16[8,2,32,1536]{3,2,1,0:T(8,128)(2,1)} custom-call(bf16[256,1536]{1,0:T(8,128)(2,1)} %bitcast.21, bf16[256,1536]{1,0:T(8,128)(2,1)} %bitcast.23, f32[1,64]{1,0:T(1,128)} %bitcast.28, f32[1,64]{1,0:T(1,128)} %bitcast.31), custom_call_target="tpu_custom_call" | custom-call | bytes 18450000 | tf_op jit(solution)/shard_map/norm/pallas_call | solution.py:132
  12.9 4.6 %all-to-all-start = ((bf16[8,2,32,1536]{3,2,1,0:T(8,128)(2,1)}), bf16[8,2,32,1536]{3,2,1,0:T(8,128)(2,1)S(1)}, u32[]{:S(2)}, u32[]{:S(2)}) async-start(bf16[8,2,32,1536]{3,2,1,0:T(8,128)(2,1)} %norm.1.qk_ref), calls=%async_computation | async-start | bytes 3145728 | tf_op jit(solution)/shard_map/all_to_all | solution.py:662
  19.4 8.7 %grad_mixed.1.gm_ref = bf16[256,1536]{1,0:T(8,128)(2,1)} custom-call(bf16[256,3072]{1,0:T(8,128)(2,1)} %bitcast.19, bf16[1536,3072]{1,0:T(8,128)(2,1)} %weight_ref.3), custom_call_target="tpu_custom_call" | custom-call | bytes 32103000 | tf_op jit(solution)/shard_map/grad_mixed/pallas_call | solution.py:481
  28.0 0.7 stack.15.counts_ref
  28.7 7.1 %space_forward.1 = (bf16[8,2,32,1536]{3,2,1,0:T(8,128)(2,1)}, f32[12,512,256]{2,1,0:T(8,128)}) custom-call(s32[6]{0:T(128)} %stack.15.counts_ref, bf16[8,2,32,1536]{3,2,1,0:T(8,128)(2,1)} %norm.1.qk_ref, bf16[256,1536]{1,0:T(8,128)(2,1)} %bitcast.25, bf16[256,1536]{1,0:T(8,128)(2,1)} %grad_mixed.1.gm_ref), custom_call_target="tpu_custom_call" | custom-call | bytes 25830000 | tf_op jit(solution)/shard_map/space_forward/pallas_call | solution.py:196
  35.8 3.3 %all-to-all-done.qk_ref = bf16[8,2,32,1536]{3,2,1,0:T(8,128)(2,1)S(1)} async-done(((bf16[8,2,32,1536]{3,2,1,0:T(8,128)(2,1)}), bf16[8,2,32,1536]{3,2,1,0:T(8,128)(2,1)S(1)}, u32[]{:S(2)}, u32[]{:S(2)}) %all-to-all-start) | async-done | bytes 1572896 | tf_op jit(solution)/shard_map/all_to_all | solution.py:662
  39.0 3.6 %all-to-all-start.1 = ((bf16[8,2,32,1536]{3,2,1,0:T(8,128)(2,1)}), bf16[8,2,32,1536]{3,2,1,0:T(8,128)(2,1)S(1)}, u32[]{:S(2)}, u32[]{:S(2)}) async-start(bf16[8,2,32,1536]{3,2,1,0:T(8,128)(2,1)} %get-tuple-element.38), calls=%async_computation.1 | async-start | bytes 3145728 | tf_op jit(solution)/shard_map/all_to_all | solution.py:662
  42.6 0.0 copy-start.2
  42.6 5.7 %hats.1 = (f32[256,1536]{1,0:T(8,128)}, f32[256,1536]{1,0:T(8,128)}, f32[256,1536]{1,0:T(8,128)}, f32[256,1536]{1,0:T(8,128)}) custom-call(bf16[256,1536]{1,0:T(8,128)(2,1)} %bitcast.22, bf16[256,1536]{1,0:T(8,128)(2,1)} %bitcast.24), custom_call_target="tpu_custom_call" | custom-call | bytes 20664000 | tf_op jit(solution)/shard_map/hats/pallas_call | solution.py:157
  48.3 15.8 %all-to-all-done.1.sg_ref = bf16[8,2,32,1536]{3,2,1,0:T(8,128)(2,1)S(1)} async-done(((bf16[8,2,32,1536]{3,2,1,0:T(8,128)(2,1)}), bf16[8,2,32,1536]{3,2,1,0:T(8,128)(2,1)S(1)}, u32[]{:S(2)}, u32[]{:S(2)}) %all-to-all-start.1) | async-done | bytes 1572896 | tf_op jit(solution)/shard_map/all_to_all | solution.py:662
  64.1 0.0 copy-done.2
  64.1 3.5 %time_forward.1 = bf16[8,32,1536]{2,1,0:T(8,128)(2,1)S(1)} custom-call(s32[6]{0:T(128)S(1)} %copy-done.2, bf16[8,2,32,1536]{3,2,1,0:T(8,128)(2,1)S(1)} %all-to-all-done.qk_ref, bf16[8,2,32,1536]{3,2,1,0:T(8,128)(2,1)S(1)} %all-to-all-done.1.sg_ref), custom_call_target="tpu_custom_call" | custom-call | bytes 18450000 | tf_op jit(solution)/shard_map/time_forward/pallas_call | solution.py:391
  67.7 0.0 copy-start
  67.7 0.9 copy-done
  68.5 4.2 %all-to-all-start.2 = ((bf16[8,32,1536]{2,1,0:T(8,128)(2,1)}), bf16[8,32,1536]{2,1,0:T(8,128)(2,1)}, u32[]{:S(2)}, u32[]{:S(2)}) async-start(bf16[8,32,1536]{2,1,0:T(8,128)(2,1)} %copy-done), calls=%async_computation.2 | async-start | bytes 1572864 | tf_op jit(solution)/shard_map/all_to_all | solution.py:662
  72.8 0.0 all-gather.4.cloned.1.call-start
  72.8 5.8 %time_back.1 = (bf16[8,2,32,1536]{3,2,1,0:T(8,128)(2,1)}, bf16[8,32,1536]{2,1,0:T(8,128)(2,1)S(1)}, f32[8,128]{1,0:T(8,128)S(1)}) custom-call(s32[6]{0:T(128)S(1)} %copy-done.2, bf16[8,2,32,1536]{3,2,1,0:T(8,128)(2,1)S(1)} %all-to-all-done.qk_ref, bf16[8,2,32,1536]{3,2,1,0:T(8,128)(2,1)S(1)} %all-to-all-done.1.sg_ref), custom_call_target="tpu_custom_call" | custom-call | bytes 23985000 | tf_op jit(solution)/shard_map/time_back/pallas_call | solution.py:406
  78.6 0.9 copy-done.1
  79.5 0.6 copy-done.3
  80.1 5.8 %all-to-all-done.2 = bf16[8,32,1536]{2,1,0:T(8,128)(2,1)} async-done(((bf16[8,32,1536]{2,1,0:T(8,128)(2,1)}), bf16[8,32,1536]{2,1,0:T(8,128)(2,1)}, u32[]{:S(2)}, u32[]{:S(2)}) %all-to-all-start.2) | async-done | bytes 786464 | tf_op jit(solution)/shard_map/all_to_all | solution.py:662
  85.9 0.0 all-gather.4.cloned.1.call-update
  85.9 17.5 %all_to_all.30 = bf16[8,32,1536]{2,1,0:T(8,128)(2,1)} all-to-all(bf16[8,32,1536]{2,1,0:T(8,128)(2,1)} %copy-done.1), channel_id=1, replica_groups=mesh['x'=4,'z'=4,'y'=4,'core'=2] {'y','core'}, dimensions={0} | all-to-all | bytes 1572864 | tf_op jit(solution)/shard_map/all_to_all | solution.py:662
  103.4 3.6 %all-to-all-start.4 = ((bf16[8,2,32,1536]{3,2,1,0:T(8,128)(2,1)}), bf16[8,2,32,1536]{3,2,1,0:T(8,128)(2,1)S(1)}, u32[]{:S(2)}, u32[]{:S(2)}) async-start(bf16[8,2,32,1536]{3,2,1,0:T(8,128)(2,1)} %get-tuple-element.57), calls=%async_computation.4 | async-start | bytes 3145728 | tf_op jit(solution)/shard_map/all_to_all | solution.py:662
  107.0 9.2 %space_back.1 = (f32[256,1536]{1,0:T(8,128)}, f32[256,1536]{1,0:T(8,128)}, bf16[256,1536]{1,0:T(8,128)(2,1)}, f32[8,128]{1,0:T(8,128)}) custom-call(f32[8,128]{1,0:T(8,128)} %copy-done.3, f32[1,64]{1,0:T(1,128)} %bitcast.29, f32[1,64]{1,0:T(1,128)} %bitcast.32, f32[256,1536]{1,0:T(8,128)} %get-tuple-element.46.hat_q_ref, ...), custom_call_target="tpu_custom_call" | custom-call | bytes 33210000 | tf_op jit(solution)/shard_map/space_back/pallas_call | solution.py:276
  116.2 0.4 collective-permute-start
  116.6 1.0 collective-permute-done
  117.7 0.7 add.7.refs_0_
  118.4 1.5 collective-permute-start.1
  119.8 2.8 %collective-permute-start.2 = (f32[8,128]{1,0:T(8,128)S(1)}, f32[8,128]{1,0:T(8,128)S(1)}, u32[]{:S(2)}, u32[]{:S(2)}) collective-permute-start(f32[8,128]{1,0:T(8,128)S(1)} %add.7.refs_0_), channel_id=1, source_target_pairs={{0,64},{32,96},{64,0},{96,32},{1,65},{33,97},{65,1},{97,33},{2,66}... | collective-permute-start | bytes 12296 | tf_op jit(solution)/shard_map/ppermute | solution.py:690
  122.6 1.4 collective-permute-start.3
  124.0 0.0 collective-permute-done.1.refs_1_
  124.0 1.0 collective-permute-done.2.refs_2_
  125.0 1.2 collective-permute-done.3.refs_3_
  126.2 1.2 all-gather.4.cloned.1.call-done.mixed_hbm
  127.5 0.0 copy-done.5
  127.5 0.0 copy-done.6
  127.5 0.0 copy-done.7
  127.5 0.0 copy-done.8
  127.5 11.6 %weight_parts.1 = bf16[16,80,512]{2,1,0:T(8,128)(2,1)} custom-call(s32[6]{0:T(128)} %stack.15.counts_ref, bf16[2,192,384]{2,1,0:T(8,128)(2,1)} %constant.16.clone.order_ref, bf16[2048,1536]{1,0:T(8,128)(2,1)} %all-gather.4.cloned.1.call-done.mixed_hbm, bf16[2048,3072]{1,0:T(8,128)(2,1)} %bitcast.18, f32[8,128]{1,0:T(8,128)} %copy-done.5, ...), custom_call_target="tpu_custom_call" | custom-call | bytes 27675000 | tf_op jit(solution)/shard_map/weight_parts/pallas_call | solution.py:575
  139.1 0.0 all-to-all-done.4.late_ref
  139.1 0.0 copy-start.4
  139.1 7.5 %all-to-all-start.5 = ((bf16[16,80,512]{2,1,0:T(8,128)(2,1)}), bf16[16,80,512]{2,1,0:T(8,128)(2,1)S(1)}, u32[]{:S(2)}, u32[]{:S(2)}) async-start(bf16[16,80,512]{2,1,0:T(8,128)(2,1)} %weight_parts.1), calls=%async_computation.5 | async-start | bytes 2621440 | tf_op jit(solution)/shard_map/all_to_all | solution.py:662
  146.6 7.0 %project.1 = bf16[256,3072]{1,0:T(8,128)(2,1)} custom-call(bf16[256,1536]{1,0:T(8,128)(2,1)} %bitcast.9.mixed_ref, bf16[1536,3072]{1,0:T(8,128)(2,1)} %weight_ref.3), custom_call_target="tpu_custom_call" | custom-call | bytes 25830000 | tf_op jit(solution)/shard_map/project/pallas_call | solution.py:503
  153.6 6.9 %norm_back.1 = (bf16[256,1536]{1,0:T(8,128)(2,1)}, bf16[256,1536]{1,0:T(8,128)(2,1)}) custom-call(f32[256,1536]{1,0:T(8,128)} %get-tuple-element.46.hat_q_ref, f32[256,1536]{1,0:T(8,128)} %get-tuple-element.47.hat_k_ref, f32[256,1536]{1,0:T(8,128)} %get-tuple-element.48.inverse_q_ref, f32[256,1536]{1,0:T(8,128)} %get-tuple-element.49.inverse_k_ref, ...), custom_call_target="tpu_custom_call" | custom-call | bytes 25830000 | tf_op jit(solution)/shard_map/norm_back/pallas_call | solution.py:453
  160.6 6.7 %all-to-all-done.5.parts_ref = bf16[16,80,512]{2,1,0:T(8,128)(2,1)S(1)} async-done(((bf16[16,80,512]{2,1,0:T(8,128)(2,1)}), bf16[16,80,512]{2,1,0:T(8,128)(2,1)S(1)}, u32[]{:S(2)}, u32[]{:S(2)}) %all-to-all-start.5) | async-done | bytes 1310752 | tf_op jit(solution)/shard_map/all_to_all | solution.py:662
  167.3 0.9 sum_parts.1
  (8 shorter events, 0.0 us)
Async XLA Ops:
  7.2 78.8 %all-gather.6.cloned.1.call-start = ((), (), s32[]{:S(2)}) async-start(), calls=%async_computation.7 | async-start | bytes 14155776 | tf_op jit(solution)/shard_map/all_gather | solution.py:667
  12.9 26.1 %all-to-all-start = ((bf16[8,2,32,1536]{3,2,1,0:T(8,128)(2,1)}), bf16[8,2,32,1536]{3,2,1,0:T(8,128)(2,1)S(1)}, u32[]{:S(2)}, u32[]{:S(2)}) async-start(bf16[8,2,32,1536]{3,2,1,0:T(8,128)(2,1)} %norm.1.qk_ref), calls=%async_computation | async-start | bytes 3145728 | tf_op jit(solution)/shard_map/all_to_all | solution.py:662
  39.0 25.1 %all-to-all-start.1 = ((bf16[8,2,32,1536]{3,2,1,0:T(8,128)(2,1)}), bf16[8,2,32,1536]{3,2,1,0:T(8,128)(2,1)S(1)}, u32[]{:S(2)}, u32[]{:S(2)}) async-start(bf16[8,2,32,1536]{3,2,1,0:T(8,128)(2,1)} %get-tuple-element.38), calls=%async_computation.1 | async-start | bytes 3145728 | tf_op jit(solution)/shard_map/all_to_all | solution.py:662
  42.6 21.5 %copy-start.2 = (s32[6]{0:T(128)S(1)}, s32[6]{0:T(128)}, u32[]{:S(2)}) copy-start(s32[6]{0:T(128)} %stack.15.counts_ref) | copy-start | bytes 76
  67.7 0.9 copy-start
  68.5 17.4 %all-to-all-start.2 = ((bf16[8,32,1536]{2,1,0:T(8,128)(2,1)}), bf16[8,32,1536]{2,1,0:T(8,128)(2,1)}, u32[]{:S(2)}, u32[]{:S(2)}) async-start(bf16[8,32,1536]{2,1,0:T(8,128)(2,1)} %copy-done), calls=%async_computation.2 | async-start | bytes 1572864 | tf_op jit(solution)/shard_map/all_to_all | solution.py:662
  72.8 54.7 %all-gather.4.cloned.1.call-start = ((), (), s32[]{:S(2)}) async-start(), calls=%async_computation.6 | async-start | bytes 7077888 | tf_op jit(solution)/shard_map/all_gather | solution.py:679
  78.6 0.9 copy-start.1
  79.5 0.6 copy-start.3
  103.4 35.7 %all-to-all-start.4 = ((bf16[8,2,32,1536]{3,2,1,0:T(8,128)(2,1)}), bf16[8,2,32,1536]{3,2,1,0:T(8,128)(2,1)S(1)}, u32[]{:S(2)}, u32[]{:S(2)}) async-start(bf16[8,2,32,1536]{3,2,1,0:T(8,128)(2,1)} %get-tuple-element.57), calls=%async_computation.4 | async-start | bytes 3145728 | tf_op jit(solution)/shard_map/all_to_all | solution.py:662
  116.2 1.5 collective-permute-start
  118.4 9.1 %copy-start.5 = (f32[8,128]{1,0:T(8,128)}, f32[8,128]{1,0:T(8,128)S(1)}, u32[]{:S(2)}) copy-start(f32[8,128]{1,0:T(8,128)S(1)} %add.7.refs_0_) | copy-start | bytes 12292
  118.4 5.6 %collective-permute-start.1 = (f32[8,128]{1,0:T(8,128)S(1)}, f32[8,128]{1,0:T(8,128)S(1)}, u32[]{:S(2)}, u32[]{:S(2)}) collective-permute-start(f32[8,128]{1,0:T(8,128)S(1)} %add.7.refs_0_), channel_id=1, source_target_pairs={{0,32},{32,64},{64,96},{96,0},{1,33},{33,65},{65,97},{97,1},{2,34}... | collective-permute-start | bytes 12296 | tf_op jit(solution)/shard_map/ppermute | solution.py:690
  119.8 5.2 %collective-permute-start.2 = (f32[8,128]{1,0:T(8,128)S(1)}, f32[8,128]{1,0:T(8,128)S(1)}, u32[]{:S(2)}, u32[]{:S(2)}) collective-permute-start(f32[8,128]{1,0:T(8,128)S(1)} %add.7.refs_0_), channel_id=1, source_target_pairs={{0,64},{32,96},{64,0},{96,32},{1,65},{33,97},{65,1},{97,33},{2,66}... | collective-permute-start | bytes 12296 | tf_op jit(solution)/shard_map/ppermute | solution.py:690
  122.6 3.6 %collective-permute-start.3 = (f32[8,128]{1,0:T(8,128)S(1)}, f32[8,128]{1,0:T(8,128)S(1)}, u32[]{:S(2)}, u32[]{:S(2)}) collective-permute-start(f32[8,128]{1,0:T(8,128)S(1)} %add.7.refs_0_), channel_id=1, source_target_pairs={{0,96},{32,0},{64,32},{96,64},{1,97},{33,1},{65,33},{97,65},{2,98}... | collective-permute-start | bytes 12296 | tf_op jit(solution)/shard_map/ppermute | solution.py:690
  124.0 3.5 %copy-start.6 = (f32[8,128]{1,0:T(8,128)}, f32[8,128]{1,0:T(8,128)S(1)}, u32[]{:S(2)}) copy-start(f32[8,128]{1,0:T(8,128)S(1)} %collective-permute-done.1.refs_1_) | copy-start | bytes 12292
  125.0 2.5 %copy-start.7 = (f32[8,128]{1,0:T(8,128)}, f32[8,128]{1,0:T(8,128)S(1)}, u32[]{:S(2)}) copy-start(f32[8,128]{1,0:T(8,128)S(1)} %collective-permute-done.2.refs_2_) | copy-start | bytes 12292
  126.2 1.3 copy-start.8
  139.1 14.5 %copy-start.4 = (bf16[8,2,32,1536]{3,2,1,0:T(8,128)(2,1)}, bf16[8,2,32,1536]{3,2,1,0:T(8,128)(2,1)S(1)}, u32[]{:S(2)}) copy-start(bf16[8,2,32,1536]{3,2,1,0:T(8,128)(2,1)S(1)} %all-to-all-done.4.late_ref) | copy-start | bytes 4718596
  139.1 28.2 %all-to-all-start.5 = ((bf16[16,80,512]{2,1,0:T(8,128)(2,1)}), bf16[16,80,512]{2,1,0:T(8,128)(2,1)S(1)}, u32[]{:S(2)}, u32[]{:S(2)}) async-start(bf16[16,80,512]{2,1,0:T(8,128)(2,1)} %weight_parts.1), calls=%async_computation.5 | async-start | bytes 2621440 | tf_op jit(solution)/shard_map/all_to_all | solution.py:662
Sparse Core Ops, SparseCore 0:
  9.7 69.7 all-gather.5
  86.1 41.3 all-gather.3

commit v6 on v4

--- a/solution.py
+++ b/solution.py
@@ -22,6 +22,8 @@
 SCALE = HD**-0.5
 PARAMS = pltpu.CompilerParams(vmem_limit_bytes=56 * 1024 * 1024)
 SMALL = pltpu.CompilerParams(vmem_limit_bytes=16 * 1024 * 1024)
+MEDIUM = pltpu.CompilerParams(vmem_limit_bytes=24 * 1024 * 1024)
+LARGE = pltpu.CompilerParams(vmem_limit_bytes=46 * 1024 * 1024)
 
 
 def cost(microseconds):
@@ -294,7 +296,7 @@
             jax.ShapeDtypeStruct((CELLS, inner), BF),
             jax.ShapeDtypeStruct((8, LANES), F32),
         ],
-        compiler_params=PARAMS,
+        compiler_params=LARGE,
         cost_estimate=cost(9),
         name="space_back",
     )(late_sums, gain_query, gain_key, *hats, normed, values, upstream, chances)
@@ -559,7 +561,7 @@
                     ].astype(BF)
 
 
-def weight_parts(place, order, mixed, cotangents, gain_sums, shares):
+def weight_parts(counts, order, mixed, cotangents, gain_sums, shares):
     tokens, width = cotangents.shape
     _, features, wide = order.shape
     block = width // PIECES
@@ -572,8 +574,8 @@
             num_scalar_prefetch=1,
             grid=(STEPS,),
             in_specs=[
-                pl.BlockSpec((1, features, wide), lambda n, place: (place[1], 0, 0)),
-                pl.BlockSpec((tokens, wide), lambda n, place: (0, place[0])),
+                pl.BlockSpec((1, features, wide), lambda n, place: (place[5], 0, 0)),
+                pl.BlockSpec((tokens, wide), lambda n, place: (0, place[4])),
                 pl.BlockSpec((tokens, columns), lambda n, place: (0, n)),
             ]
             + [gain] * len(gain_sums),
@@ -584,10 +586,10 @@
             ],
         ),
         out_shape=jax.ShapeDtypeStruct((shares, rows, block), BF),
-        compiler_params=PARAMS,
+        compiler_params=MEDIUM,
         cost_estimate=cost(9.5),
         name="weight_parts",
-    )(place, order, mixed, cotangents, *gain_sums)
+    )(counts, order, mixed, cotangents, *gain_sums)
 
 
 def sum_kernel(parts_ref, out_ref, gain_q_ref, gain_k_ref):
@@ -649,7 +651,8 @@
     shares = lax.axis_size("z") * lax.axis_size("y")
     inner = out_weight.shape[0]
     rank = lax.axis_index(seq).astype(jnp.int32)
-    counts = jnp.stack([frame_counts[0], heights[0], widths[0], rank])
+    place = [lax.axis_index("x").astype(jnp.int32), lax.axis_index("core").astype(jnp.int32)]
+    counts = jnp.stack([frame_counts[0], heights[0], widths[0], rank, *place])
     gains = gain_query.reshape(1, HD), gain_key.reshape(1, HD)
     query_rows, key_rows, value_rows = queries[0, 0], keys_proj[0, 0], values_proj[0, 0]
     cot_rows = cotangent[0, 0]
@@ -672,7 +675,6 @@
     mixed_cells = time_forward(counts, normed_cells, arrived)
     mixed = exchange(mixed_cells, seq).reshape(CELLS, inner)
     late_cells, dspatial_cells, late_gains = time_back(counts, normed_cells, arrived)
-    place = jnp.stack([lax.axis_index("x"), lax.axis_index("core")]).astype(jnp.int32)
     first = (cotangents, dspatial_cells)
     gathered = lax.all_gather(after(mixed, first), group, axis=0, tiled=True)
     dspatial = exchange(after(dspatial_cells, mixed), seq).reshape(CELLS, inner)
@@ -690,7 +692,7 @@
     ]
     grad_queries, grad_keys = norm_back(hats, *gains, dq, dk, late)
     order = feature_order(inner, planes, cores, shares)
-    parts = weight_parts(place, order, gathered, cotangents, gain_sums, shares)
+    parts = weight_parts(counts, order, gathered, cotangents, gain_sums, shares)
     parts = exchange(after(parts, late), sums)
     own = order.shape[1] // shares
     grad_weight, grad_gain_query, grad_gain_key = sum_parts(parts, own)

time: 174 us -> 180 us (1.034)
  local copies, waits for them, and re-layouts: 2.37 us -> 15.5 us
  Pallas kernels: 69.2 us -> 64.1 us
  waiting for transfers between devices: 36.3 us -> 34.3 us
  other arithmetic: 1.93 us -> 0.01 us
    unnamed x18 -> x30, local copies, waits for them, and re-layouts: 2.37 us -> 14.9 us
    pallas_call x1, Pallas kernels: 9.58 us -> 6.55 us  [weight_parts(): pl.pallas_call(weight_kernel, grid_spec=pltpu.PrefetchScalarGridSpec(num_...]
  transfers between devices with their start and end apart: 11 -> 11, of which waited for: 8 -> 7; matrix products, arithmetic and copies ran while one was open for 1% -> 0% of each run, Pallas kernels for 40% -> 35%
where the time goes in v6:
time: 180 us; the launch traced here: 179 us
  Pallas kernels  64.1 us (36%)
  waiting for transfers between devices  34.3 us (19%)
  starting transfers between devices  31.3 us (17%)
  blocking collectives  17.5 us (10%)
  between operations  16.1 us (9%)
  local copies, waits for them, and re-layouts  15.5 us (9%)
    all_to_all x5, waiting for transfers between devices, exchange(): return lax.all_to_all(tensor, axes, split_axis=0, concat_axis=0, tiled=True)  30.5 us
    all_to_all x5, starting transfers between devices, exchange(): return lax.all_to_all(tensor, axes, split_axis=0, concat_axis=0, tiled=True)  25.2 us
    all_to_all x1, blocking collectives, exchange(): return lax.all_to_all(tensor, axes, split_axis=0, concat_axis=0, tiled=True)  17.5 us
    unnamed x30, local copies, waits for them, and re-layouts  14.9 us
    pallas_call x1, Pallas kernels, grad_mixed_of(): pl.pallas_call(grad_mixed_kernel, grid=(inner // WIDE,), in_specs=[pl.Blo...  8.65 us
    pallas_call x1, Pallas kernels, space_back(): pl.pallas_call(space_back_kernel, grid=(inner // WIDE,), in_specs=[pl.Blo...  7.76 us
    pallas_call x1, Pallas kernels, space_forward(): pl.pallas_call(space_kernel, grid=(inner // WIDE,), in_specs=[SMEM, pl.Bl...  7 us
    pallas_call x1, Pallas kernels, project(): pl.pallas_call(project_kernel, grid=(4,), in_specs=[pl.BlockSpec((CELLS,...  6.98 us
  transfers between devices with their start and end apart: 11, of which 7 were waited for; matrix products, arithmetic and copies ran while one was open for 0% of the time, Pallas kernels for 35%

profile of v6, /device:TPU:0, one launch (start us, length us, event | category | flops | bytes accessed | tf_op | source)
XLA Modules:
  0.0 178.8 jit_solution(6168438588653019135)
XLA Ops:
  7.2 0.0 all-gather.6.cloned.1.call-start
  7.2 0.7 all-gather.6.cloned.1.call-update
  7.9 5.0 %norm.1.qk_ref = bf16[8,2,32,1536]{3,2,1,0:T(8,128)(2,1)} custom-call(bf16[256,1536]{1,0:T(8,128)(2,1)} %bitcast.29, bf16[256,1536]{1,0:T(8,128)(2,1)} %bitcast.31, f32[1,64]{1,0:T(1,128)} %bitcast.22, f32[1,64]{1,0:T(1,128)} %bitcast.25), custom_call_target="tpu_custom_call" | custom-call | bytes 18450000 | tf_op jit(solution)/shard_map/norm/pallas_call | solution.py:134
  12.9 4.6 %all-to-all-start = ((bf16[8,2,32,1536]{3,2,1,0:T(8,128)(2,1)}), bf16[8,2,32,1536]{3,2,1,0:T(8,128)(2,1)S(1)}, u32[]{:S(2)}, u32[]{:S(2)}) async-start(bf16[8,2,32,1536]{3,2,1,0:T(8,128)(2,1)} %norm.1.qk_ref), calls=%async_computation | async-start | bytes 3145728 | tf_op jit(solution)/shard_map/all_to_all | solution.py:662
  19.4 8.7 %grad_mixed.1.gm_ref = bf16[256,1536]{1,0:T(8,128)(2,1)} custom-call(bf16[256,3072]{1,0:T(8,128)(2,1)} %bitcast.28, bf16[1536,3072]{1,0:T(8,128)(2,1)} %weight_ref.3), custom_call_target="tpu_custom_call" | custom-call | bytes 32103000 | tf_op jit(solution)/shard_map/grad_mixed/pallas_call | solution.py:483
  28.0 0.6 stack.15.counts_ref.place_ref
  28.6 7.0 %space_forward.1 = (bf16[8,2,32,1536]{3,2,1,0:T(8,128)(2,1)}, f32[12,512,256]{2,1,0:T(8,128)}) custom-call(s32[6]{0:T(128)} %stack.15.counts_ref.place_ref, bf16[8,2,32,1536]{3,2,1,0:T(8,128)(2,1)} %norm.1.qk_ref, bf16[256,1536]{1,0:T(8,128)(2,1)} %bitcast.20, bf16[256,1536]{1,0:T(8,128)(2,1)} %grad_mixed.1.gm_ref), custom_call_target="tpu_custom_call" | custom-call | bytes 25830000 | tf_op jit(solution)/shard_map/space_forward/pallas_call | solution.py:198
  35.6 3.4 %all-to-all-done.qk_ref = bf16[8,2,32,1536]{3,2,1,0:T(8,128)(2,1)S(1)} async-done(((bf16[8,2,32,1536]{3,2,1,0:T(8,128)(2,1)}), bf16[8,2,32,1536]{3,2,1,0:T(8,128)(2,1)S(1)}, u32[]{:S(2)}, u32[]{:S(2)}) %all-to-all-start) | async-done | bytes 1572896 | tf_op jit(solution)/shard_map/all_to_all | solution.py:662
  39.0 3.6 %all-to-all-start.1 = ((bf16[8,2,32,1536]{3,2,1,0:T(8,128)(2,1)}), bf16[8,2,32,1536]{3,2,1,0:T(8,128)(2,1)S(1)}, u32[]{:S(2)}, u32[]{:S(2)}) async-start(bf16[8,2,32,1536]{3,2,1,0:T(8,128)(2,1)} %get-tuple-element.38), calls=%async_computation.1 | async-start | bytes 3145728 | tf_op jit(solution)/shard_map/all_to_all | solution.py:662
  42.6 0.0 copy-start.12
  42.6 5.7 %hats.1 = (f32[256,1536]{1,0:T(8,128)}, f32[256,1536]{1,0:T(8,128)}, f32[256,1536]{1,0:T(8,128)}, f32[256,1536]{1,0:T(8,128)}) custom-call(bf16[256,1536]{1,0:T(8,128)(2,1)} %bitcast.30, bf16[256,1536]{1,0:T(8,128)(2,1)} %bitcast.32), custom_call_target="tpu_custom_call" | custom-call | bytes 20664000 | tf_op jit(solution)/shard_map/hats/pallas_call | solution.py:159
  48.3 15.8 %all-to-all-done.1.sg_ref = bf16[8,2,32,1536]{3,2,1,0:T(8,128)(2,1)S(1)} async-done(((bf16[8,2,32,1536]{3,2,1,0:T(8,128)(2,1)}), bf16[8,2,32,1536]{3,2,1,0:T(8,128)(2,1)S(1)}, u32[]{:S(2)}, u32[]{:S(2)}) %all-to-all-start.1) | async-done | bytes 1572896 | tf_op jit(solution)/shard_map/all_to_all | solution.py:662
  64.1 0.0 copy-done.12
  64.1 3.5 %time_forward.1 = bf16[8,32,1536]{2,1,0:T(8,128)(2,1)S(1)} custom-call(s32[6]{0:T(128)S(1)} %copy-done.12, bf16[8,2,32,1536]{3,2,1,0:T(8,128)(2,1)S(1)} %all-to-all-done.qk_ref, bf16[8,2,32,1536]{3,2,1,0:T(8,128)(2,1)S(1)} %all-to-all-done.1.sg_ref), custom_call_target="tpu_custom_call" | custom-call | bytes 18450000 | tf_op jit(solution)/shard_map/time_forward/pallas_call | solution.py:393
  67.7 0.0 copy-start.5
  67.7 0.9 copy-done.5
  68.5 4.2 %all-to-all-start.2 = ((bf16[8,32,1536]{2,1,0:T(8,128)(2,1)}), bf16[8,32,1536]{2,1,0:T(8,128)(2,1)}, u32[]{:S(2)}, u32[]{:S(2)}) async-start(bf16[8,32,1536]{2,1,0:T(8,128)(2,1)} %copy-done.5), calls=%async_computation.2 | async-start | bytes 1572864 | tf_op jit(solution)/shard_map/all_to_all | solution.py:662
  72.8 0.0 all-gather.4.cloned.1.call-start
  72.8 5.2 %time_back.1 = (bf16[8,2,32,1536]{3,2,1,0:T(8,128)(2,1)S(1)}, bf16[8,32,1536]{2,1,0:T(8,128)(2,1)S(1)}, f32[8,128]{1,0:T(8,128)S(1)}) custom-call(s32[6]{0:T(128)S(1)} %copy-done.12, bf16[8,2,32,1536]{3,2,1,0:T(8,128)(2,1)S(1)} %all-to-all-done.qk_ref, bf16[8,2,32,1536]{3,2,1,0:T(8,128)(2,1)S(1)} %all-to-all-done.1.sg_ref), custom_call_target="tpu_custom_call" | custom-call | bytes 23985000 | tf_op jit(solution)/shard_map/time_back/pallas_call | solution.py:408
  78.0 1.1 copy-done.7
  79.2 0.9 copy-done.10
  80.1 5.9 %all-to-all-done.2 = bf16[8,32,1536]{2,1,0:T(8,128)(2,1)} async-done(((bf16[8,32,1536]{2,1,0:T(8,128)(2,1)}), bf16[8,32,1536]{2,1,0:T(8,128)(2,1)}, u32[]{:S(2)}, u32[]{:S(2)}) %all-to-all-start.2) | async-done | bytes 786464 | tf_op jit(solution)/shard_map/all_to_all | solution.py:662
  85.9 0.0 all-gather.4.cloned.1.call-update
  85.9 17.5 %all_to_all.30 = bf16[8,32,1536]{2,1,0:T(8,128)(2,1)} all-to-all(bf16[8,32,1536]{2,1,0:T(8,128)(2,1)} %copy-done.10), channel_id=1, replica_groups=mesh['x'=4,'z'=4,'y'=4,'core'=2] {'y','core'}, dimensions={0} | all-to-all | bytes 1572864 | tf_op jit(solution)/shard_map/all_to_all | solution.py:662
  103.4 4.6 %all-to-all-start.4 = ((bf16[8,2,32,1536]{3,2,1,0:T(8,128)(2,1)}), bf16[8,2,32,1536]{3,2,1,0:T(8,128)(2,1)}, u32[]{:S(2)}, u32[]{:S(2)}) async-start(bf16[8,2,32,1536]{3,2,1,0:T(8,128)(2,1)} %copy-done.7), calls=%async_computation.4 | async-start | bytes 3145728 | tf_op jit(solution)/shard_map/all_to_all | solution.py:662
  108.0 1.1 copy-done.4
  109.2 1.2 copy-done.6
  110.4 7.8 %space_back.1 = (f32[256,1536]{1,0:T(8,128)S(1)}, f32[256,1536]{1,0:T(8,128)S(1)}, bf16[256,1536]{1,0:T(8,128)(2,1)}, f32[8,128]{1,0:T(8,128)S(1)}) custom-call(f32[8,128]{1,0:T(8,128)S(1)} %get-tuple-element.50.late_ref, f32[1,64]{1,0:T(1,128)S(1)} %bitcast.24, f32[1,64]{1,0:T(1,128)S(1)} %bitcast.27, f32[256,1536]{1,0:T(8,128)S(1)} %copy-done.2, ...), custom_call_target="tpu_custom_call" | custom-call | bytes 33210000 | tf_op jit(solution)/shard_map/space_back/pallas_call | solution.py:278
  118.1 1.1 copy-done.8
  119.3 1.2 copy-done.9
  120.4 0.5 collective-permute-start
  120.9 0.8 collective-permute-done
  121.8 1.4 collective-permute-start.1
  123.2 2.8 %collective-permute-start.2 = (f32[8,128]{1,0:T(8,128)S(1)}, f32[8,128]{1,0:T(8,128)S(1)}, u32[]{:S(2)}, u32[]{:S(2)}) collective-permute-start(f32[8,128]{1,0:T(8,128)S(1)} %add.7.refs_0_), channel_id=1, source_target_pairs={{0,64},{32,96},{64,0},{96,32},{1,65},{33,97},{65,1},{97,33},{2,66}... | collective-permute-start | bytes 12296 | tf_op jit(solution)/shard_map/ppermute | solution.py:690
  125.9 1.4 collective-permute-start.3
  127.3 0.0 collective-permute-done.1.refs_1_
  127.3 0.9 collective-permute-done.2.refs_2_
  128.3 1.3 collective-permute-done.3.refs_3_
  129.6 0.0 copy-done.11
  129.6 4.6 %copy-done = bf16[1,1,2048,3072]{3,2,1,0:T(8,128)(2,1)S(1)} copy-done((bf16[1,1,2048,3072]{3,2,1,0:T(8,128)(2,1)S(1)}, bf16[1,1,2048,3072]{3,2,1,0:T(8,128)(2,1)}, u32[]{:S(2)}) %copy-start) | copy-done | bytes 12582936
  134.1 2.8 %copy-done.1 = bf16[2048,1536]{1,0:T(8,128)(2,1)S(1)} copy-done((bf16[2048,1536]{1,0:T(8,128)(2,1)S(1)}, bf16[2048,1536]{1,0:T(8,128)(2,1)}, u32[]{:S(2)}) %copy-start.1) | copy-done | bytes 6291480
  136.9 6.5 %weight_parts.1 = bf16[16,80,512]{2,1,0:T(8,128)(2,1)} custom-call(s32[6]{0:T(128)S(1)} %copy-done.12, bf16[2,192,384]{2,1,0:T(8,128)(2,1)S(1)} %copy-done.11, bf16[2048,1536]{1,0:T(8,128)(2,1)S(1)} %copy-done.1, bf16[2048,3072]{1,0:T(8,128)(2,1)S(1)} %bitcast.18, f32[8,128]{1,0:T(8,128)S(1)} %add.7.refs_0_, f32[8,128]{1,0:T(8,128)S(1)} %collective-permute-done.1.refs_1_, ...), custom_call_target="tpu_custom_call" | custom-call | bytes 35055000 | tf_op jit(solution)/shard_map/weight_parts/pallas_call | solution.py:571
  143.5 0.0 all-to-all-done.4.late_ref
  143.5 8.2 %all-to-all-start.5 = ((bf16[16,80,512]{2,1,0:T(8,128)(2,1)}), bf16[16,80,512]{2,1,0:T(8,128)(2,1)S(1)}, u32[]{:S(2)}, u32[]{:S(2)}) async-start(bf16[16,80,512]{2,1,0:T(8,128)(2,1)} %weight_parts.1), calls=%async_computation.5 | async-start | bytes 2621440 | tf_op jit(solution)/shard_map/all_to_all | solution.py:662
  151.7 7.0 %project.1 = bf16[256,3072]{1,0:T(8,128)(2,1)} custom-call(bf16[256,1536]{1,0:T(8,128)(2,1)} %bitcast.9.mixed_ref, bf16[1536,3072]{1,0:T(8,128)(2,1)} %weight_ref.3), custom_call_target="tpu_custom_call" | custom-call | bytes 25830000 | tf_op jit(solution)/shard_map/project/pallas_call | solution.py:505
  158.7 6.9 %norm_back.1 = (bf16[256,1536]{1,0:T(8,128)(2,1)}, bf16[256,1536]{1,0:T(8,128)(2,1)}) custom-call(f32[256,1536]{1,0:T(8,128)} %get-tuple-element.46.hat_q_ref, f32[256,1536]{1,0:T(8,128)} %get-tuple-element.47.hat_k_ref, f32[256,1536]{1,0:T(8,128)} %get-tuple-element.48.inverse_q_ref, f32[256,1536]{1,0:T(8,128)} %get-tuple-element.49.inverse_k_ref, ...), custom_call_target="tpu_custom_call" | custom-call | bytes 25830000 | tf_op jit(solution)/shard_map/norm_back/pallas_call | solution.py:455
  165.6 5.5 %all-to-all-done.5.parts_ref = bf16[16,80,512]{2,1,0:T(8,128)(2,1)S(1)} async-done(((bf16[16,80,512]{2,1,0:T(8,128)(2,1)}), bf16[16,80,512]{2,1,0:T(8,128)(2,1)S(1)}, u32[]{:S(2)}, u32[]{:S(2)}) %all-to-all-start.5) | async-done | bytes 1310752 | tf_op jit(solution)/shard_map/all_to_all | solution.py:662
  171.1 0.9 sum_parts.1
  (20 shorter events, 0.0 us)
Async XLA Ops:
  7.2 78.8 %all-gather.6.cloned.1.call-start = ((), (), s32[]{:S(2)}) async-start(), calls=%async_computation.7 | async-start | bytes 14155776 | tf_op jit(solution)/shard_map/all_gather | solution.py:667
  12.9 26.1 %all-to-all-start = ((bf16[8,2,32,1536]{3,2,1,0:T(8,128)(2,1)}), bf16[8,2,32,1536]{3,2,1,0:T(8,128)(2,1)S(1)}, u32[]{:S(2)}, u32[]{:S(2)}) async-start(bf16[8,2,32,1536]{3,2,1,0:T(8,128)(2,1)} %norm.1.qk_ref), calls=%async_computation | async-start | bytes 3145728 | tf_op jit(solution)/shard_map/all_to_all | solution.py:662
  39.0 25.1 %all-to-all-start.1 = ((bf16[8,2,32,1536]{3,2,1,0:T(8,128)(2,1)}), bf16[8,2,32,1536]{3,2,1,0:T(8,128)(2,1)S(1)}, u32[]{:S(2)}, u32[]{:S(2)}) async-start(bf16[8,2,32,1536]{3,2,1,0:T(8,128)(2,1)} %get-tuple-element.38), calls=%async_computation.1 | async-start | bytes 3145728 | tf_op jit(solution)/shard_map/all_to_all | solution.py:662
  42.6 21.5 %copy-start.12 = (s32[6]{0:T(128)S(1)}, s32[6]{0:T(128)}, u32[]{:S(2)}) copy-start(s32[6]{0:T(128)} %stack.15.counts_ref.place_ref) | copy-start | bytes 76
  67.7 0.9 copy-start.5
  68.5 17.4 %all-to-all-start.2 = ((bf16[8,32,1536]{2,1,0:T(8,128)(2,1)}), bf16[8,32,1536]{2,1,0:T(8,128)(2,1)}, u32[]{:S(2)}, u32[]{:S(2)}) async-start(bf16[8,32,1536]{2,1,0:T(8,128)(2,1)} %copy-done.5), calls=%async_computation.2 | async-start | bytes 1572864 | tf_op jit(solution)/shard_map/all_to_all | solution.py:662
  72.8 56.8 %all-gather.4.cloned.1.call-start = ((), (), s32[]{:S(2)}) async-start(), calls=%async_computation.6 | async-start | bytes 7077888 | tf_op jit(solution)/shard_map/all_gather | solution.py:679
  78.0 1.1 copy-start.7
  79.2 0.9 copy-start.10
  103.4 4.6 %copy-start.2 = (f32[256,1536]{1,0:T(8,128)S(1)}, f32[256,1536]{1,0:T(8,128)}, u32[]{:S(2)}) copy-start(f32[256,1536]{1,0:T(8,128)} %get-tuple-element.46.hat_q_ref) | copy-start | bytes 4718596
  103.4 4.6 %copy-start.3 = (f32[256,1536]{1,0:T(8,128)S(1)}, f32[256,1536]{1,0:T(8,128)}, u32[]{:S(2)}) copy-start(f32[256,1536]{1,0:T(8,128)} %get-tuple-element.47.hat_k_ref) | copy-start | bytes 4718596
  103.4 4.6 %copy-start.13 = (f32[64]{0:T(128)S(1)}, f32[64]{0:T(128)}, u32[]{:S(2)}) copy-start(f32[64]{0:T(128)} %param.14) | copy-start | bytes 772
  103.4 4.6 %copy-start.14 = (f32[64]{0:T(128)S(1)}, f32[64]{0:T(128)}, u32[]{:S(2)}) copy-start(f32[64]{0:T(128)} %param.15) | copy-start | bytes 772
  103.4 40.1 %all-to-all-start.4 = ((bf16[8,2,32,1536]{3,2,1,0:T(8,128)(2,1)}), bf16[8,2,32,1536]{3,2,1,0:T(8,128)(2,1)}, u32[]{:S(2)}, u32[]{:S(2)}) async-start(bf16[8,2,32,1536]{3,2,1,0:T(8,128)(2,1)} %copy-done.7), calls=%async_computation.4 | async-start | bytes 3145728 | tf_op jit(solution)/shard_map/all_to_all | solution.py:662
  108.0 1.1 copy-start.4
  109.2 1.2 copy-start.6
  110.4 19.2 %copy-start.11 = (bf16[2,192,384]{2,1,0:T(8,128)(2,1)S(1)}, bf16[2,192,384]{2,1,0:T(8,128)(2,1)}, u32[]{:S(2)}) copy-start(bf16[2,192,384]{2,1,0:T(8,128)(2,1)} %constant.16.clone.order_ref) | copy-start | bytes 884740
  118.1 1.1 copy-start.8
  119.3 1.2 copy-start.9
  120.4 1.3 collective-permute-start
  121.8 5.6 %collective-permute-start.1 = (f32[8,128]{1,0:T(8,128)S(1)}, f32[8,128]{1,0:T(8,128)S(1)}, u32[]{:S(2)}, u32[]{:S(2)}) collective-permute-start(f32[8,128]{1,0:T(8,128)S(1)} %add.7.refs_0_), channel_id=1, source_target_pairs={{0,32},{32,64},{64,96},{96,0},{1,33},{33,65},{65,97},{97,1},{2,34}... | collective-permute-start | bytes 12296 | tf_op jit(solution)/shard_map/ppermute | solution.py:690
  123.2 5.1 %collective-permute-start.2 = (f32[8,128]{1,0:T(8,128)S(1)}, f32[8,128]{1,0:T(8,128)S(1)}, u32[]{:S(2)}, u32[]{:S(2)}) collective-permute-start(f32[8,128]{1,0:T(8,128)S(1)} %add.7.refs_0_), channel_id=1, source_target_pairs={{0,64},{32,96},{64,0},{96,32},{1,65},{33,97},{65,1},{97,33},{2,66}... | collective-permute-start | bytes 12296 | tf_op jit(solution)/shard_map/ppermute | solution.py:690
  125.9 3.6 %collective-permute-start.3 = (f32[8,128]{1,0:T(8,128)S(1)}, f32[8,128]{1,0:T(8,128)S(1)}, u32[]{:S(2)}, u32[]{:S(2)}) collective-permute-start(f32[8,128]{1,0:T(8,128)S(1)} %add.7.refs_0_), channel_id=1, source_target_pairs={{0,96},{32,0},{64,32},{96,64},{1,97},{33,1},{65,33},{97,65},{2,98}... | collective-permute-start | bytes 12296 | tf_op jit(solution)/shard_map/ppermute | solution.py:690
  129.6 4.6 %copy-start = (bf16[1,1,2048,3072]{3,2,1,0:T(8,128)(2,1)S(1)}, bf16[1,1,2048,3072]{3,2,1,0:T(8,128)(2,1)}, u32[]{:S(2)}) copy-start(bf16[1,1,2048,3072]{3,2,1,0:T(8,128)(2,1)} %all-gather.6.cloned.1.call-done) | copy-start | bytes 37748740
  134.1 2.8 %copy-start.1 = (bf16[2048,1536]{1,0:T(8,128)(2,1)S(1)}, bf16[2048,1536]{1,0:T(8,128)(2,1)}, u32[]{:S(2)}) copy-start(bf16[2048,1536]{1,0:T(8,128)(2,1)} %all-gather.4.cloned.1.call-done.mixed_ref) | copy-start | bytes 18874372
  143.5 27.6 %all-to-all-start.5 = ((bf16[16,80,512]{2,1,0:T(8,128)(2,1)}), bf16[16,80,512]{2,1,0:T(8,128)(2,1)S(1)}, u32[]{:S(2)}, u32[]{:S(2)}) async-start(bf16[16,80,512]{2,1,0:T(8,128)(2,1)} %weight_parts.1), calls=%async_computation.5 | async-start | bytes 2621440 | tf_op jit(solution)/shard_map/all_to_all | solution.py:662
Sparse Core Ops, SparseCore 0:
  9.7 69.7 all-gather.5
  86.1 41.1 all-gather.3

commit v7 on v6

--- a/solution.py
+++ b/solution.py
@@ -22,8 +22,6 @@
 SCALE = HD**-0.5
 PARAMS = pltpu.CompilerParams(vmem_limit_bytes=56 * 1024 * 1024)
 SMALL = pltpu.CompilerParams(vmem_limit_bytes=16 * 1024 * 1024)
-MEDIUM = pltpu.CompilerParams(vmem_limit_bytes=24 * 1024 * 1024)
-LARGE = pltpu.CompilerParams(vmem_limit_bytes=46 * 1024 * 1024)
 
 
 def cost(microseconds):
@@ -296,7 +294,7 @@
             jax.ShapeDtypeStruct((CELLS, inner), BF),
             jax.ShapeDtypeStruct((8, LANES), F32),
         ],
-        compiler_params=LARGE,
+        compiler_params=PARAMS,
         cost_estimate=cost(9),
         name="space_back",
     )(late_sums, gain_query, gain_key, *hats, normed, values, upstream, chances)
@@ -586,7 +584,7 @@
             ],
         ),
         out_shape=jax.ShapeDtypeStruct((shares, rows, block), BF),
-        compiler_params=MEDIUM,
+        compiler_params=PARAMS,
         cost_estimate=cost(9.5),
         name="weight_parts",
     )(counts, order, mixed, cotangents, *gain_sums)
@@ -620,7 +618,8 @@
     )(parts)
 
 
-def feature_order(inner, planes, cores, shares):
+def feature_order(inner, planes, cores, shares, heights):
+    depths = shares // heights
     wide = inner // planes
     features = wide // cores
     own = features // shares
@@ -628,6 +627,8 @@
     for core in range(cores):
         for feature in range(features):
             share, row = divmod(feature, own)
+            y, z = divmod(share, depths)
+            share = z * heights + y
             order[core, feature, own * (cores * share + core) + row] = 1.0
     return jnp.asarray(order, BF)
 
@@ -646,7 +647,7 @@
 ):
     seq = ("y", "core")
     group = ("x", "core")
-    sums = ("z", "y")
+    sums = ("y", "z")
     planes, cores = lax.axis_size("x"), lax.axis_size("core")
     shares = lax.axis_size("z") * lax.axis_size("y")
     inner = out_weight.shape[0]
@@ -691,7 +692,7 @@
         for step in range(1, planes)
     ]
     grad_queries, grad_keys = norm_back(hats, *gains, dq, dk, late)
-    order = feature_order(inner, planes, cores, shares)
+    order = feature_order(inner, planes, cores, shares, lax.axis_size("y"))
     parts = weight_parts(counts, order, gathered, cotangents, gain_sums, shares)
     parts = exchange(after(parts, late), sums)
     own = order.shape[1] // shares

time: 180 us -> 174 us (0.967)
  local copies, waits for them, and re-layouts: 15.5 us -> 3.03 us
  Pallas kernels: 64.1 us -> 69.3 us
  waiting for transfers between devices: 34.3 us -> 36.8 us
    unnamed x30 -> x18, local copies, waits for them, and re-layouts: 14.9 us -> 2.37 us
    pallas_call x1, Pallas kernels: 6.55 us -> 9.58 us  [weight_parts(): pl.pallas_call(weight_kernel, grid_spec=pltpu.PrefetchScalarGridSpec(num_...]
  transfers between devices with their start and end apart: 11 -> 11, of which waited for: 7 -> 8; matrix products, arithmetic and copies ran while one was open for 0% -> 1% of each run, Pallas kernels for 35% -> 40%
where the time goes in v7:
time: 174 us; the launch traced here: 173 us
  Pallas kernels  69.3 us (40%)
  waiting for transfers between devices  36.8 us (21%)
  starting transfers between devices  29.6 us (17%)
  blocking collectives  17.5 us (10%)
  between operations  16.1 us (9%)
  local copies, waits for them, and re-layouts  3.03 us (2%)
    all_to_all x5, waiting for transfers between devices, exchange(): return lax.all_to_all(tensor, axes, split_axis=0, concat_axis=0, tiled=True)  31.6 us
    all_to_all x5, starting transfers between devices, exchange(): return lax.all_to_all(tensor, axes, split_axis=0, concat_axis=0, tiled=True)  23.4 us
    all_to_all x1, blocking collectives, exchange(): return lax.all_to_all(tensor, axes, split_axis=0, concat_axis=0, tiled=True)  17.5 us
    pallas_call x1, Pallas kernels, weight_parts(): pl.pallas_call(weight_kernel, grid_spec=pltpu.PrefetchScalarGridSpec(num_...  9.58 us
    pallas_call x1, Pallas kernels, space_back(): pl.pallas_call(space_back_kernel, grid=(inner // WIDE,), in_specs=[pl.Blo...  9.21 us
    pallas_call x1, Pallas kernels, grad_mixed_of(): pl.pallas_call(grad_mixed_kernel, grid=(inner // WIDE,), in_specs=[pl.Blo...  8.65 us
    pallas_call x1, Pallas kernels, space_forward(): pl.pallas_call(space_kernel, grid=(inner // WIDE,), in_specs=[SMEM, pl.Bl...  7.06 us
    pallas_call x1, Pallas kernels, project(): pl.pallas_call(project_kernel, grid=(4,), in_specs=[pl.BlockSpec((CELLS,...  6.98 us
  transfers between devices with their start and end apart: 11, of which 8 were waited for; matrix products, arithmetic and copies ran while one was open for 1% of the time, Pallas kernels for 40%

profile of v7, /device:TPU:0, one launch (start us, length us, event | category | flops | bytes accessed | tf_op | source)
XLA Modules:
  0.0 173.0 jit_solution(1849162691732219037)
XLA Ops:
  7.2 0.0 all-gather.6.cloned.1.call-start
  7.2 0.7 all-gather.6.cloned.1.call-update
  7.9 5.0 %norm.1.qk_ref = bf16[8,2,32,1536]{3,2,1,0:T(8,128)(2,1)} custom-call(bf16[256,1536]{1,0:T(8,128)(2,1)} %bitcast.21, bf16[256,1536]{1,0:T(8,128)(2,1)} %bitcast.23, f32[1,64]{1,0:T(1,128)} %bitcast.28, f32[1,64]{1,0:T(1,128)} %bitcast.31), custom_call_target="tpu_custom_call" | custom-call | bytes 18450000 | tf_op jit(solution)/shard_map/norm/pallas_call | solution.py:132
  12.9 4.6 %all-to-all-start = ((bf16[8,2,32,1536]{3,2,1,0:T(8,128)(2,1)}), bf16[8,2,32,1536]{3,2,1,0:T(8,128)(2,1)S(1)}, u32[]{:S(2)}, u32[]{:S(2)}) async-start(bf16[8,2,32,1536]{3,2,1,0:T(8,128)(2,1)} %norm.1.qk_ref), calls=%async_computation | async-start | bytes 3145728 | tf_op jit(solution)/shard_map/all_to_all | solution.py:663
  19.4 8.7 %grad_mixed.1.gm_ref = bf16[256,1536]{1,0:T(8,128)(2,1)} custom-call(bf16[256,3072]{1,0:T(8,128)(2,1)} %bitcast.19, bf16[1536,3072]{1,0:T(8,128)(2,1)} %weight_ref.3), custom_call_target="tpu_custom_call" | custom-call | bytes 32103000 | tf_op jit(solution)/shard_map/grad_mixed/pallas_call | solution.py:481
  28.0 0.7 stack.15.counts_ref.place_ref
  28.7 7.1 %space_forward.1 = (bf16[8,2,32,1536]{3,2,1,0:T(8,128)(2,1)}, f32[12,512,256]{2,1,0:T(8,128)}) custom-call(s32[6]{0:T(128)} %stack.15.counts_ref.place_ref, bf16[8,2,32,1536]{3,2,1,0:T(8,128)(2,1)} %norm.1.qk_ref, bf16[256,1536]{1,0:T(8,128)(2,1)} %bitcast.25, bf16[256,1536]{1,0:T(8,128)(2,1)} %grad_mixed.1.gm_ref), custom_call_target="tpu_custom_call" | custom-call | bytes 25830000 | tf_op jit(solution)/shard_map/space_forward/pallas_call | solution.py:196
  35.8 3.3 %all-to-all-done.qk_ref = bf16[8,2,32,1536]{3,2,1,0:T(8,128)(2,1)S(1)} async-done(((bf16[8,2,32,1536]{3,2,1,0:T(8,128)(2,1)}), bf16[8,2,32,1536]{3,2,1,0:T(8,128)(2,1)S(1)}, u32[]{:S(2)}, u32[]{:S(2)}) %all-to-all-start) | async-done | bytes 1572896 | tf_op jit(solution)/shard_map/all_to_all | solution.py:663
  39.0 3.6 %all-to-all-start.1 = ((bf16[8,2,32,1536]{3,2,1,0:T(8,128)(2,1)}), bf16[8,2,32,1536]{3,2,1,0:T(8,128)(2,1)S(1)}, u32[]{:S(2)}, u32[]{:S(2)}) async-start(bf16[8,2,32,1536]{3,2,1,0:T(8,128)(2,1)} %get-tuple-element.38), calls=%async_computation.1 | async-start | bytes 3145728 | tf_op jit(solution)/shard_map/all_to_all | solution.py:663
  42.6 0.0 copy-start.2
  42.6 5.7 %hats.1 = (f32[256,1536]{1,0:T(8,128)}, f32[256,1536]{1,0:T(8,128)}, f32[256,1536]{1,0:T(8,128)}, f32[256,1536]{1,0:T(8,128)}) custom-call(bf16[256,1536]{1,0:T(8,128)(2,1)} %bitcast.22, bf16[256,1536]{1,0:T(8,128)(2,1)} %bitcast.24), custom_call_target="tpu_custom_call" | custom-call | bytes 20664000 | tf_op jit(solution)/shard_map/hats/pallas_call | solution.py:157
  48.3 15.8 %all-to-all-done.1.sg_ref = bf16[8,2,32,1536]{3,2,1,0:T(8,128)(2,1)S(1)} async-done(((bf16[8,2,32,1536]{3,2,1,0:T(8,128)(2,1)}), bf16[8,2,32,1536]{3,2,1,0:T(8,128)(2,1)S(1)}, u32[]{:S(2)}, u32[]{:S(2)}) %all-to-all-start.1) | async-done | bytes 1572896 | tf_op jit(solution)/shard_map/all_to_all | solution.py:663
  64.1 0.0 copy-done.2
  64.1 3.5 %time_forward.1 = bf16[8,32,1536]{2,1,0:T(8,128)(2,1)S(1)} custom-call(s32[6]{0:T(128)S(1)} %copy-done.2, bf16[8,2,32,1536]{3,2,1,0:T(8,128)(2,1)S(1)} %all-to-all-done.qk_ref, bf16[8,2,32,1536]{3,2,1,0:T(8,128)(2,1)S(1)} %all-to-all-done.1.sg_ref), custom_call_target="tpu_custom_call" | custom-call | bytes 18450000 | tf_op jit(solution)/shard_map/time_forward/pallas_call | solution.py:391
  67.7 0.0 copy-start
  67.7 0.9 copy-done
  68.5 4.2 %all-to-all-start.2 = ((bf16[8,32,1536]{2,1,0:T(8,128)(2,1)}), bf16[8,32,1536]{2,1,0:T(8,128)(2,1)}, u32[]{:S(2)}, u32[]{:S(2)}) async-start(bf16[8,32,1536]{2,1,0:T(8,128)(2,1)} %copy-done), calls=%async_computation.2 | async-start | bytes 1572864 | tf_op jit(solution)/shard_map/all_to_all | solution.py:663
  72.8 0.0 all-gather.4.cloned.1.call-start
  72.8 5.8 %time_back.1 = (bf16[8,2,32,1536]{3,2,1,0:T(8,128)(2,1)}, bf16[8,32,1536]{2,1,0:T(8,128)(2,1)S(1)}, f32[8,128]{1,0:T(8,128)S(1)}) custom-call(s32[6]{0:T(128)S(1)} %copy-done.2, bf16[8,2,32,1536]{3,2,1,0:T(8,128)(2,1)S(1)} %all-to-all-done.qk_ref, bf16[8,2,32,1536]{3,2,1,0:T(8,128)(2,1)S(1)} %all-to-all-done.1.sg_ref), custom_call_target="tpu_custom_call" | custom-call | bytes 23985000 | tf_op jit(solution)/shard_map/time_back/pallas_call | solution.py:406
  78.6 0.9 copy-done.1
  79.5 0.6 copy-done.3
  80.1 5.8 %all-to-all-done.2 = bf16[8,32,1536]{2,1,0:T(8,128)(2,1)} async-done(((bf16[8,32,1536]{2,1,0:T(8,128)(2,1)}), bf16[8,32,1536]{2,1,0:T(8,128)(2,1)}, u32[]{:S(2)}, u32[]{:S(2)}) %all-to-all-start.2) | async-done | bytes 786464 | tf_op jit(solution)/shard_map/all_to_all | solution.py:663
  85.9 0.0 all-gather.4.cloned.1.call-update
  85.9 17.5 %all_to_all.30 = bf16[8,32,1536]{2,1,0:T(8,128)(2,1)} all-to-all(bf16[8,32,1536]{2,1,0:T(8,128)(2,1)} %copy-done.1), channel_id=1, replica_groups=mesh['x'=4,'z'=4,'y'=4,'core'=2] {'y','core'}, dimensions={0} | all-to-all | bytes 1572864 | tf_op jit(solution)/shard_map/all_to_all | solution.py:663
  103.4 3.6 %all-to-all-start.4 = ((bf16[8,2,32,1536]{3,2,1,0:T(8,128)(2,1)}), bf16[8,2,32,1536]{3,2,1,0:T(8,128)(2,1)S(1)}, u32[]{:S(2)}, u32[]{:S(2)}) async-start(bf16[8,2,32,1536]{3,2,1,0:T(8,128)(2,1)} %get-tuple-element.57), calls=%async_computation.4 | async-start | bytes 3145728 | tf_op jit(solution)/shard_map/all_to_all | solution.py:663
  107.0 9.2 %space_back.1 = (f32[256,1536]{1,0:T(8,128)}, f32[256,1536]{1,0:T(8,128)}, bf16[256,1536]{1,0:T(8,128)(2,1)}, f32[8,128]{1,0:T(8,128)}) custom-call(f32[8,128]{1,0:T(8,128)} %copy-done.3, f32[1,64]{1,0:T(1,128)} %bitcast.29, f32[1,64]{1,0:T(1,128)} %bitcast.32, f32[256,1536]{1,0:T(8,128)} %get-tuple-element.46.hat_q_ref, ...), custom_call_target="tpu_custom_call" | custom-call | bytes 33210000 | tf_op jit(solution)/shard_map/space_back/pallas_call | solution.py:276
  116.2 0.4 collective-permute-start
  116.6 1.0 collective-permute-done
  117.7 0.7 add.7.refs_0_
  118.4 1.5 collective-permute-start.1
  119.8 2.8 %collective-permute-start.2 = (f32[8,128]{1,0:T(8,128)S(1)}, f32[8,128]{1,0:T(8,128)S(1)}, u32[]{:S(2)}, u32[]{:S(2)}) collective-permute-start(f32[8,128]{1,0:T(8,128)S(1)} %add.7.refs_0_), channel_id=1, source_target_pairs={{0,64},{32,96},{64,0},{96,32},{1,65},{33,97},{65,1},{97,33},{2,66}... | collective-permute-start | bytes 12296 | tf_op jit(solution)/shard_map/ppermute | solution.py:691
  122.6 1.4 collective-permute-start.3
  124.0 0.0 collective-permute-done.1.refs_1_
  124.0 1.0 collective-permute-done.2.refs_2_
  125.0 1.2 collective-permute-done.3.refs_3_
  126.2 1.2 all-gather.4.cloned.1.call-done.mixed_ref
  127.5 0.0 copy-done.5
  127.5 0.0 copy-done.6
  127.5 0.0 copy-done.7
  127.5 0.0 copy-done.8
  127.5 9.6 %weight_parts.1 = bf16[16,80,512]{2,1,0:T(8,128)(2,1)} custom-call(s32[6]{0:T(128)} %stack.15.counts_ref.place_ref, bf16[2,192,384]{2,1,0:T(8,128)(2,1)} %constant.16.clone.order_ref, bf16[2048,1536]{1,0:T(8,128)(2,1)} %all-gather.4.cloned.1.call-done.mixed_ref, bf16[2048,3072]{1,0:T(8,128)(2,1)} %bitcast.18, f32[8,128]{1,0:T(8,128)} %copy-done.5, ...), custom_call_target="tpu_custom_call" | custom-call | bytes 35055000 | tf_op jit(solution)/shard_map/weight_parts/pallas_call | solution.py:569
  137.1 0.0 all-to-all-done.4.late_ref
  137.1 7.5 %all-to-all-start.5 = ((bf16[16,80,512]{2,1,0:T(8,128)(2,1)}), bf16[16,80,512]{2,1,0:T(8,128)(2,1)S(1)}, u32[]{:S(2)}, u32[]{:S(2)}) async-start(bf16[16,80,512]{2,1,0:T(8,128)(2,1)} %weight_parts.1), calls=%async_computation.5 | async-start | bytes 2621440 | tf_op jit(solution)/shard_map/all_to_all | solution.py:663
  144.6 7.0 %project.1 = bf16[256,3072]{1,0:T(8,128)(2,1)} custom-call(bf16[256,1536]{1,0:T(8,128)(2,1)} %bitcast.9.mixed_ref, bf16[1536,3072]{1,0:T(8,128)(2,1)} %weight_ref.3), custom_call_target="tpu_custom_call" | custom-call | bytes 25830000 | tf_op jit(solution)/shard_map/project/pallas_call | solution.py:503
  151.6 0.0 copy-done.4
  151.6 6.9 %norm_back.1 = (bf16[256,1536]{1,0:T(8,128)(2,1)}, bf16[256,1536]{1,0:T(8,128)(2,1)}) custom-call(f32[256,1536]{1,0:T(8,128)} %get-tuple-element.46.hat_q_ref, f32[256,1536]{1,0:T(8,128)} %get-tuple-element.47.hat_k_ref, f32[256,1536]{1,0:T(8,128)} %get-tuple-element.48.inverse_q_ref, f32[256,1536]{1,0:T(8,128)} %get-tuple-element.49.inverse_k_ref, ...), custom_call_target="tpu_custom_call" | custom-call | bytes 25830000 | tf_op jit(solution)/shard_map/norm_back/pallas_call | solution.py:453
  158.5 6.8 %all-to-all-done.5.parts_ref = bf16[16,80,512]{2,1,0:T(8,128)(2,1)S(1)} async-done(((bf16[16,80,512]{2,1,0:T(8,128)(2,1)}), bf16[16,80,512]{2,1,0:T(8,128)(2,1)S(1)}, u32[]{:S(2)}, u32[]{:S(2)}) %all-to-all-start.5) | async-done | bytes 1310752 | tf_op jit(solution)/shard_map/all_to_all | solution.py:663
  165.2 0.9 sum_parts.1
  (8 shorter events, 0.0 us)
Async XLA Ops:
  7.2 78.8 %all-gather.6.cloned.1.call-start = ((), (), s32[]{:S(2)}) async-start(), calls=%async_computation.7 | async-start | bytes 14155776 | tf_op jit(solution)/shard_map/all_gather | solution.py:668
  12.9 26.1 %all-to-all-start = ((bf16[8,2,32,1536]{3,2,1,0:T(8,128)(2,1)}), bf16[8,2,32,1536]{3,2,1,0:T(8,128)(2,1)S(1)}, u32[]{:S(2)}, u32[]{:S(2)}) async-start(bf16[8,2,32,1536]{3,2,1,0:T(8,128)(2,1)} %norm.1.qk_ref), calls=%async_computation | async-start | bytes 3145728 | tf_op jit(solution)/shard_map/all_to_all | solution.py:663
  39.0 25.1 %all-to-all-start.1 = ((bf16[8,2,32,1536]{3,2,1,0:T(8,128)(2,1)}), bf16[8,2,32,1536]{3,2,1,0:T(8,128)(2,1)S(1)}, u32[]{:S(2)}, u32[]{:S(2)}) async-start(bf16[8,2,32,1536]{3,2,1,0:T(8,128)(2,1)} %get-tuple-element.38), calls=%async_computation.1 | async-start | bytes 3145728 | tf_op jit(solution)/shard_map/all_to_all | solution.py:663
  42.6 21.5 %copy-start.2 = (s32[6]{0:T(128)S(1)}, s32[6]{0:T(128)}, u32[]{:S(2)}) copy-start(s32[6]{0:T(128)} %stack.15.counts_ref.place_ref) | copy-start | bytes 76
  67.7 0.9 copy-start
  68.5 17.4 %all-to-all-start.2 = ((bf16[8,32,1536]{2,1,0:T(8,128)(2,1)}), bf16[8,32,1536]{2,1,0:T(8,128)(2,1)}, u32[]{:S(2)}, u32[]{:S(2)}) async-start(bf16[8,32,1536]{2,1,0:T(8,128)(2,1)} %copy-done), calls=%async_computation.2 | async-start | bytes 1572864 | tf_op jit(solution)/shard_map/all_to_all | solution.py:663
  72.8 54.7 %all-gather.4.cloned.1.call-start = ((), (), s32[]{:S(2)}) async-start(), calls=%async_computation.6 | async-start | bytes 7077888 | tf_op jit(solution)/shard_map/all_gather | solution.py:680
  78.6 0.9 copy-start.1
  79.5 0.6 copy-start.3
  103.4 33.7 %all-to-all-start.4 = ((bf16[8,2,32,1536]{3,2,1,0:T(8,128)(2,1)}), bf16[8,2,32,1536]{3,2,1,0:T(8,128)(2,1)S(1)}, u32[]{:S(2)}, u32[]{:S(2)}) async-start(bf16[8,2,32,1536]{3,2,1,0:T(8,128)(2,1)} %get-tuple-element.57), calls=%async_computation.4 | async-start | bytes 3145728 | tf_op jit(solution)/shard_map/all_to_all | solution.py:663
  116.2 1.5 collective-permute-start
  118.4 9.1 %copy-start.5 = (f32[8,128]{1,0:T(8,128)}, f32[8,128]{1,0:T(8,128)S(1)}, u32[]{:S(2)}) copy-start(f32[8,128]{1,0:T(8,128)S(1)} %add.7.refs_0_) | copy-start | bytes 12292
  118.4 5.6 %collective-permute-start.1 = (f32[8,128]{1,0:T(8,128)S(1)}, f32[8,128]{1,0:T(8,128)S(1)}, u32[]{:S(2)}, u32[]{:S(2)}) collective-permute-start(f32[8,128]{1,0:T(8,128)S(1)} %add.7.refs_0_), channel_id=1, source_target_pairs={{0,32},{32,64},{64,96},{96,0},{1,33},{33,65},{65,97},{97,1},{2,34}... | collective-permute-start | bytes 12296 | tf_op jit(solution)/shard_map/ppermute | solution.py:691
  119.8 5.2 %collective-permute-start.2 = (f32[8,128]{1,0:T(8,128)S(1)}, f32[8,128]{1,0:T(8,128)S(1)}, u32[]{:S(2)}, u32[]{:S(2)}) collective-permute-start(f32[8,128]{1,0:T(8,128)S(1)} %add.7.refs_0_), channel_id=1, source_target_pairs={{0,64},{32,96},{64,0},{96,32},{1,65},{33,97},{65,1},{97,33},{2,66}... | collective-permute-start | bytes 12296 | tf_op jit(solution)/shard_map/ppermute | solution.py:691
  122.6 3.6 %collective-permute-start.3 = (f32[8,128]{1,0:T(8,128)S(1)}, f32[8,128]{1,0:T(8,128)S(1)}, u32[]{:S(2)}, u32[]{:S(2)}) collective-permute-start(f32[8,128]{1,0:T(8,128)S(1)} %add.7.refs_0_), channel_id=1, source_target_pairs={{0,96},{32,0},{64,32},{96,64},{1,97},{33,1},{65,33},{97,65},{2,98}... | collective-permute-start | bytes 12296 | tf_op jit(solution)/shard_map/ppermute | solution.py:691
  124.0 3.5 %copy-start.6 = (f32[8,128]{1,0:T(8,128)}, f32[8,128]{1,0:T(8,128)S(1)}, u32[]{:S(2)}) copy-start(f32[8,128]{1,0:T(8,128)S(1)} %collective-permute-done.1.refs_1_) | copy-start | bytes 12292
  125.0 2.5 %copy-start.7 = (f32[8,128]{1,0:T(8,128)}, f32[8,128]{1,0:T(8,128)S(1)}, u32[]{:S(2)}) copy-start(f32[8,128]{1,0:T(8,128)S(1)} %collective-permute-done.2.refs_2_) | copy-start | bytes 12292
  126.2 1.3 copy-start.8
  137.1 14.5 %copy-start.4 = (bf16[8,2,32,1536]{3,2,1,0:T(8,128)(2,1)}, bf16[8,2,32,1536]{3,2,1,0:T(8,128)(2,1)S(1)}, u32[]{:S(2)}) copy-start(bf16[8,2,32,1536]{3,2,1,0:T(8,128)(2,1)S(1)} %all-to-all-done.4.late_ref) | copy-start | bytes 4718596
  137.1 28.2 %all-to-all-start.5 = ((bf16[16,80,512]{2,1,0:T(8,128)(2,1)}), bf16[16,80,512]{2,1,0:T(8,128)(2,1)S(1)}, u32[]{:S(2)}, u32[]{:S(2)}) async-start(bf16[16,80,512]{2,1,0:T(8,128)(2,1)} %weight_parts.1), calls=%async_computation.5 | async-start | bytes 2621440 | tf_op jit(solution)/shard_map/all_to_all | solution.py:663
Sparse Core Ops, SparseCore 0:
  9.7 69.7 all-gather.5
  86.1 41.3 all-gather.3

commit v8 on v7

--- a/solution.py
+++ b/solution.py
@@ -515,7 +515,7 @@
     )(mixed, weight)
 
 
-PIECES = 6
+PIECES = 24
 STEPS = 3
 TAIL = 8
 
@@ -531,7 +531,9 @@
             terms.append(rest.astype(BF).astype(F32))
             rest = rest - terms[-1]
     rows = jnp.concatenate(terms + [jnp.zeros((TAIL - 6, LANES), F32)], 0)
-    return jnp.concatenate([rows, jnp.zeros((TAIL, block - LANES), F32)], 1).astype(BF)
+    if block > LANES:
+        rows = jnp.concatenate([rows, jnp.zeros((TAIL, block - LANES), F32)], 1)
+    return rows.astype(BF)
 
 
 def weight_kernel(place_ref, order_ref, mixed_ref, cot_ref, *refs):

time: 174 us -> 173 us (level)
  no operation moved by 1% of the time
where the time goes in v8:
time: 173 us; the launch traced here: 172 us
  Pallas kernels  69.3 us (40%)
  waiting for transfers between devices  36.1 us (21%)
  starting transfers between devices  29.6 us (17%)
  blocking collectives  17.5 us (10%)
  between operations  16.1 us (9%)
  local copies, waits for them, and re-layouts  3.03 us (2%)
    all_to_all x5, waiting for transfers between devices, exchange(): return lax.all_to_all(tensor, axes, split_axis=0, concat_axis=0, tiled=True)  30.9 us
    all_to_all x5, starting transfers between devices, exchange(): return lax.all_to_all(tensor, axes, split_axis=0, concat_axis=0, tiled=True)  23.4 us
    all_to_all x1, blocking collectives, exchange(): return lax.all_to_all(tensor, axes, split_axis=0, concat_axis=0, tiled=True)  17.5 us
    pallas_call x1, Pallas kernels, weight_parts(): pl.pallas_call(weight_kernel, grid_spec=pltpu.PrefetchScalarGridSpec(num_...  9.63 us
    pallas_call x1, Pallas kernels, space_back(): pl.pallas_call(space_back_kernel, grid=(inner // WIDE,), in_specs=[pl.Blo...  9.21 us
    pallas_call x1, Pallas kernels, grad_mixed_of(): pl.pallas_call(grad_mixed_kernel, grid=(inner // WIDE,), in_specs=[pl.Blo...  8.65 us
    pallas_call x1, Pallas kernels, space_forward(): pl.pallas_call(space_kernel, grid=(inner // WIDE,), in_specs=[SMEM, pl.Bl...  7.06 us
    pallas_call x1, Pallas kernels, project(): pl.pallas_call(project_kernel, grid=(4,), in_specs=[pl.BlockSpec((CELLS,...  6.98 us
  transfers between devices with their start and end apart: 11, of which 8 were waited for; matrix products, arithmetic and copies ran while one was open for 1% of the time, Pallas kernels for 40%

profile of v8, /device:TPU:0, one launch (start us, length us, event | category | flops | bytes accessed | tf_op | source)
XLA Modules:
  0.0 172.3 jit_solution(17804058785359571849)
XLA Ops:
  7.2 0.0 all-gather.6.cloned.1.call-start
  7.2 0.7 all-gather.6.cloned.1.call-update
  7.9 5.0 %norm.1.qk_ref = bf16[8,2,32,1536]{3,2,1,0:T(8,128)(2,1)} custom-call(bf16[256,1536]{1,0:T(8,128)(2,1)} %bitcast.21, bf16[256,1536]{1,0:T(8,128)(2,1)} %bitcast.23, f32[1,64]{1,0:T(1,128)} %bitcast.28, f32[1,64]{1,0:T(1,128)} %bitcast.31), custom_call_target="tpu_custom_call" | custom-call | bytes 18450000 | tf_op jit(solution)/shard_map/norm/pallas_call | solution.py:132
  12.9 4.6 %all-to-all-start = ((bf16[8,2,32,1536]{3,2,1,0:T(8,128)(2,1)}), bf16[8,2,32,1536]{3,2,1,0:T(8,128)(2,1)S(1)}, u32[]{:S(2)}, u32[]{:S(2)}) async-start(bf16[8,2,32,1536]{3,2,1,0:T(8,128)(2,1)} %norm.1.qk_ref), calls=%async_computation | async-start | bytes 3145728 | tf_op jit(solution)/shard_map/all_to_all | solution.py:665
  19.4 8.7 %grad_mixed.1.gm_ref = bf16[256,1536]{1,0:T(8,128)(2,1)} custom-call(bf16[256,3072]{1,0:T(8,128)(2,1)} %bitcast.19, bf16[1536,3072]{1,0:T(8,128)(2,1)} %weight_ref.3), custom_call_target="tpu_custom_call" | custom-call | bytes 32103000 | tf_op jit(solution)/shard_map/grad_mixed/pallas_call | solution.py:481
  28.0 0.7 stack.15.counts_ref.place_ref
  28.7 7.1 %space_forward.1 = (bf16[8,2,32,1536]{3,2,1,0:T(8,128)(2,1)}, f32[12,512,256]{2,1,0:T(8,128)}) custom-call(s32[6]{0:T(128)} %stack.15.counts_ref.place_ref, bf16[8,2,32,1536]{3,2,1,0:T(8,128)(2,1)} %norm.1.qk_ref, bf16[256,1536]{1,0:T(8,128)(2,1)} %bitcast.25, bf16[256,1536]{1,0:T(8,128)(2,1)} %grad_mixed.1.gm_ref), custom_call_target="tpu_custom_call" | custom-call | bytes 25830000 | tf_op jit(solution)/shard_map/space_forward/pallas_call | solution.py:196
  35.8 3.3 %all-to-all-done.qk_ref = bf16[8,2,32,1536]{3,2,1,0:T(8,128)(2,1)S(1)} async-done(((bf16[8,2,32,1536]{3,2,1,0:T(8,128)(2,1)}), bf16[8,2,32,1536]{3,2,1,0:T(8,128)(2,1)S(1)}, u32[]{:S(2)}, u32[]{:S(2)}) %all-to-all-start) | async-done | bytes 1572896 | tf_op jit(solution)/shard_map/all_to_all | solution.py:665
  39.0 3.6 %all-to-all-start.1 = ((bf16[8,2,32,1536]{3,2,1,0:T(8,128)(2,1)}), bf16[8,2,32,1536]{3,2,1,0:T(8,128)(2,1)S(1)}, u32[]{:S(2)}, u32[]{:S(2)}) async-start(bf16[8,2,32,1536]{3,2,1,0:T(8,128)(2,1)} %get-tuple-element.38), calls=%async_computation.1 | async-start | bytes 3145728 | tf_op jit(solution)/shard_map/all_to_all | solution.py:665
  42.6 0.0 copy-start.2
  42.6 5.7 %hats.1 = (f32[256,1536]{1,0:T(8,128)}, f32[256,1536]{1,0:T(8,128)}, f32[256,1536]{1,0:T(8,128)}, f32[256,1536]{1,0:T(8,128)}) custom-call(bf16[256,1536]{1,0:T(8,128)(2,1)} %bitcast.22, bf16[256,1536]{1,0:T(8,128)(2,1)} %bitcast.24), custom_call_target="tpu_custom_call" | custom-call | bytes 20664000 | tf_op jit(solution)/shard_map/hats/pallas_call | solution.py:157
  48.3 15.8 %all-to-all-done.1.sg_ref = bf16[8,2,32,1536]{3,2,1,0:T(8,128)(2,1)S(1)} async-done(((bf16[8,2,32,1536]{3,2,1,0:T(8,128)(2,1)}), bf16[8,2,32,1536]{3,2,1,0:T(8,128)(2,1)S(1)}, u32[]{:S(2)}, u32[]{:S(2)}) %all-to-all-start.1) | async-done | bytes 1572896 | tf_op jit(solution)/shard_map/all_to_all | solution.py:665
  64.1 0.0 copy-done.2
  64.1 3.5 %time_forward.1 = bf16[8,32,1536]{2,1,0:T(8,128)(2,1)S(1)} custom-call(s32[6]{0:T(128)S(1)} %copy-done.2, bf16[8,2,32,1536]{3,2,1,0:T(8,128)(2,1)S(1)} %all-to-all-done.qk_ref, bf16[8,2,32,1536]{3,2,1,0:T(8,128)(2,1)S(1)} %all-to-all-done.1.sg_ref), custom_call_target="tpu_custom_call" | custom-call | bytes 18450000 | tf_op jit(solution)/shard_map/time_forward/pallas_call | solution.py:391
  67.7 0.0 copy-start
  67.7 0.9 copy-done
  68.5 4.2 %all-to-all-start.2 = ((bf16[8,32,1536]{2,1,0:T(8,128)(2,1)}), bf16[8,32,1536]{2,1,0:T(8,128)(2,1)}, u32[]{:S(2)}, u32[]{:S(2)}) async-start(bf16[8,32,1536]{2,1,0:T(8,128)(2,1)} %copy-done), calls=%async_computation.2 | async-start | bytes 1572864 | tf_op jit(solution)/shard_map/all_to_all | solution.py:665
  72.8 0.0 all-gather.4.cloned.1.call-start
  72.8 5.8 %time_back.1 = (bf16[8,2,32,1536]{3,2,1,0:T(8,128)(2,1)}, bf16[8,32,1536]{2,1,0:T(8,128)(2,1)S(1)}, f32[8,128]{1,0:T(8,128)S(1)}) custom-call(s32[6]{0:T(128)S(1)} %copy-done.2, bf16[8,2,32,1536]{3,2,1,0:T(8,128)(2,1)S(1)} %all-to-all-done.qk_ref, bf16[8,2,32,1536]{3,2,1,0:T(8,128)(2,1)S(1)} %all-to-all-done.1.sg_ref), custom_call_target="tpu_custom_call" | custom-call | bytes 23985000 | tf_op jit(solution)/shard_map/time_back/pallas_call | solution.py:406
  78.6 0.9 copy-done.1
  79.5 0.6 copy-done.3
  80.1 5.8 %all-to-all-done.2 = bf16[8,32,1536]{2,1,0:T(8,128)(2,1)} async-done(((bf16[8,32,1536]{2,1,0:T(8,128)(2,1)}), bf16[8,32,1536]{2,1,0:T(8,128)(2,1)}, u32[]{:S(2)}, u32[]{:S(2)}) %all-to-all-start.2) | async-done | bytes 786464 | tf_op jit(solution)/shard_map/all_to_all | solution.py:665
  85.9 0.0 all-gather.4.cloned.1.call-update
  85.9 17.5 %all_to_all.30 = bf16[8,32,1536]{2,1,0:T(8,128)(2,1)} all-to-all(bf16[8,32,1536]{2,1,0:T(8,128)(2,1)} %copy-done.1), channel_id=1, replica_groups=mesh['x'=4,'z'=4,'y'=4,'core'=2] {'y','core'}, dimensions={0} | all-to-all | bytes 1572864 | tf_op jit(solution)/shard_map/all_to_all | solution.py:665
  103.4 3.6 %all-to-all-start.4 = ((bf16[8,2,32,1536]{3,2,1,0:T(8,128)(2,1)}), bf16[8,2,32,1536]{3,2,1,0:T(8,128)(2,1)S(1)}, u32[]{:S(2)}, u32[]{:S(2)}) async-start(bf16[8,2,32,1536]{3,2,1,0:T(8,128)(2,1)} %get-tuple-element.57), calls=%async_computation.4 | async-start | bytes 3145728 | tf_op jit(solution)/shard_map/all_to_all | solution.py:665
  107.0 9.2 %space_back.1 = (f32[256,1536]{1,0:T(8,128)}, f32[256,1536]{1,0:T(8,128)}, bf16[256,1536]{1,0:T(8,128)(2,1)}, f32[8,128]{1,0:T(8,128)}) custom-call(f32[8,128]{1,0:T(8,128)} %copy-done.3, f32[1,64]{1,0:T(1,128)} %bitcast.29, f32[1,64]{1,0:T(1,128)} %bitcast.32, f32[256,1536]{1,0:T(8,128)} %get-tuple-element.46.hat_q_ref, ...), custom_call_target="tpu_custom_call" | custom-call | bytes 33210000 | tf_op jit(solution)/shard_map/space_back/pallas_call | solution.py:276
  116.2 0.4 collective-permute-start
  116.6 1.0 collective-permute-done
  117.7 0.7 add.7.refs_0_
  118.4 1.5 collective-permute-start.1
  119.8 2.8 %collective-permute-start.2 = (f32[8,128]{1,0:T(8,128)S(1)}, f32[8,128]{1,0:T(8,128)S(1)}, u32[]{:S(2)}, u32[]{:S(2)}) collective-permute-start(f32[8,128]{1,0:T(8,128)S(1)} %add.7.refs_0_), channel_id=1, source_target_pairs={{0,64},{32,96},{64,0},{96,32},{1,65},{33,97},{65,1},{97,33},{2,66}... | collective-permute-start | bytes 12296 | tf_op jit(solution)/shard_map/ppermute | solution.py:693
  122.6 1.4 collective-permute-start.3
  124.0 0.0 collective-permute-done.1.refs_1_
  124.0 1.0 collective-permute-done.2.refs_2_
  125.0 1.2 collective-permute-done.3.refs_3_
  126.2 1.2 all-gather.4.cloned.1.call-done.mixed_ref
  127.5 0.0 copy-done.5
  127.5 0.0 copy-done.6
  127.5 0.0 copy-done.7
  127.5 0.0 copy-done.8
  127.5 9.6 %weight_parts.1 = bf16[16,304,128]{2,1,0:T(8,128)(2,1)} custom-call(s32[6]{0:T(128)} %stack.15.counts_ref.place_ref, bf16[2,192,384]{2,1,0:T(8,128)(2,1)} %constant.16.clone.order_ref, bf16[2048,1536]{1,0:T(8,128)(2,1)} %all-gather.4.cloned.1.call-done.mixed_ref, bf16[2048,3072]{1,0:T(8,128)(2,1)} %bitcast.18, f32[8,128]{1,0:T(8,128)} %copy-done.5, ...), custom_call_target="tpu_custom_call" | custom-call | bytes 35055000 | tf_op jit(solution)/shard_map/weight_parts/pallas_call | solution.py:571
  137.1 0.0 all-to-all-done.4.late_ref
  137.1 7.5 %all-to-all-start.5 = ((bf16[16,304,128]{2,1,0:T(8,128)(2,1)}), bf16[16,304,128]{2,1,0:T(8,128)(2,1)S(1)}, u32[]{:S(2)}, u32[]{:S(2)}) async-start(bf16[16,304,128]{2,1,0:T(8,128)(2,1)} %weight_parts.1), calls=%async_computation.5 | async-start | bytes 2490368 | tf_op jit(solution)/shard_map/all_to_all | solution.py:665
  144.6 7.0 %project.1 = bf16[256,3072]{1,0:T(8,128)(2,1)} custom-call(bf16[256,1536]{1,0:T(8,128)(2,1)} %bitcast.9.mixed_ref, bf16[1536,3072]{1,0:T(8,128)(2,1)} %weight_ref.3), custom_call_target="tpu_custom_call" | custom-call | bytes 25830000 | tf_op jit(solution)/shard_map/project/pallas_call | solution.py:503
  151.6 0.0 copy-done.4
  151.6 6.9 %norm_back.1 = (bf16[256,1536]{1,0:T(8,128)(2,1)}, bf16[256,1536]{1,0:T(8,128)(2,1)}) custom-call(f32[256,1536]{1,0:T(8,128)} %get-tuple-element.46.hat_q_ref, f32[256,1536]{1,0:T(8,128)} %get-tuple-element.47.hat_k_ref, f32[256,1536]{1,0:T(8,128)} %get-tuple-element.48.inverse_q_ref, f32[256,1536]{1,0:T(8,128)} %get-tuple-element.49.inverse_k_ref, ...), custom_call_target="tpu_custom_call" | custom-call | bytes 25830000 | tf_op jit(solution)/shard_map/norm_back/pallas_call | solution.py:453
  158.5 6.0 %all-to-all-done.5.parts_ref = bf16[16,304,128]{2,1,0:T(8,128)(2,1)S(1)} async-done(((bf16[16,304,128]{2,1,0:T(8,128)(2,1)}), bf16[16,304,128]{2,1,0:T(8,128)(2,1)S(1)}, u32[]{:S(2)}, u32[]{:S(2)}) %all-to-all-start.5) | async-done | bytes 1245216 | tf_op jit(solution)/shard_map/all_to_all | solution.py:665
  164.5 0.9 sum_parts.1
  (8 shorter events, 0.0 us)
Async XLA Ops:
  7.2 78.8 %all-gather.6.cloned.1.call-start = ((), (), s32[]{:S(2)}) async-start(), calls=%async_computation.7 | async-start | bytes 14155776 | tf_op jit(solution)/shard_map/all_gather | solution.py:670
  12.9 26.1 %all-to-all-start = ((bf16[8,2,32,1536]{3,2,1,0:T(8,128)(2,1)}), bf16[8,2,32,1536]{3,2,1,0:T(8,128)(2,1)S(1)}, u32[]{:S(2)}, u32[]{:S(2)}) async-start(bf16[8,2,32,1536]{3,2,1,0:T(8,128)(2,1)} %norm.1.qk_ref), calls=%async_computation | async-start | bytes 3145728 | tf_op jit(solution)/shard_map/all_to_all | solution.py:665
  39.0 25.1 %all-to-all-start.1 = ((bf16[8,2,32,1536]{3,2,1,0:T(8,128)(2,1)}), bf16[8,2,32,1536]{3,2,1,0:T(8,128)(2,1)S(1)}, u32[]{:S(2)}, u32[]{:S(2)}) async-start(bf16[8,2,32,1536]{3,2,1,0:T(8,128)(2,1)} %get-tuple-element.38), calls=%async_computation.1 | async-start | bytes 3145728 | tf_op jit(solution)/shard_map/all_to_all | solution.py:665
  42.6 21.5 %copy-start.2 = (s32[6]{0:T(128)S(1)}, s32[6]{0:T(128)}, u32[]{:S(2)}) copy-start(s32[6]{0:T(128)} %stack.15.counts_ref.place_ref) | copy-start | bytes 76
  67.7 0.9 copy-start
  68.5 17.4 %all-to-all-start.2 = ((bf16[8,32,1536]{2,1,0:T(8,128)(2,1)}), bf16[8,32,1536]{2,1,0:T(8,128)(2,1)}, u32[]{:S(2)}, u32[]{:S(2)}) async-start(bf16[8,32,1536]{2,1,0:T(8,128)(2,1)} %copy-done), calls=%async_computation.2 | async-start | bytes 1572864 | tf_op jit(solution)/shard_map/all_to_all | solution.py:665
  72.8 54.7 %all-gather.4.cloned.1.call-start = ((), (), s32[]{:S(2)}) async-start(), calls=%async_computation.6 | async-start | bytes 7077888 | tf_op jit(solution)/shard_map/all_gather | solution.py:682
  78.6 0.9 copy-start.1
  79.5 0.6 copy-start.3
  103.4 33.7 %all-to-all-start.4 = ((bf16[8,2,32,1536]{3,2,1,0:T(8,128)(2,1)}), bf16[8,2,32,1536]{3,2,1,0:T(8,128)(2,1)S(1)}, u32[]{:S(2)}, u32[]{:S(2)}) async-start(bf16[8,2,32,1536]{3,2,1,0:T(8,128)(2,1)} %get-tuple-element.57), calls=%async_computation.4 | async-start | bytes 3145728 | tf_op jit(solution)/shard_map/all_to_all | solution.py:665
  116.2 1.5 collective-permute-start
  118.4 9.1 %copy-start.5 = (f32[8,128]{1,0:T(8,128)}, f32[8,128]{1,0:T(8,128)S(1)}, u32[]{:S(2)}) copy-start(f32[8,128]{1,0:T(8,128)S(1)} %add.7.refs_0_) | copy-start | bytes 12292
  118.4 5.6 %collective-permute-start.1 = (f32[8,128]{1,0:T(8,128)S(1)}, f32[8,128]{1,0:T(8,128)S(1)}, u32[]{:S(2)}, u32[]{:S(2)}) collective-permute-start(f32[8,128]{1,0:T(8,128)S(1)} %add.7.refs_0_), channel_id=1, source_target_pairs={{0,32},{32,64},{64,96},{96,0},{1,33},{33,65},{65,97},{97,1},{2,34}... | collective-permute-start | bytes 12296 | tf_op jit(solution)/shard_map/ppermute | solution.py:693
  119.8 5.2 %collective-permute-start.2 = (f32[8,128]{1,0:T(8,128)S(1)}, f32[8,128]{1,0:T(8,128)S(1)}, u32[]{:S(2)}, u32[]{:S(2)}) collective-permute-start(f32[8,128]{1,0:T(8,128)S(1)} %add.7.refs_0_), channel_id=1, source_target_pairs={{0,64},{32,96},{64,0},{96,32},{1,65},{33,97},{65,1},{97,33},{2,66}... | collective-permute-start | bytes 12296 | tf_op jit(solution)/shard_map/ppermute | solution.py:693
  122.6 3.6 %collective-permute-start.3 = (f32[8,128]{1,0:T(8,128)S(1)}, f32[8,128]{1,0:T(8,128)S(1)}, u32[]{:S(2)}, u32[]{:S(2)}) collective-permute-start(f32[8,128]{1,0:T(8,128)S(1)} %add.7.refs_0_), channel_id=1, source_target_pairs={{0,96},{32,0},{64,32},{96,64},{1,97},{33,1},{65,33},{97,65},{2,98}... | collective-permute-start | bytes 12296 | tf_op jit(solution)/shard_map/ppermute | solution.py:693
  124.0 3.5 %copy-start.6 = (f32[8,128]{1,0:T(8,128)}, f32[8,128]{1,0:T(8,128)S(1)}, u32[]{:S(2)}) copy-start(f32[8,128]{1,0:T(8,128)S(1)} %collective-permute-done.1.refs_1_) | copy-start | bytes 12292
  125.0 2.5 %copy-start.7 = (f32[8,128]{1,0:T(8,128)}, f32[8,128]{1,0:T(8,128)S(1)}, u32[]{:S(2)}) copy-start(f32[8,128]{1,0:T(8,128)S(1)} %collective-permute-done.2.refs_2_) | copy-start | bytes 12292
  126.2 1.3 copy-start.8
  137.1 14.5 %copy-start.4 = (bf16[8,2,32,1536]{3,2,1,0:T(8,128)(2,1)}, bf16[8,2,32,1536]{3,2,1,0:T(8,128)(2,1)S(1)}, u32[]{:S(2)}) copy-start(bf16[8,2,32,1536]{3,2,1,0:T(8,128)(2,1)S(1)} %all-to-all-done.4.late_ref) | copy-start | bytes 4718596
  137.1 27.4 %all-to-all-start.5 = ((bf16[16,304,128]{2,1,0:T(8,128)(2,1)}), bf16[16,304,128]{2,1,0:T(8,128)(2,1)S(1)}, u32[]{:S(2)}, u32[]{:S(2)}) async-start(bf16[16,304,128]{2,1,0:T(8,128)(2,1)} %weight_parts.1), calls=%async_computation.5 | async-start | bytes 2490368 | tf_op jit(solution)/shard_map/all_to_all | solution.py:665
Sparse Core Ops, SparseCore 0:
  9.7 69.7 all-gather.5
  86.1 41.3 all-gather.3
